TPU v7x, 512 devices: a whole 4x8x8 slice. The times are simulated.
512 devices in a mesh: gx: 8 (over z_lo, core), gy: 8 (over y), gz: 8 (over x, z_hi).
Axes of the slice: x: 4, y: 8, z: 8 (z_hi: 2, z_lo: 4; z = z_hi * 4 + z_lo), core: 2. Of those that a mesh axis runs over, the one named last changes fastest.
Arguments:
- positions: float32 [3, 8, 8, 8, 32], P(None, 'gx', 'gy', 'gz'), as said below
- species: int32 [8, 8, 8, 32], P('gx', 'gy', 'gz'), may hold values from 0 to 88
- atom_count: int32 [8, 8, 8], P('gx', 'gy', 'gz'), may hold values from 16 to 32, as said below
- edge_count: int32 [8, 8, 8], P('gx', 'gy', 'gz'), may hold values from 0 to 1792, as said below
- sender: int32 [8, 8, 8, 1792], P('gx', 'gy', 'gz'), may hold values from 0 to 863, as said below
- receiver: int32 [8, 8, 8, 1792], P('gx', 'gy', 'gz'), may hold values from 0 to 31, as said below
- image_shift: int32 [3, 8, 8, 8, 1792], P(None, 'gx', 'gy', 'gz'), may hold values from -1 to 1, as said below
- embed: float32 [89, 128], replicated, may hold values from -6 to 6
- radial_in: float32 [2, 8, 64], replicated, may hold values from -2 to 2
- radial_out: float32 [2, 64, 384], replicated, may hold values from -0.75 to 0.75
- w_up: float32 [2, 128, 128], replicated, may hold values from -0.5 to 0.5
- lam: float32 [2, 2, 128], replicated, may hold values from -4 to 4
- w_mix: float32 [2, 128, 128], replicated, may hold values from -0.5 to 0.5
- read_one: float32 [128], replicated, may hold values from -0.5 to 0.5
- read_hidden: float32 [128, 16], replicated, may hold values from -0.5 to 0.5
- read_out: float32 [16], replicated, may hold values from -1.5 to 1.5
Outputs:
- site_energy: float32 [8, 8, 8, 32], P('gx', 'gy', 'gz')
- forces: float32 [3, 8, 8, 8, 32], P(None, 'gx', 'gy', 'gz')
Inputs may be any that keep to these rules, and one draw needn't show every extreme that they name: `atom_count`: slots at and above a brick's count are empty: no edge names them, and their species and positions are placeholders. At least one brick is full. `edge_count`: some brick has all 1792 edge slots live. A live edge names an owned slot of the neighbour block; sender and receiver are 0 on edges that are not live. Each live edge's image-shifted sender lies within 5.5 angstrom of its receiver; every pair of owned atoms within 5 angstrom of each other, over all periodic images, is a live edge of the receiver's brick; the (sender image, receiver) pairs within a brick are distinct. A live edge's receiver is below atom_count. `image_shift`: nonzero only where the neighbour block lies across the box's boundary; 0 on edges that are not live. `positions`: any two atoms are at least 1 angstrom apart.
All inputs are finite; a program needn't handle non-finite values.
Results may differ from a plain program's by a relative error of at most 0.0085.
Values may be sent and summed in bfloat16 or wider, within the bound.
No kernel may reach another device: no remote copies, remote signals or barrier semaphores. Data moves between devices by JAX's collectives and lax.ppermute only.
A program may use at most 128 MiB of HBM per device.

v0:
```python
import jax
import jax.numpy as jnp
from jax import lax
from jax.sharding import PartitionSpec as P

cutoff_radius = 5.0
lattice_step = 2.25
mean_degree = 8.0


def padded(cells, sides, width):
    for axis, dim in sides:
        count = lax.axis_size(axis)
        head = lax.slice_in_dim(cells, 0, width, axis=dim)
        tail = lax.slice_in_dim(cells, cells.shape[dim] - width, cells.shape[dim], axis=dim)
        cells = jnp.concatenate(
            [
                lax.ppermute(tail, axis, [(i, (i + 1) % count) for i in range(count)]),
                cells,
                lax.ppermute(head, axis, [((i + 1) % count, i) for i in range(count)]),
            ],
            axis=dim,
        )
    return cells


def embed_rows(embed, kinds):
    table = (kinds[:, None] == jnp.arange(embed.shape[0], dtype=jnp.int32)[None, :]).astype(
        jnp.float32
    )
    return jnp.dot(table, embed, precision=lax.Precision.HIGHEST).astype(jnp.bfloat16)


def layer(
    w_in,
    w_out,
    w_lift,
    weights_sq,
    w_merge,
    own_pos,
    ghost_pos,
    ghost_h,
    own_h,
    sender,
    receiver,
    shift_len,
    valid,
):
    atoms = own_pos.shape[1]
    width = ghost_h.shape[1]
    rel = (
        jnp.take(ghost_pos, sender, axis=1) + shift_len - jnp.take(own_pos, receiver, axis=1)
    ) / cutoff_radius
    dist2 = jnp.sum(rel * rel, axis=0)
    envelope = jnp.square(jnp.maximum(1.0 - dist2, 0.0)) * valid
    nbasis = w_in.shape[0]
    centres = jnp.arange(nbasis, dtype=jnp.float32) / (nbasis - 1)
    basis = jnp.exp(-jnp.square((dist2[None, :] - centres[:, None]) * nbasis))
    hidden = jax.nn.silu(
        lax.dot_general(basis, w_in, (((0,), (0,)), ((), ())), precision=lax.Precision.HIGHEST)
    )
    radial = jnp.dot(hidden, w_out, precision=lax.Precision.HIGHEST) * envelope[:, None]
    lifted = jnp.take(jnp.dot(ghost_h, w_lift, precision=lax.Precision.HIGHEST), sender, axis=0)
    xpos, ypos, zpos = (rel[0], rel[1], rel[2])
    harmonics = jnp.stack(
        [
            jnp.ones_like(xpos),
            3.0**0.5 * xpos,
            3.0**0.5 * ypos,
            3.0**0.5 * zpos,
            15.0**0.5 * xpos * ypos,
            15.0**0.5 * ypos * zpos,
            15.0**0.5 * xpos * zpos,
            0.5 * 15.0**0.5 * (xpos * xpos - ypos * ypos),
            0.5 * 5.0**0.5 * (2.0 * zpos * zpos - xpos * xpos - ypos * ypos),
        ]
    )
    onehot = (receiver[None, :] == jnp.arange(atoms, dtype=jnp.int32)[:, None]).astype(jnp.float32)
    pooling = onehot[None, :, :] * harmonics[:, None, :] / mean_degree
    base_zero = radial[:, :width] * lifted
    base_one = radial[:, width : 2 * width] * lifted
    base_two = radial[:, 2 * width :] * lifted
    scalar = jnp.dot(pooling[0], base_zero, precision=lax.Precision.HIGHEST)
    order_one = jnp.einsum("mae,ec->mac", pooling[1:4], base_one, precision=lax.Precision.HIGHEST)
    order_two = jnp.einsum("mae,ec->mac", pooling[4:], base_two, precision=lax.Precision.HIGHEST)
    first = jnp.sum(jnp.square(order_one), axis=0)
    second = jnp.sum(jnp.square(order_two), axis=0)
    product = scalar + weights_sq[0] * first + weights_sq[1] * second
    return own_h + jnp.dot(product, w_merge, precision=lax.Precision.HIGHEST)


def readout_two(h_two, read_hidden, read_out):
    inner = jax.nn.silu(jnp.dot(h_two, read_hidden, precision=lax.Precision.HIGHEST))
    return jnp.dot(inner, read_out, precision=lax.Precision.HIGHEST)


def fold_back(pieces):
    spread = padded(pieces, (("gx", 0), ("gy", 1), ("gz", 2)), 1)
    return jnp.sum(spread[::2, ::2, ::2], axis=(0, 1, 2))


def coord_layout(ghost_grad, atoms):
    return ghost_grad.reshape(3, 3, 3, 3, atoms).transpose(1, 2, 3, 4, 0)


def local(
    positions,
    species,
    atom_count,
    edge_count,
    sender,
    receiver,
    image_shift,
    embed,
    radial_in,
    radial_out,
    w_up,
    lam,
    w_mix,
    read_one,
    read_hidden,
    read_out,
):
    atoms = positions.shape[-1]
    ghosts = 27 * atoms
    width = embed.shape[1]
    box = jnp.array(
        [
            lax.axis_size("gx") * 4 * lattice_step,
            lax.axis_size("gy") * 4 * lattice_step,
            lax.axis_size("gz") * (atoms // 16) * lattice_step,
        ],
        jnp.float32,
    )
    own_pos = positions[:, 0, 0, 0, :]
    ghost_pos = padded(positions, (("gx", 1), ("gy", 2), ("gz", 3)), 1).reshape(3, ghosts)
    own_rows = embed_rows(embed, species[0, 0, 0])
    ghost_h0 = (
        padded(own_rows[None, None, None], (("gx", 0), ("gy", 1), ("gz", 2)), 1)
        .reshape(ghosts, width)
        .astype(jnp.float32)
    )
    own_h0 = own_rows.astype(jnp.float32)
    senders = sender[0, 0, 0]
    receivers = receiver[0, 0, 0]
    shift_len = image_shift[:, 0, 0, 0, :].astype(jnp.float32) * box[:, None]
    valid = (jnp.arange(senders.shape[0], dtype=jnp.int32) < edge_count[0, 0, 0]).astype(
        jnp.float32
    )
    mask = (jnp.arange(atoms, dtype=jnp.int32) < atom_count[0, 0, 0]).astype(jnp.float32)

    def first(pos_own, pos_ghost):
        h_one = layer(
            radial_in[0],
            radial_out[0],
            w_up[0],
            lam[0],
            w_mix[0],
            pos_own,
            pos_ghost,
            ghost_h0,
            own_h0,
            senders,
            receivers,
            shift_len,
            valid,
        )
        return (h_one, jnp.dot(h_one, read_one, precision=lax.Precision.HIGHEST) * mask)

    (h_one, energy_one), back_one = jax.vjp(first, own_pos, ghost_pos)
    h_stored = h_one.astype(jnp.bfloat16)
    ghost_h1 = (
        padded(h_stored[None, None, None], (("gx", 0), ("gy", 1), ("gz", 2)), 1)
        .reshape(ghosts, width)
        .astype(jnp.float32)
    )
    own_h1 = h_stored.astype(jnp.float32)

    def second(pos_own, pos_ghost, feat_ghost, feat_own):
        h_two = layer(
            radial_in[1],
            radial_out[1],
            w_up[1],
            lam[1],
            w_mix[1],
            pos_own,
            pos_ghost,
            feat_ghost,
            feat_own,
            senders,
            receivers,
            shift_len,
            valid,
        )
        return readout_two(h_two, read_hidden, read_out) * mask

    energy_two, back_two = jax.vjp(second, own_pos, ghost_pos, ghost_h1, own_h1)
    d_own_two, d_ghost_two, d_feat_ghost, d_feat_own = back_two(jnp.ones_like(energy_two))
    coord_two = fold_back(coord_layout(d_ghost_two, atoms))
    d_h_one = d_feat_own + fold_back(d_feat_ghost.reshape(3, 3, 3, atoms, width))
    d_own_one, d_ghost_one = back_one((d_h_one, jnp.ones_like(energy_one)))
    coord_sum = coord_two + fold_back(coord_layout(d_ghost_one, atoms))
    forces = -(d_own_one + d_own_two + coord_sum.T)
    site_energy = (energy_one + energy_two)[None, None, None]
    return (site_energy, forces[:, None, None, None, :])


def solution(mesh):
    in_specs = (
        P(None, "gx", "gy", "gz", None),
        P("gx", "gy", "gz", None),
        P("gx", "gy", "gz"),
        P("gx", "gy", "gz"),
        P("gx", "gy", "gz", None),
        P("gx", "gy", "gz", None),
        P(None, "gx", "gy", "gz", None),
        P(),
        P(),
        P(),
        P(),
        P(),
        P(),
        P(),
        P(),
        P(),
    )
    out_specs = (P("gx", "gy", "gz", None), P(None, "gx", "gy", "gz", None))
    return jax.shard_map(local, mesh=mesh, in_specs=in_specs, out_specs=out_specs, check_vma=False)
```

profile of v0, /device:TPU:4, one launch (start us, length us, event | category | flops | bytes accessed | tf_op | source)
XLA Modules:
  0.0 369.2 jit_solution(2757225147103608497)
XLA Ops:
  0.7 7.5 %collective-permute-start.1 = (f32[3,1,1,1,32]{4,3,2,1,0:T(1,128)}, f32[3,1,1,1,32]{4,3,2,1,0:T(1,128)S(1)}, u32[]{:S(2)}, u32[]{:S(2)}) collective-permute-start(f32[3,1,1,1,32]{4,3,2,1,0:T(1,128)} %param.21), channel_id=1, source_target_pairs={{64,0},{128,64},{192,128},{256,192},{320,256},{384,320},{448,384},... | collective-permute-start | bytes 1160 | tf_op jit(solution)/shard_map/ppermute | solution.py:20
  10.9 5.4 %collective-permute-start.7 = (bf16[1,1,1,32,128]{4,3,2,1,0:T(8,128)(2,1)S(1)}, bf16[1,1,1,32,128]{4,3,2,1,0:T(8,128)(2,1)S(1)}, u32[]{:S(2)}, u32[]{:S(2)}) collective-permute-start(bf16[1,1,1,32,128]{4,3,2,1,0:T(8,128)(2,1)S(1)} %bitcast.235), channel_id=1, source_target_pairs={{64,0},{128,64},{192,128},{256,192},{320,256},{384,320},{448,384},... | collective-permute-start | bytes 24584 | tf_op jit(solution)/shard_map/ppermute | solution.py:20
  22.7 5.4 %collective-permute-start.3 = (f32[3,3,1,1,32]{4,3,2,1,0:T(1,128)S(1)}, f32[3,3,1,1,32]{4,3,2,1,0:T(1,128)S(1)}, u32[]{:S(2)}, u32[]{:S(2)}) collective-permute-start(f32[3,3,1,1,32]{4,3,2,1,0:T(1,128)S(1)} %constant_dynamic-update-slice_fusion), channel_id=1, source_target_pairs={{8,0},{16,8},{24,16},{32,24},{40,32},{48,40},{56,48},{0,56},{9,1},... | collective-permute-start | bytes 3464 | tf_op jit(solution)/shard_map/ppermute | solution.py:20
  30.0 4.8 %collective-permute-done.2 = f32[3,3,1,1,32]{4,3,2,1,0:T(1,128)S(1)} collective-permute-done((f32[3,3,1,1,32]{4,3,2,1,0:T(1,128)S(1)}, f32[3,3,1,1,32]{4,3,2,1,0:T(1,128)S(1)}, u32[]{:S(2)}, u32[]{:S(2)}) %collective-permute-start.2) | collective-permute-done | bytes 1184 | tf_op jit(solution)/shard_map/ppermute | solution.py:18
  34.8 8.2 %collective-permute-start.5 = (f32[3,3,3,1,32]{4,3,2,1,0:T(1,128)S(1)}, f32[3,3,3,1,32]{4,3,2,1,0:T(1,128)S(1)}, u32[]{:S(2)}, u32[]{:S(2)}) collective-permute-start(f32[3,3,3,1,32]{4,3,2,1,0:T(1,128)S(1)} %pad_maximum_fusion.34), channel_id=1, source_target_pairs={{1,0},{2,1},{3,2},{4,3},{5,4},{6,5},{7,6},{0,7},{9,8},{10,9},{11,1... | collective-permute-start | bytes 10376 | tf_op jit(solution)/shard_map/ppermute | solution.py:20
  47.0 3.1 gather_fusion.3
  50.4 3.0 collective-permute-done.4
  53.7 3.1 gather_fusion.2
  59.1 2.4 fusion.75
  64.3 3.8 %collective-permute-start.8 = (bf16[3,1,1,32,128]{4,3,2,1,0:T(8,128)(2,1)S(1)}, bf16[3,1,1,32,128]{4,3,2,1,0:T(8,128)(2,1)S(1)}, u32[]{:S(2)}, u32[]{:S(2)}) collective-permute-start(bf16[3,1,1,32,128]{4,3,2,1,0:T(8,128)(2,1)S(1)} %pad_maximum_fusion.32), channel_id=1, source_target_pairs={{0,8},{8,16},{16,24},{24,32},{32,40},{40,48},{48,56},{56,0},{1,9},... | collective-permute-start | bytes 73736 | tf_op jit(solution)/shard_map/ppermute | solution.py:18
  68.1 3.1 collective-permute-done.8
  71.3 5.8 %collective-permute-start.11 = (bf16[3,3,1,32,128]{4,3,2,1,0:T(8,128)(2,1)S(1)}, bf16[3,3,1,32,128]{4,3,2,1,0:T(8,128)(2,1)S(1)}, u32[]{:S(2)}, u32[]{:S(2)}) collective-permute-start(bf16[3,3,1,32,128]{4,3,2,1,0:T(8,128)(2,1)S(1)} %pad_maximum_fusion.13), channel_id=1, source_target_pairs={{1,0},{2,1},{3,2},{4,3},{5,4},{6,5},{7,6},{0,7},{9,8},{10,9},{11,1... | collective-permute-start | bytes 221192 | tf_op jit(solution)/shard_map/ppermute | solution.py:20
  77.1 4.4 %collective-permute-start.10 = (bf16[3,3,1,32,128]{4,3,2,1,0:T(8,128)(2,1)S(1)}, bf16[3,3,1,32,128]{4,3,2,1,0:T(8,128)(2,1)S(1)}, u32[]{:S(2)}, u32[]{:S(2)}) collective-permute-start(bf16[3,3,1,32,128]{4,3,2,1,0:T(8,128)(2,1)S(1)} %pad_maximum_fusion.13), channel_id=1, source_target_pairs={{0,1},{1,2},{2,3},{3,4},{4,5},{5,6},{6,7},{7,0},{8,9},{9,10},{10,1... | collective-permute-start | bytes 221192 | tf_op jit(solution)/shard_map/ppermute | solution.py:18
  81.5 5.7 %broadcast_multiply_fusion.1 = (f32[1792,384]{0,1:T(8,128)}, f32[1792,384]{0,1:T(8,128)}, f32[1792,384]{0,1:T(8,128)}) fusion(f32[1792]{0:T(1024)S(1)} %multiply_select_fusion, f32[1792,384]{0,1:T(8,128)S(1)} %fusion.75, f32[2,64,384]{2,1,0:T(8,128)S(1)} %copy-done.24, f32[1792,64]{0,1:T(8,128)S(1)} %fusion.133), kind=kOutput, calls=%fused_computation.53 | convolution fusion | flops 530317312 | bytes 11575296 | tf_op jit(solution)/shard_map/jvp()/dot_general | solution.py:62
  88.6 4.2 %gather_fusion = f32[1792,128]{1,0:T(8,128)} fusion(f32[864,128]{1,0:T(8,128)S(1)} %fusion.119, s32[2048]{0:T(1024)S(1)} %get-tuple-element.87), kind=kCustom, calls=%fused_computation.2 | custom fusion | bytes 1842176 | tf_op jit(solution)/shard_map/jvp(jit(_take))/gather | solution.py:63
  94.3 2.8 multiply_reduce_fusion.5
  97.1 3.0 multiply_reduce_fusion.3
  104.5 2.4 collective-permute-start.12
  106.9 4.3 %collective-permute-done.12 = bf16[1,1,1,32,128]{4,3,2,1,0:T(8,128)(2,1)S(1)} collective-permute-done((bf16[1,1,1,32,128]{4,3,2,1,0:T(8,128)(2,1)S(1)}, bf16[1,1,1,32,128]{4,3,2,1,0:T(8,128)(2,1)S(1)}, u32[]{:S(2)}, u32[]{:S(2)}) %collective-permute-start.12) | collective-permute-done | bytes 8224 | tf_op jit(solution)/shard_map/ppermute | solution.py:18
  113.3 3.8 %collective-permute-start.14 = (bf16[3,1,1,32,128]{4,3,2,1,0:T(8,128)(2,1)S(1)}, bf16[3,1,1,32,128]{4,3,2,1,0:T(8,128)(2,1)S(1)}, u32[]{:S(2)}, u32[]{:S(2)}) collective-permute-start(bf16[3,1,1,32,128]{4,3,2,1,0:T(8,128)(2,1)S(1)} %pad_maximum_fusion.33), channel_id=1, source_target_pairs={{0,8},{8,16},{16,24},{24,32},{32,40},{40,48},{48,56},{56,0},{1,9},... | collective-permute-start | bytes 73736 | tf_op jit(solution)/shard_map/ppermute | solution.py:18
  117.8 2.4 collective-permute-done.14
  120.3 5.7 %collective-permute-start.17 = (bf16[3,3,1,32,128]{4,3,2,1,0:T(8,128)(2,1)S(1)}, bf16[3,3,1,32,128]{4,3,2,1,0:T(8,128)(2,1)S(1)}, u32[]{:S(2)}, u32[]{:S(2)}) collective-permute-start(bf16[3,3,1,32,128]{4,3,2,1,0:T(8,128)(2,1)S(1)} %pad_maximum_fusion.14), channel_id=1, source_target_pairs={{1,0},{2,1},{3,2},{4,3},{5,4},{6,5},{7,6},{0,7},{9,8},{10,9},{11,1... | collective-permute-start | bytes 221192 | tf_op jit(solution)/shard_map/ppermute | solution.py:20
  126.0 4.6 %collective-permute-start.16 = (bf16[3,3,1,32,128]{4,3,2,1,0:T(8,128)(2,1)S(1)}, bf16[3,3,1,32,128]{4,3,2,1,0:T(8,128)(2,1)S(1)}, u32[]{:S(2)}, u32[]{:S(2)}) collective-permute-start(bf16[3,3,1,32,128]{4,3,2,1,0:T(8,128)(2,1)S(1)} %pad_maximum_fusion.14), channel_id=1, source_target_pairs={{0,1},{1,2},{2,3},{3,4},{4,5},{5,6},{6,7},{7,0},{8,9},{9,10},{10,1... | collective-permute-start | bytes 221192 | tf_op jit(solution)/shard_map/ppermute | solution.py:18
  132.5 4.5 %collective-permute-done.16 = bf16[3,3,1,32,128]{4,3,2,1,0:T(8,128)(2,1)S(1)} collective-permute-done((bf16[3,3,1,32,128]{4,3,2,1,0:T(8,128)(2,1)S(1)}, bf16[3,3,1,32,128]{4,3,2,1,0:T(8,128)(2,1)S(1)}, u32[]{:S(2)}, u32[]{:S(2)}) %collective-permute-start.16) | collective-permute-done | bytes 73760 | tf_op jit(solution)/shard_map/ppermute | solution.py:18
  137.4 3.7 gather_fusion.1
  156.6 2.6 fusion.4
  159.2 3.1 fusion.60
  163.5 13.5 %scatter_custom_fusion = f32[864,128]{1,0:T(8,128)S(1)} fusion(s32[1792]{0:T(1024)} %copy-done.43, f32[1792,128]{1,0:T(8,128)} %copy.187, f32[]{:T(128)} %constant.98.clone.1), kind=kCustom, calls=%fused_computation.152 | custom fusion | flops 229376 | bytes 442880 | tf_op jit(solution)/shard_map/transpose(jvp(jit(_take)))/scatter-add | solution.py:63
  180.4 2.5 collective-permute-start.18
  182.9 4.0 %fusion.22 = f32[9,1792]{1,0:T(8,128)S(1)} fusion(f32[1,32,1792]{2,1,0:T(8,128)} %convolution_bitcast_fusion.4, f32[9,32,1792]{2,1,0:T(8,128)} %fusion.60, f32[32,1792]{1,0:T(8,128)S(1)} %fusion.88, f32[1792,384]{0,1:T(8,128)} %get-tuple-element.71, f32[1792,128]{0,1:T(8,128)S(1)} %copy.184, pred[1792]{0:T(1024)(128)(4,1)S(1)} %get-tuple-element.90, ...), kind=kOutput, calls=%fused_computation.48 | convolution fusion | flops 266760448 | bytes 4489984 | tf_op jit(solution)/shard_map/transpose(jvp())/pad | solution.py:84
  190.8 5.1 %collective-permute-start.21 = (f32[5,1,3,32,128]{4,3,2,1,0:T(8,128)S(1)}, f32[5,1,3,32,128]{4,3,2,1,0:T(8,128)S(1)}, u32[]{:S(2)}, u32[]{:S(2)}) collective-permute-start(f32[5,1,3,32,128]{4,3,2,1,0:T(8,128)S(1)} %get-tuple-element.29), channel_id=1, source_target_pairs={{8,0},{16,8},{24,16},{32,24},{40,32},{48,40},{56,48},{0,56},{9,1},... | collective-permute-start | bytes 737288 | tf_op jit(solution)/shard_map/ppermute | solution.py:20
  199.6 3.7 %collective-permute-start.22 = (f32[5,5,1,32,128]{4,3,2,1,0:T(8,128)S(1)}, f32[5,5,1,32,128]{4,3,2,1,0:T(8,128)S(1)}, u32[]{:S(2)}, u32[]{:S(2)}) collective-permute-start(f32[5,5,1,32,128]{4,3,2,1,0:T(8,128)S(1)} %get-tuple-element.22), channel_id=1, source_target_pairs={{0,1},{1,2},{2,3},{3,4},{4,5},{5,6},{6,7},{7,0},{8,9},{9,10},{10,1... | collective-permute-start | bytes 1228808 | tf_op jit(solution)/shard_map/ppermute | solution.py:18
  203.4 6.9 %collective-permute-start.23 = (f32[5,5,1,32,128]{4,3,2,1,0:T(8,128)S(1)}, f32[5,5,1,32,128]{4,3,2,1,0:T(8,128)S(1)}, u32[]{:S(2)}, u32[]{:S(2)}) collective-permute-start(f32[5,5,1,32,128]{4,3,2,1,0:T(8,128)S(1)} %get-tuple-element.23), channel_id=1, source_target_pairs={{1,0},{2,1},{3,2},{4,3},{5,4},{6,5},{7,6},{0,7},{9,8},{10,9},{11,1... | collective-permute-start | bytes 1228808 | tf_op jit(solution)/shard_map/ppermute | solution.py:20
  210.4 19.9 %collective-permute-done.22 = f32[5,5,1,32,128]{4,3,2,1,0:T(8,128)S(1)} collective-permute-done((f32[5,5,1,32,128]{4,3,2,1,0:T(8,128)S(1)}, f32[5,5,1,32,128]{4,3,2,1,0:T(8,128)S(1)}, u32[]{:S(2)}, u32[]{:S(2)}) %collective-permute-start.22) | collective-permute-done | bytes 409632 | tf_op jit(solution)/shard_map/ppermute | solution.py:18
  230.3 7.8 %collective-permute-done.23 = f32[5,5,1,32,128]{4,3,2,1,0:T(8,128)S(1)} collective-permute-done((f32[5,5,1,32,128]{4,3,2,1,0:T(8,128)S(1)}, f32[5,5,1,32,128]{4,3,2,1,0:T(8,128)S(1)}, u32[]{:S(2)}, u32[]{:S(2)}) %collective-permute-start.23) | collective-permute-done | bytes 409632 | tf_op jit(solution)/shard_map/ppermute | solution.py:20
  251.7 13.4 %scatter_custom_fusion.3 = f32[3,864]{0,1:T(8,128)S(1)} fusion(s32[1792]{0:T(1024)} %copy-done.41, f32[1792,3]{1,0:T(8,128)S(1)} %copy.196, f32[]{:T(128)} %constant.98.clone.1), kind=kCustom, calls=%fused_computation.150 | custom fusion | flops 5376 | bytes 10880 | tf_op jit(solution)/shard_map/transpose(jvp(jit(_take)))/scatter-add | solution.py:52
  267.3 5.4 %collective-permute-start.25 = (f32[1,3,3,32,3]{3,4,2,1,0:T(4,128)S(1)}, f32[1,3,3,32,3]{3,4,2,1,0:T(4,128)S(1)}, u32[]{:S(2)}, u32[]{:S(2)}) collective-permute-start(f32[1,3,3,32,3]{3,4,2,1,0:T(4,128)S(1)} %get-tuple-element.51), channel_id=1, source_target_pairs={{64,0},{128,64},{192,128},{256,192},{320,256},{384,320},{448,384},... | collective-permute-start | bytes 10376 | tf_op jit(solution)/shard_map/ppermute | solution.py:20
  273.0 13.2 %scatter_custom_fusion.4 = f32[3,864]{0,1:T(8,128)S(1)} fusion(s32[1792]{0:T(1024)} %copy-done.41, f32[1792,3]{1,0:T(8,128)S(1)} %copy.198, f32[]{:T(128)} %constant.98.clone.1), kind=kCustom, calls=%fused_computation.148 | custom fusion | flops 5376 | bytes 10880 | tf_op jit(solution)/shard_map/transpose(jvp(jit(_take)))/scatter-add | solution.py:52
  286.8 14.4 %scatter_custom_fusion.2 = f32[3,32]{0,1:T(8,128)S(1)} fusion(s32[1792]{0:T(1024)} %copy-done.42, f32[1792,3]{1,0:T(8,128)S(1)} %copy.193, f32[]{:T(128)} %constant.98.clone.1), kind=kCustom, calls=%fused_computation.280 | custom fusion | flops 5376 | bytes 896 | tf_op jit(solution)/shard_map/transpose(jvp(jit(_take)))/scatter-add | solution.py:52
  303.3 5.4 %collective-permute-start.31 = (f32[1,3,3,32,3]{3,4,2,1,0:T(4,128)S(1)}, f32[1,3,3,32,3]{3,4,2,1,0:T(4,128)S(1)}, u32[]{:S(2)}, u32[]{:S(2)}) collective-permute-start(f32[1,3,3,32,3]{3,4,2,1,0:T(4,128)S(1)} %get-tuple-element.49), channel_id=1, source_target_pairs={{64,0},{128,64},{192,128},{256,192},{320,256},{384,320},{448,384},... | collective-permute-start | bytes 10376 | tf_op jit(solution)/shard_map/ppermute | solution.py:20
  309.1 14.4 %scatter_custom_fusion.1 = f32[3,32]{0,1:T(8,128)S(1)} fusion(s32[1792]{0:T(1024)} %copy-done.42, f32[1792,3]{1,0:T(8,128)S(1)} %copy.190, f32[]{:T(128)} %constant.98.clone.1), kind=kCustom, calls=%fused_computation.282 | custom fusion | flops 5376 | bytes 896 | tf_op jit(solution)/shard_map/transpose(jvp(jit(_take)))/scatter-add | solution.py:52
  325.6 5.1 %collective-permute-start.27 = (f32[5,1,3,32,3]{3,4,2,1,0:T(4,128)S(1)}, f32[5,1,3,32,3]{3,4,2,1,0:T(4,128)S(1)}, u32[]{:S(2)}, u32[]{:S(2)}) collective-permute-start(f32[5,1,3,32,3]{3,4,2,1,0:T(4,128)S(1)} %get-tuple-element.43), channel_id=1, source_target_pairs={{8,0},{16,8},{24,16},{32,24},{40,32},{48,40},{56,48},{0,56},{9,1},... | collective-permute-start | bytes 17288 | tf_op jit(solution)/shard_map/ppermute | solution.py:20
  330.7 2.4 collective-permute-start.32
  333.2 4.6 %collective-permute-start.33 = (f32[5,1,3,32,3]{3,4,2,1,0:T(4,128)S(1)}, f32[5,1,3,32,3]{3,4,2,1,0:T(4,128)S(1)}, u32[]{:S(2)}, u32[]{:S(2)}) collective-permute-start(f32[5,1,3,32,3]{3,4,2,1,0:T(4,128)S(1)} %get-tuple-element.41), channel_id=1, source_target_pairs={{8,0},{16,8},{24,16},{32,24},{40,32},{48,40},{56,48},{0,56},{9,1},... | collective-permute-start | bytes 17288 | tf_op jit(solution)/shard_map/ppermute | solution.py:20
  337.9 9.7 %collective-permute-start.28 = (f32[5,5,1,32,3]{3,4,2,1,0:T(4,128)S(1)}, f32[5,5,1,32,3]{3,4,2,1,0:T(4,128)S(1)}, u32[]{:S(2)}, u32[]{:S(2)}) collective-permute-start(f32[5,5,1,32,3]{3,4,2,1,0:T(4,128)S(1)} %get-tuple-element.34), channel_id=1, source_target_pairs={{0,1},{1,2},{2,3},{3,4},{4,5},{5,6},{6,7},{7,0},{8,9},{9,10},{10,1... | collective-permute-start | bytes 28808 | tf_op jit(solution)/shard_map/ppermute | solution.py:18
  349.6 7.9 %collective-permute-start.34 = (f32[5,5,1,32,3]{3,4,2,1,0:T(4,128)S(1)}, f32[5,5,1,32,3]{3,4,2,1,0:T(4,128)S(1)}, u32[]{:S(2)}, u32[]{:S(2)}) collective-permute-start(f32[5,5,1,32,3]{3,4,2,1,0:T(4,128)S(1)} %get-tuple-element.32), channel_id=1, source_target_pairs={{0,1},{1,2},{2,3},{3,4},{4,5},{5,6},{6,7},{7,0},{8,9},{9,10},{10,1... | collective-permute-start | bytes 28808 | tf_op jit(solution)/shard_map/ppermute | solution.py:18
  357.5 2.7 collective-permute-start.35
  360.4 7.9 %collective-permute-done.35 = f32[5,5,1,32,3]{3,4,2,1,0:T(4,128)S(1)} collective-permute-done((f32[5,5,1,32,3]{3,4,2,1,0:T(4,128)S(1)}, f32[5,5,1,32,3]{3,4,2,1,0:T(4,128)S(1)}, u32[]{:S(2)}, u32[]{:S(2)}) %collective-permute-start.35) | collective-permute-done | bytes 9632 | tf_op jit(solution)/shard_map/ppermute | solution.py:20
  (272 shorter events, 82.2 us)
Async XLA Ops:
  0.6 56.5 %copy-start.61 = (f32[3]{0:T(128)S(1)}, f32[3]{0:T(128)}, u32[]{:S(2)}) copy-start(f32[3]{0:T(128)} %constant.107.clone) | copy-start | bytes 40
  0.7 56.5 %copy-start.44 = (s32[3,1,1,1,1792]{4,3,2,1,0:T(1,128)S(1)}, s32[3,1,1,1,1792]{4,3,2,1,0:T(1,128)}, u32[]{:S(2)}) copy-start(s32[3,1,1,1,1792]{4,3,2,1,0:T(1,128)} %param.27) | copy-start | bytes 64516
  0.7 22.0 %collective-permute-start.1 = (f32[3,1,1,1,32]{4,3,2,1,0:T(1,128)}, f32[3,1,1,1,32]{4,3,2,1,0:T(1,128)S(1)}, u32[]{:S(2)}, u32[]{:S(2)}) collective-permute-start(f32[3,1,1,1,32]{4,3,2,1,0:T(1,128)} %param.21), channel_id=1, source_target_pairs={{64,0},{128,64},{192,128},{256,192},{320,256},{384,320},{448,384},... | collective-permute-start | bytes 1160 | tf_op jit(solution)/shard_map/ppermute | solution.py:20
  8.1 13.8 %collective-permute-start = (f32[3,1,1,1,32]{4,3,2,1,0:T(1,128)}, f32[3,1,1,1,32]{4,3,2,1,0:T(1,128)S(1)}, u32[]{:S(2)}, u32[]{:S(2)}) collective-permute-start(f32[3,1,1,1,32]{4,3,2,1,0:T(1,128)} %param.21), channel_id=1, source_target_pairs={{0,64},{64,128},{128,192},{192,256},{256,320},{320,384},{384,448},... | collective-permute-start | bytes 1160 | tf_op jit(solution)/shard_map/ppermute | solution.py:18
  10.9 77.2 %copy-start.28 = (bf16[32,128]{1,0:T(8,128)(2,1)}, bf16[32,128]{1,0:T(8,128)(2,1)S(1)}, u32[]{:S(2)}) copy-start(bf16[32,128]{1,0:T(8,128)(2,1)S(1)} %convolution_convert_fusion) | copy-start | bytes 24580
  10.9 51.2 %collective-permute-start.7 = (bf16[1,1,1,32,128]{4,3,2,1,0:T(8,128)(2,1)S(1)}, bf16[1,1,1,32,128]{4,3,2,1,0:T(8,128)(2,1)S(1)}, u32[]{:S(2)}, u32[]{:S(2)}) collective-permute-start(bf16[1,1,1,32,128]{4,3,2,1,0:T(8,128)(2,1)S(1)} %bitcast.235), channel_id=1, source_target_pairs={{64,0},{128,64},{192,128},{256,192},{320,256},{384,320},{448,384},... | collective-permute-start | bytes 24584 | tf_op jit(solution)/shard_map/ppermute | solution.py:20
  16.4 45.8 %collective-permute-start.6 = (bf16[1,1,1,32,128]{4,3,2,1,0:T(8,128)(2,1)S(1)}, bf16[1,1,1,32,128]{4,3,2,1,0:T(8,128)(2,1)S(1)}, u32[]{:S(2)}, u32[]{:S(2)}) collective-permute-start(bf16[1,1,1,32,128]{4,3,2,1,0:T(8,128)(2,1)S(1)} %bitcast.236), channel_id=1, source_target_pairs={{0,64},{64,128},{128,192},{192,256},{256,320},{320,384},{384,448},... | collective-permute-start | bytes 24584 | tf_op jit(solution)/shard_map/ppermute | solution.py:18
  19.0 38.1 %copy-start.43 = (s32[1792]{0:T(1024)}, s32[1792]{0:T(1024)S(1)}, u32[]{:S(2)}) copy-start(s32[1792]{0:T(1024)S(1)} %fusion.172) | copy-start | bytes 21508
  20.5 37.2 %copy-start.42 = (s32[1792]{0:T(1024)}, s32[1792]{0:T(1024)S(1)}, u32[]{:S(2)}) copy-start(s32[1792]{0:T(1024)S(1)} %compare_select_fusion.1) | copy-start | bytes 21508
  20.6 37.2 %copy-start.41 = (s32[1792]{0:T(1024)}, s32[1792]{0:T(1024)S(1)}, u32[]{:S(2)}) copy-start(s32[1792]{0:T(1024)S(1)} %compare_select_fusion.2) | copy-start | bytes 21508
  22.0 66.6 %copy-start.30 = (s32[2048]{0:T(1024)}, s32[2048]{0:T(1024)S(1)}, u32[]{:S(2)}) copy-start(s32[2048]{0:T(1024)S(1)} %get-tuple-element.87) | copy-start | bytes 24580
  22.7 7.3 %collective-permute-start.3 = (f32[3,3,1,1,32]{4,3,2,1,0:T(1,128)S(1)}, f32[3,3,1,1,32]{4,3,2,1,0:T(1,128)S(1)}, u32[]{:S(2)}, u32[]{:S(2)}) collective-permute-start(f32[3,3,1,1,32]{4,3,2,1,0:T(1,128)S(1)} %constant_dynamic-update-slice_fusion), channel_id=1, source_target_pairs={{8,0},{16,8},{24,16},{32,24},{40,32},{48,40},{56,48},{0,56},{9,1},... | collective-permute-start | bytes 3464 | tf_op jit(solution)/shard_map/ppermute | solution.py:20
  28.1 6.7 %collective-permute-start.2 = (f32[3,3,1,1,32]{4,3,2,1,0:T(1,128)S(1)}, f32[3,3,1,1,32]{4,3,2,1,0:T(1,128)S(1)}, u32[]{:S(2)}, u32[]{:S(2)}) collective-permute-start(f32[3,3,1,1,32]{4,3,2,1,0:T(1,128)S(1)} %constant_dynamic-update-slice_fusion), channel_id=1, source_target_pairs={{0,8},{8,16},{16,24},{24,32},{32,40},{40,48},{48,56},{56,0},{1,9},... | collective-permute-start | bytes 3464 | tf_op jit(solution)/shard_map/ppermute | solution.py:18
  34.8 15.6 %collective-permute-start.5 = (f32[3,3,3,1,32]{4,3,2,1,0:T(1,128)S(1)}, f32[3,3,3,1,32]{4,3,2,1,0:T(1,128)S(1)}, u32[]{:S(2)}, u32[]{:S(2)}) collective-permute-start(f32[3,3,3,1,32]{4,3,2,1,0:T(1,128)S(1)} %pad_maximum_fusion.34), channel_id=1, source_target_pairs={{1,0},{2,1},{3,2},{4,3},{5,4},{6,5},{7,6},{0,7},{9,8},{10,9},{11,1... | collective-permute-start | bytes 10376 | tf_op jit(solution)/shard_map/ppermute | solution.py:20
  43.0 10.4 %collective-permute-start.4 = (f32[3,3,3,1,32]{4,3,2,1,0:T(1,128)S(1)}, f32[3,3,3,1,32]{4,3,2,1,0:T(1,128)S(1)}, u32[]{:S(2)}, u32[]{:S(2)}) collective-permute-start(f32[3,3,3,1,32]{4,3,2,1,0:T(1,128)S(1)} %pad_maximum_fusion.34), channel_id=1, source_target_pairs={{0,1},{1,2},{2,3},{3,4},{4,5},{5,6},{6,7},{7,0},{8,9},{9,10},{10,1... | collective-permute-start | bytes 10376 | tf_op jit(solution)/shard_map/ppermute | solution.py:18
  57.7 42.4 %copy-start.6 = (f32[9,32,1792]{2,1,0:T(8,128)}, f32[9,32,1792]{2,1,0:T(8,128)S(1)}, u32[]{:S(2)}) copy-start(f32[9,32,1792]{2,1,0:T(8,128)S(1)} %multiply_multiply_fusion) | copy-start | bytes 6193156
  59.1 28.1 %copy-start.7 = (f32[1792,64]{0,1:T(8,128)}, f32[1792,64]{0,1:T(8,128)S(1)}, u32[]{:S(2)}) copy-start(f32[1792,64]{0,1:T(8,128)S(1)} %fusion.131) | copy-start | bytes 1376260
  62.2 5.9 %collective-permute-start.9 = (bf16[3,1,1,32,128]{4,3,2,1,0:T(8,128)(2,1)S(1)}, bf16[3,1,1,32,128]{4,3,2,1,0:T(8,128)(2,1)S(1)}, u32[]{:S(2)}, u32[]{:S(2)}) collective-permute-start(bf16[3,1,1,32,128]{4,3,2,1,0:T(8,128)(2,1)S(1)} %pad_maximum_fusion.32), channel_id=1, source_target_pairs={{8,0},{16,8},{24,16},{32,24},{40,32},{48,40},{56,48},{0,56},{9,1},... | collective-permute-start | bytes 73736 | tf_op jit(solution)/shard_map/ppermute | solution.py:20
  64.3 6.9 %collective-permute-start.8 = (bf16[3,1,1,32,128]{4,3,2,1,0:T(8,128)(2,1)S(1)}, bf16[3,1,1,32,128]{4,3,2,1,0:T(8,128)(2,1)S(1)}, u32[]{:S(2)}, u32[]{:S(2)}) collective-permute-start(bf16[3,1,1,32,128]{4,3,2,1,0:T(8,128)(2,1)S(1)} %pad_maximum_fusion.32), channel_id=1, source_target_pairs={{0,8},{8,16},{16,24},{24,32},{32,40},{40,48},{48,56},{56,0},{1,9},... | collective-permute-start | bytes 73736 | tf_op jit(solution)/shard_map/ppermute | solution.py:18
  71.3 15.9 %collective-permute-start.11 = (bf16[3,3,1,32,128]{4,3,2,1,0:T(8,128)(2,1)S(1)}, bf16[3,3,1,32,128]{4,3,2,1,0:T(8,128)(2,1)S(1)}, u32[]{:S(2)}, u32[]{:S(2)}) collective-permute-start(bf16[3,3,1,32,128]{4,3,2,1,0:T(8,128)(2,1)S(1)} %pad_maximum_fusion.13), channel_id=1, source_target_pairs={{1,0},{2,1},{3,2},{4,3},{5,4},{6,5},{7,6},{0,7},{9,8},{10,9},{11,1... | collective-permute-start | bytes 221192 | tf_op jit(solution)/shard_map/ppermute | solution.py:20
  77.1 11.1 %collective-permute-start.10 = (bf16[3,3,1,32,128]{4,3,2,1,0:T(8,128)(2,1)S(1)}, bf16[3,3,1,32,128]{4,3,2,1,0:T(8,128)(2,1)S(1)}, u32[]{:S(2)}, u32[]{:S(2)}) collective-permute-start(bf16[3,3,1,32,128]{4,3,2,1,0:T(8,128)(2,1)S(1)} %pad_maximum_fusion.13), channel_id=1, source_target_pairs={{0,1},{1,2},{2,3},{3,4},{4,5},{5,6},{6,7},{7,0},{8,9},{9,10},{10,1... | collective-permute-start | bytes 221192 | tf_op jit(solution)/shard_map/ppermute | solution.py:18
  100.1 36.9 %copy-start.16 = (f32[2,128,128]{2,1,0:T(8,128)S(1)}, f32[2,128,128]{2,1,0:T(8,128)}, u32[]{:S(2)}) copy-start(f32[2,128,128]{2,1,0:T(8,128)} %param.31) | copy-start | bytes 393220
  102.6 4.3 %collective-permute-start.13 = (bf16[1,1,1,32,128]{4,3,2,1,0:T(8,128)(2,1)S(1)}, bf16[1,1,1,32,128]{4,3,2,1,0:T(8,128)(2,1)S(1)}, u32[]{:S(2)}, u32[]{:S(2)}) collective-permute-start(bf16[1,1,1,32,128]{4,3,2,1,0:T(8,128)(2,1)S(1)} %convert_bitcast_fusion), channel_id=1, source_target_pairs={{64,0},{128,64},{192,128},{256,192},{320,256},{384,320},{448,384},... | collective-permute-start | bytes 24584 | tf_op jit(solution)/shard_map/ppermute | solution.py:20
  104.5 6.8 %collective-permute-start.12 = (bf16[1,1,1,32,128]{4,3,2,1,0:T(8,128)(2,1)S(1)}, bf16[1,1,1,32,128]{4,3,2,1,0:T(8,128)(2,1)S(1)}, u32[]{:S(2)}, u32[]{:S(2)}) collective-permute-start(bf16[1,1,1,32,128]{4,3,2,1,0:T(8,128)(2,1)S(1)} %convert_bitcast_fusion), channel_id=1, source_target_pairs={{0,64},{64,128},{128,192},{192,256},{256,320},{320,384},{384,448},... | collective-permute-start | bytes 24584 | tf_op jit(solution)/shard_map/ppermute | solution.py:18
  111.3 6.5 %collective-permute-start.15 = (bf16[3,1,1,32,128]{4,3,2,1,0:T(8,128)(2,1)S(1)}, bf16[3,1,1,32,128]{4,3,2,1,0:T(8,128)(2,1)S(1)}, u32[]{:S(2)}, u32[]{:S(2)}) collective-permute-start(bf16[3,1,1,32,128]{4,3,2,1,0:T(8,128)(2,1)S(1)} %pad_maximum_fusion.33), channel_id=1, source_target_pairs={{8,0},{16,8},{24,16},{32,24},{40,32},{48,40},{56,48},{0,56},{9,1},... | collective-permute-start | bytes 73736 | tf_op jit(solution)/shard_map/ppermute | solution.py:20
  113.3 6.9 %collective-permute-start.14 = (bf16[3,1,1,32,128]{4,3,2,1,0:T(8,128)(2,1)S(1)}, bf16[3,1,1,32,128]{4,3,2,1,0:T(8,128)(2,1)S(1)}, u32[]{:S(2)}, u32[]{:S(2)}) collective-permute-start(bf16[3,1,1,32,128]{4,3,2,1,0:T(8,128)(2,1)S(1)} %pad_maximum_fusion.33), channel_id=1, source_target_pairs={{0,8},{8,16},{16,24},{24,32},{32,40},{40,48},{48,56},{56,0},{1,9},... | collective-permute-start | bytes 73736 | tf_op jit(solution)/shard_map/ppermute | solution.py:18
  120.3 12.2 %collective-permute-start.17 = (bf16[3,3,1,32,128]{4,3,2,1,0:T(8,128)(2,1)S(1)}, bf16[3,3,1,32,128]{4,3,2,1,0:T(8,128)(2,1)S(1)}, u32[]{:S(2)}, u32[]{:S(2)}) collective-permute-start(bf16[3,3,1,32,128]{4,3,2,1,0:T(8,128)(2,1)S(1)} %pad_maximum_fusion.14), channel_id=1, source_target_pairs={{1,0},{2,1},{3,2},{4,3},{5,4},{6,5},{7,6},{0,7},{9,8},{10,9},{11,1... | collective-permute-start | bytes 221192 | tf_op jit(solution)/shard_map/ppermute | solution.py:20
  126.0 11.1 %collective-permute-start.16 = (bf16[3,3,1,32,128]{4,3,2,1,0:T(8,128)(2,1)S(1)}, bf16[3,3,1,32,128]{4,3,2,1,0:T(8,128)(2,1)S(1)}, u32[]{:S(2)}, u32[]{:S(2)}) collective-permute-start(bf16[3,3,1,32,128]{4,3,2,1,0:T(8,128)(2,1)S(1)} %pad_maximum_fusion.14), channel_id=1, source_target_pairs={{0,1},{1,2},{2,3},{3,4},{4,5},{5,6},{6,7},{7,0},{8,9},{9,10},{10,1... | collective-permute-start | bytes 221192 | tf_op jit(solution)/shard_map/ppermute | solution.py:18
  178.4 8.7 %collective-permute-start.19 = (f32[1,3,3,32,128]{4,3,2,1,0:T(8,128)S(1)}, f32[1,3,3,32,128]{4,3,2,1,0:T(8,128)S(1)}, u32[]{:S(2)}, u32[]{:S(2)}) collective-permute-start(f32[1,3,3,32,128]{4,3,2,1,0:T(8,128)S(1)} %bitcast.234), channel_id=1, source_target_pairs={{64,0},{128,64},{192,128},{256,192},{320,256},{384,320},{448,384},... | collective-permute-start | bytes 442376 | tf_op jit(solution)/shard_map/ppermute | solution.py:20
  180.4 8.4 %collective-permute-start.18 = (f32[1,3,3,32,128]{4,3,2,1,0:T(8,128)S(1)}, f32[1,3,3,32,128]{4,3,2,1,0:T(8,128)S(1)}, u32[]{:S(2)}, u32[]{:S(2)}) collective-permute-start(f32[1,3,3,32,128]{4,3,2,1,0:T(8,128)S(1)} %bitcast.233), channel_id=1, source_target_pairs={{0,64},{64,128},{128,192},{192,256},{256,320},{320,384},{384,448},... | collective-permute-start | bytes 442376 | tf_op jit(solution)/shard_map/ppermute | solution.py:18
  188.8 9.3 %collective-permute-start.20 = (f32[5,1,3,32,128]{4,3,2,1,0:T(8,128)S(1)}, f32[5,1,3,32,128]{4,3,2,1,0:T(8,128)S(1)}, u32[]{:S(2)}, u32[]{:S(2)}) collective-permute-start(f32[5,1,3,32,128]{4,3,2,1,0:T(8,128)S(1)} %get-tuple-element.28), channel_id=1, source_target_pairs={{0,8},{8,16},{16,24},{24,32},{32,40},{40,48},{48,56},{56,0},{1,9},... | collective-permute-start | bytes 737288 | tf_op jit(solution)/shard_map/ppermute | solution.py:18
  190.8 8.8 %collective-permute-start.21 = (f32[5,1,3,32,128]{4,3,2,1,0:T(8,128)S(1)}, f32[5,1,3,32,128]{4,3,2,1,0:T(8,128)S(1)}, u32[]{:S(2)}, u32[]{:S(2)}) collective-permute-start(f32[5,1,3,32,128]{4,3,2,1,0:T(8,128)S(1)} %get-tuple-element.29), channel_id=1, source_target_pairs={{8,0},{16,8},{24,16},{32,24},{40,32},{48,40},{56,48},{0,56},{9,1},... | collective-permute-start | bytes 737288 | tf_op jit(solution)/shard_map/ppermute | solution.py:20
  199.6 30.7 %collective-permute-start.22 = (f32[5,5,1,32,128]{4,3,2,1,0:T(8,128)S(1)}, f32[5,5,1,32,128]{4,3,2,1,0:T(8,128)S(1)}, u32[]{:S(2)}, u32[]{:S(2)}) collective-permute-start(f32[5,5,1,32,128]{4,3,2,1,0:T(8,128)S(1)} %get-tuple-element.22), channel_id=1, source_target_pairs={{0,1},{1,2},{2,3},{3,4},{4,5},{5,6},{6,7},{7,0},{8,9},{9,10},{10,1... | collective-permute-start | bytes 1228808 | tf_op jit(solution)/shard_map/ppermute | solution.py:18
  203.4 34.7 %collective-permute-start.23 = (f32[5,5,1,32,128]{4,3,2,1,0:T(8,128)S(1)}, f32[5,5,1,32,128]{4,3,2,1,0:T(8,128)S(1)}, u32[]{:S(2)}, u32[]{:S(2)}) collective-permute-start(f32[5,5,1,32,128]{4,3,2,1,0:T(8,128)S(1)} %get-tuple-element.23), channel_id=1, source_target_pairs={{1,0},{2,1},{3,2},{4,3},{5,4},{6,5},{7,6},{0,7},{9,8},{10,9},{11,1... | collective-permute-start | bytes 1228808 | tf_op jit(solution)/shard_map/ppermute | solution.py:20
  210.4 27.9 %copy-start.36 = (f32[32,128]{1,0:T(8,128)S(1)}, f32[32,128]{1,0:T(8,128)}, u32[]{:S(2)}) copy-start(f32[32,128]{1,0:T(8,128)} %copy-done.35) | copy-start | bytes 49156
  210.4 27.9 %copy-start.51 = (f32[128]{0:T(128)S(1)}, f32[128]{0:T(128)}, u32[]{:S(2)}) copy-start(f32[128]{0:T(128)} %get-tuple-element.73) | copy-start | bytes 1540
  265.3 58.3 %collective-permute-start.24 = (f32[1,3,3,32,3]{3,4,2,1,0:T(4,128)S(1)}, f32[1,3,3,32,3]{3,4,2,1,0:T(4,128)S(1)}, u32[]{:S(2)}, u32[]{:S(2)}) collective-permute-start(f32[1,3,3,32,3]{3,4,2,1,0:T(4,128)S(1)} %get-tuple-element.50), channel_id=1, source_target_pairs={{0,64},{64,128},{128,192},{192,256},{256,320},{320,384},{384,448},... | collective-permute-start | bytes 10376 | tf_op jit(solution)/shard_map/ppermute | solution.py:18
  267.3 56.3 %collective-permute-start.25 = (f32[1,3,3,32,3]{3,4,2,1,0:T(4,128)S(1)}, f32[1,3,3,32,3]{3,4,2,1,0:T(4,128)S(1)}, u32[]{:S(2)}, u32[]{:S(2)}) collective-permute-start(f32[1,3,3,32,3]{3,4,2,1,0:T(4,128)S(1)} %get-tuple-element.51), channel_id=1, source_target_pairs={{64,0},{128,64},{192,128},{256,192},{320,256},{384,320},{448,384},... | collective-permute-start | bytes 10376 | tf_op jit(solution)/shard_map/ppermute | solution.py:20
  301.4 29.3 %collective-permute-start.30 = (f32[1,3,3,32,3]{3,4,2,1,0:T(4,128)S(1)}, f32[1,3,3,32,3]{3,4,2,1,0:T(4,128)S(1)}, u32[]{:S(2)}, u32[]{:S(2)}) collective-permute-start(f32[1,3,3,32,3]{3,4,2,1,0:T(4,128)S(1)} %get-tuple-element.48), channel_id=1, source_target_pairs={{0,64},{64,128},{128,192},{192,256},{256,320},{320,384},{384,448},... | collective-permute-start | bytes 10376 | tf_op jit(solution)/shard_map/ppermute | solution.py:18
  303.3 27.4 %collective-permute-start.31 = (f32[1,3,3,32,3]{3,4,2,1,0:T(4,128)S(1)}, f32[1,3,3,32,3]{3,4,2,1,0:T(4,128)S(1)}, u32[]{:S(2)}, u32[]{:S(2)}) collective-permute-start(f32[1,3,3,32,3]{3,4,2,1,0:T(4,128)S(1)} %get-tuple-element.49), channel_id=1, source_target_pairs={{64,0},{128,64},{192,128},{256,192},{320,256},{384,320},{448,384},... | collective-permute-start | bytes 10376 | tf_op jit(solution)/shard_map/ppermute | solution.py:20
  323.6 14.2 %collective-permute-start.26 = (f32[5,1,3,32,3]{3,4,2,1,0:T(4,128)S(1)}, f32[5,1,3,32,3]{3,4,2,1,0:T(4,128)S(1)}, u32[]{:S(2)}, u32[]{:S(2)}) collective-permute-start(f32[5,1,3,32,3]{3,4,2,1,0:T(4,128)S(1)} %get-tuple-element.42), channel_id=1, source_target_pairs={{0,8},{8,16},{16,24},{24,32},{32,40},{40,48},{48,56},{56,0},{1,9},... | collective-permute-start | bytes 17288 | tf_op jit(solution)/shard_map/ppermute | solution.py:18
  325.6 12.3 %collective-permute-start.27 = (f32[5,1,3,32,3]{3,4,2,1,0:T(4,128)S(1)}, f32[5,1,3,32,3]{3,4,2,1,0:T(4,128)S(1)}, u32[]{:S(2)}, u32[]{:S(2)}) collective-permute-start(f32[5,1,3,32,3]{3,4,2,1,0:T(4,128)S(1)} %get-tuple-element.43), channel_id=1, source_target_pairs={{8,0},{16,8},{24,16},{32,24},{40,32},{48,40},{56,48},{0,56},{9,1},... | collective-permute-start | bytes 17288 | tf_op jit(solution)/shard_map/ppermute | solution.py:20
  330.7 18.8 %collective-permute-start.32 = (f32[5,1,3,32,3]{3,4,2,1,0:T(4,128)S(1)}, f32[5,1,3,32,3]{3,4,2,1,0:T(4,128)S(1)}, u32[]{:S(2)}, u32[]{:S(2)}) collective-permute-start(f32[5,1,3,32,3]{3,4,2,1,0:T(4,128)S(1)} %get-tuple-element.40), channel_id=1, source_target_pairs={{0,8},{8,16},{16,24},{24,32},{32,40},{40,48},{48,56},{56,0},{1,9},... | collective-permute-start | bytes 17288 | tf_op jit(solution)/shard_map/ppermute | solution.py:18
  333.2 16.3 %collective-permute-start.33 = (f32[5,1,3,32,3]{3,4,2,1,0:T(4,128)S(1)}, f32[5,1,3,32,3]{3,4,2,1,0:T(4,128)S(1)}, u32[]{:S(2)}, u32[]{:S(2)}) collective-permute-start(f32[5,1,3,32,3]{3,4,2,1,0:T(4,128)S(1)} %get-tuple-element.41), channel_id=1, source_target_pairs={{8,0},{16,8},{24,16},{32,24},{40,32},{48,40},{56,48},{0,56},{9,1},... | collective-permute-start | bytes 17288 | tf_op jit(solution)/shard_map/ppermute | solution.py:20
  337.9 22.4 %collective-permute-start.28 = (f32[5,5,1,32,3]{3,4,2,1,0:T(4,128)S(1)}, f32[5,5,1,32,3]{3,4,2,1,0:T(4,128)S(1)}, u32[]{:S(2)}, u32[]{:S(2)}) collective-permute-start(f32[5,5,1,32,3]{3,4,2,1,0:T(4,128)S(1)} %get-tuple-element.34), channel_id=1, source_target_pairs={{0,1},{1,2},{2,3},{3,4},{4,5},{5,6},{6,7},{7,0},{8,9},{9,10},{10,1... | collective-permute-start | bytes 28808 | tf_op jit(solution)/shard_map/ppermute | solution.py:18
  347.6 12.7 %collective-permute-start.29 = (f32[5,5,1,32,3]{3,4,2,1,0:T(4,128)S(1)}, f32[5,5,1,32,3]{3,4,2,1,0:T(4,128)S(1)}, u32[]{:S(2)}, u32[]{:S(2)}) collective-permute-start(f32[5,5,1,32,3]{3,4,2,1,0:T(4,128)S(1)} %get-tuple-element.35), channel_id=1, source_target_pairs={{1,0},{2,1},{3,2},{4,3},{5,4},{6,5},{7,6},{0,7},{9,8},{10,9},{11,1... | collective-permute-start | bytes 28808 | tf_op jit(solution)/shard_map/ppermute | solution.py:20
  349.6 10.8 %collective-permute-start.34 = (f32[5,5,1,32,3]{3,4,2,1,0:T(4,128)S(1)}, f32[5,5,1,32,3]{3,4,2,1,0:T(4,128)S(1)}, u32[]{:S(2)}, u32[]{:S(2)}) collective-permute-start(f32[5,5,1,32,3]{3,4,2,1,0:T(4,128)S(1)} %get-tuple-element.32), channel_id=1, source_target_pairs={{0,1},{1,2},{2,3},{3,4},{4,5},{5,6},{6,7},{7,0},{8,9},{9,10},{10,1... | collective-permute-start | bytes 28808 | tf_op jit(solution)/shard_map/ppermute | solution.py:18
  357.5 10.8 %collective-permute-start.35 = (f32[5,5,1,32,3]{3,4,2,1,0:T(4,128)S(1)}, f32[5,5,1,32,3]{3,4,2,1,0:T(4,128)S(1)}, u32[]{:S(2)}, u32[]{:S(2)}) collective-permute-start(f32[5,5,1,32,3]{3,4,2,1,0:T(4,128)S(1)} %get-tuple-element.33), channel_id=1, source_target_pairs={{1,0},{2,1},{3,2},{4,3},{5,4},{6,5},{7,6},{0,7},{9,8},{10,9},{11,1... | collective-permute-start | bytes 28808 | tf_op jit(solution)/shard_map/ppermute | solution.py:20
  (53 other events, 495.3 us)
where the time goes:
time: 375 us; the launch traced here: 369 us
  starting transfers between devices  144 us (38%)
  other arithmetic  75.2 us (20%)
  waiting for transfers between devices  64.2 us (17%)
  matrix products  56.5 us (15%)
  local copies, waits for them, and re-layouts  25.5 us (7%)
  between operations  3.94 us (1%)
    ppermute x18, starting transfers between devices, padded(): lax.ppermute(head, axis, [((i + 1) % count, i) for i in range(count)])  83.2 us
    ppermute x18, starting transfers between devices, padded(): lax.ppermute(tail, axis, [(i, (i + 1) % count) for i in range(count)])  60.7 us
    ppermute x18, waiting for transfers between devices, padded(): lax.ppermute(tail, axis, [(i, (i + 1) % count) for i in range(count)])  45.7 us
    scatter-add x2, other arithmetic, layer(): jnp.take(own_pos, receiver, axis=1)  28.9 us
    scatter-add x2, other arithmetic, layer(): jnp.take(ghost_pos, sender, axis=1) + shift_len  26.6 us
    ppermute x18, waiting for transfers between devices, padded(): lax.ppermute(head, axis, [((i + 1) % count, i) for i in range(count)])  18.5 us
    scatter-add x1, other arithmetic, layer(): jnp.take(jnp.dot(ghost_h, w_lift, precision=lax.Precision.HIGHEST), sende...  13.5 us
    dot_general x4, matrix products, layer(): jnp.dot(hidden, w_out, precision=lax.Precision.HIGHEST) * envelope[:, None]  12.4 us
  transfers between devices with their start and end apart: 36, of which 14 were waited for; matrix products, arithmetic and copies ran while one was open for 20% of the time, Pallas kernels for 0%

commit v1 on v0

v1 whole, which is shorter than its diff:
```python
import functools

import jax
import jax.numpy as jnp
import numpy as np
from jax import lax
from jax.experimental import pallas as pl
from jax.experimental.pallas import tpu as pltpu
from jax.sharding import PartitionSpec as P

cutoff_radius = 5.0
lattice_step = 2.25
AXES = ("gx", "gy", "gz")
SIDE = 8
F32 = jnp.float32
BF16 = jnp.bfloat16
S3 = 3.0**0.5
S5 = 5.0**0.5
S15 = 15.0**0.5
HIGH = lax.Precision.HIGHEST


def place(a, b, d):
    return (a * SIDE + b) * SIDE + d


def home(a, b, d):
    return place((a % 4) * 2 + d % 2, b, (d // 2) * 2 + a // 4)


def bricks():
    return [(a, b, d) for a in range(SIDE) for b in range(SIDE) for d in range(SIDE)]


def move(x, pairs):
    return lax.ppermute(x, AXES, pairs)


def bring_home(step):
    return [(place((a + step) % SIDE, b, d), home(a, b, d)) for a, b, d in bricks()]


def send_back(step):
    return [(home(a, b, d), place((a + step) % SIDE, b, d)) for a, b, d in bricks()]


def shift(axis, step):
    pairs = []
    for cell in bricks():
        other = list(cell)
        other[axis] = (other[axis] + step) % SIDE
        pairs.append((home(*other), home(*cell)))
    return pairs


def widen(x, axis):
    return [move(x, shift(axis, -1)), x, move(x, shift(axis, 1))]


def nn(a, b, **kw):
    return lax.dot_general(a, b, (((1,), (0,)), ((), ())), preferred_element_type=F32, **kw)


def nt(a, b, **kw):
    return lax.dot_general(a, b, (((1,), (1,)), ((), ())), preferred_element_type=F32, **kw)


def tn(a, b, **kw):
    return lax.dot_general(a, b, (((0,), (0,)), ((), ())), preferred_element_type=F32, **kw)


def split(x):
    hi = x.astype(BF16)
    return hi, (x - hi.astype(F32)).astype(BF16)


def stack3(x):
    hi, lo = split(x)
    return jnp.concatenate([hi, lo, hi], axis=0)


def hot(index, rows):
    edges = index.shape[1]
    return lax.broadcasted_iota(jnp.int32, (rows, edges), 0) == index


def ones_at(index, rows):
    return jnp.where(hot(index, rows), 1.0, 0.0).astype(F32)


def small_stack(x):
    hi, lo = split(x)
    hi, lo = hi.astype(F32), lo.astype(F32)
    return jnp.concatenate([hi, lo, hi, jnp.zeros_like(x)], axis=0).astype(BF16)


def hidden_units(d2, env, denv, win):
    edges = d2.shape[1]
    centre = lax.broadcasted_iota(jnp.int32, (8, edges), 0).astype(F32) * (1.0 / 7.0)
    gap = d2 - centre
    basis = jnp.exp(-64.0 * gap * gap)
    slope = basis * (-128.0 * gap)
    pre = nn(win, small_stack(basis))
    dpre = nn(win, small_stack(slope))
    sig = 1.0 / (1.0 + jnp.exp(-pre))
    act = pre * sig
    dact = sig * (1.0 + pre * (1.0 - sig)) * dpre
    return act * env, dact * env + act * denv


def call(kernel, outs, *args, flops=1_000_000, limit=40):
    return pl.pallas_call(
        kernel,
        out_shape=tuple(jax.ShapeDtypeStruct(s, d) for s, d in outs),
        compiler_params=pltpu.CompilerParams(vmem_limit_bytes=limit * 1024 * 1024),
        cost_estimate=pl.CostEstimate(flops=flops, bytes_accessed=1_000_000, transcendentals=0),
    )(*args)


def weights_kernel(embed, rin, rout, wup, emb_o, t0_o, win_o, wout_o, woutb_o, wup_o):
    emb = embed[...].astype(BF16)
    emb_o[...] = emb
    table = nn(emb.astype(F32), wup[0], precision=HIGH)
    hi, lo = split(table.T)
    t0_o[...] = jnp.concatenate([hi, lo], axis=1)
    for t in range(2):
        hi, lo = split(rin[t])
        hi, lo = hi.astype(F32), lo.astype(F32)
        both = jnp.concatenate([hi, hi, lo, jnp.zeros_like(hi)], axis=0)
        win_o[t] = both.T.astype(BF16)
        hi, lo = split(rout[t])
        woutb_o[t] = hi
        hi, lo = hi.astype(F32), lo.astype(F32)
        both = jnp.concatenate([hi, hi, lo], axis=0)
        wout_o[t] = both.T.astype(BF16)
    hi, lo = split(wup[1].T)
    wup_o[...] = jnp.concatenate([hi, lo], axis=1)


def first_kernel(
    box, left, own, right, edges, emb, t0, win, wout, lam, wmix, read_one, read_out,
    h1_o, e1_o, seed1_o, seed2_o, geo_o, pool_o, at_o, lift_o, base_o, table,
):
    count = edges.shape[1]
    table[...] = jnp.zeros_like(table)
    table[0:9] = left[...]
    table[9:18] = own[...]
    table[18:27] = right[...]
    rows = table[...]
    hi = rows.astype(BF16).astype(F32)
    rest = rows - hi
    mid = rest.astype(BF16).astype(F32)
    low = rest - mid
    parts = [
        jnp.concatenate([p[:, 32 * c : 32 * c + 32] for p in (hi, mid, low)], axis=1)
        for c in range(4)
    ]
    lhs = jnp.concatenate(parts, axis=0).astype(BF16)
    mine = jnp.concatenate([p[13:14] for p in parts] + [jnp.zeros((4, 96), F32)], axis=0)
    sender = edges[0:1]
    receiver = edges[1:2]
    slot = ones_at(jnp.bitwise_and(sender, 31), 32).astype(BF16)
    block = ones_at(jnp.right_shift(sender, 5), 32)
    recv = ones_at(receiver, 32)
    recv_b = recv.astype(BF16)
    got = nn(lhs, jnp.concatenate([slot] * 3, axis=0))
    at_recv = nn(mine.astype(BF16), jnp.concatenate([recv_b] * 3, axis=0))
    sent = [jnp.sum(got[32 * c : 32 * c + 32] * block, axis=0, keepdims=True) for c in range(4)]
    rel = []
    for c in range(3):
        d = sent[c] - at_recv[c : c + 1]
        d = d - jnp.round(d * (1.0 / box[c])) * box[c]
        rel.append(d * (1.0 / cutoff_radius))
    x, y, z = rel
    d2 = x * x + y * y + z * z
    reach = jnp.maximum(1.0 - d2, 0.0)
    env = reach * reach
    denv = -2.0 * reach
    geo_o[...] = jnp.concatenate([x, y, z, d2, env, denv, d2, d2], axis=0)
    harmonics = [
        jnp.ones_like(x),
        S3 * x,
        S3 * y,
        S3 * z,
        S15 * x * y,
        S15 * y * z,
        S15 * x * z,
        0.5 * S15 * (x * x - y * y),
        0.5 * S5 * (2.0 * z * z - x * x - y * y),
    ]
    for m, value in enumerate(harmonics):
        pool_o[32 * m : 32 * m + 32] = (recv * (value * 0.125)).astype(BF16)
    hidden, _ = hidden_units(d2, env, denv, win[0])
    radial = nn(wout[0], stack3(hidden))
    kind = ones_at(sent[3].astype(jnp.int32), 128).astype(BF16)
    lift = nn(t0[...], jnp.concatenate([kind, kind], axis=0))
    lift_o[...] = lift.astype(BF16)
    sums = []
    for order, (a, b) in enumerate(((0, 32), (32, 128), (128, 288))):
        base = (radial[128 * order : 128 * order + 128] * lift).astype(BF16)
        base_o[128 * order : 128 * order + 128] = base
        sums.append(nt(pool_o[a:b], base))
    product = sums[0]
    for order in (1, 2):
        total = sums[order]
        weight = lam[0, order - 1 : order]
        square = sum(
            total[32 * m : 32 * m + 32] * total[32 * m : 32 * m + 32]
            for m in range(2 * order + 1)
        )
        product = product + weight * square
        first = 0 if order == 1 else 96
        at_o[first : first + 32 * (2 * order + 1)] = (2.0 * weight * total).astype(BF16)
    kinds = own[4:5, 96:128]
    mask = jnp.where(kinds >= 0.0, 1.0, 0.0)
    own_kind = jnp.where(
        lax.broadcasted_iota(jnp.int32, (128, 32), 0) == kinds.astype(jnp.int32), 1.0, 0.0
    ).astype(BF16)
    h0 = tn(own_kind, emb[...])
    h1 = h0 + nn(product, wmix[0], precision=HIGH)
    h1_o[...] = h1.astype(BF16)
    e1_o[...] = nt(read_one[...], h1, precision=HIGH) * mask
    pad = jnp.zeros((7, 32), F32)
    mask8 = jnp.concatenate([mask, pad], axis=0)
    zero = lax.broadcasted_iota(jnp.int32, (8, 128), 0) == 0
    seed1_o[...] = tn(mask8, jnp.where(zero, read_one[...], 0.0), precision=HIGH)
    zero = lax.broadcasted_iota(jnp.int32, (8, 16), 0) == 0
    seed2_o[...] = tn(mask8, jnp.where(zero, read_out[...], 0.0), precision=HIGH)


def radial_kernel(edges, geo, win, wout, hot_o, rad_o, slope_o):
    sender = edges[0:1]
    for r in range(0, 864, 96):
        row = lax.broadcasted_iota(jnp.int32, (96, sender.shape[1]), 0) + r
        hot_o[r : r + 96] = jnp.where(row == sender, 1.0, 0.0).astype(BF16)
    hidden, slope = hidden_units(geo[3:4], geo[4:5], geo[5:6], win[1])
    rad_o[...] = nn(wout[1], stack3(hidden))
    slope_o[...] = slope


def direction_kernel(edges, geo, pool, at, lift, base, win, wout, v_o):
    x, y, z = geo[0:1], geo[1:2], geo[2:3]
    recv = ones_at(edges[1:2], 32)
    _, slope = hidden_units(geo[3:4], geo[4:5], geo[5:6], win[0])
    drad = nn(wout[0], stack3(slope))
    g1 = tn(at[0:96], pool[32:128])
    g2 = tn(at[96:256], pool[128:288])
    common = drad[0:128] * 0.125 + drad[128:256] * g1 + drad[256:384] * g2
    common = lift[...].astype(F32) * common
    b1 = base[128:256].astype(F32)
    b2 = base[256:384].astype(F32)
    recv8 = recv * 0.125
    turns = (
        ((0, S15 * y), (2, S15 * z), (3, S15 * x), (4, -S5 * x)),
        ((0, S15 * x), (1, S15 * z), (3, -S15 * y), (4, -S5 * y)),
        ((1, S15 * y), (2, S15 * x), (4, 2.0 * S5 * z)),
    )
    for k, coordinate in enumerate((x, y, z)):
        h1 = tn(at[32 * k : 32 * k + 32], (recv8 * S3).astype(BF16))
        left = jnp.concatenate([at[96 + 32 * m : 128 + 32 * m] for m, _ in turns[k]], axis=0)
        right = jnp.concatenate([(recv8 * f).astype(BF16) for _, f in turns[k]], axis=0)
        h2 = tn(left, right)
        v = common * (2.0 * coordinate) + b1 * h1 + b2 * h2
        v_o[128 * k : 128 * k + 128] = v.astype(BF16)


def second_kernel(
    left, own, right, hotref, rad, pool, wup, lam, wmix, read_hidden, seed2,
    dleft_o, down_o, dright_o, dh2_o, e2_o, drad_o, base_o, da_o,
):
    feats = jnp.concatenate([left[...], own[...], right[...]], axis=0)
    got = tn(feats, hotref[...]).astype(BF16)
    lift = nn(wup[...], jnp.concatenate([got, got], axis=0))
    sums = []
    spans = ((0, 32), (32, 128), (128, 288))
    for order, (a, b) in enumerate(spans):
        base = (rad[128 * order : 128 * order + 128] * lift).astype(BF16)
        base_o[128 * order : 128 * order + 128] = base
        sums.append(nt(pool[a:b], base))
    product = sums[0]
    for order in (1, 2):
        total = sums[order]
        square = sum(
            total[32 * m : 32 * m + 32] * total[32 * m : 32 * m + 32]
            for m in range(2 * order + 1)
        )
        product = product + lam[1, order - 1 : order] * square
    h2 = own[128:160].astype(F32) + nn(product, wmix[1], precision=HIGH)
    pre = nn(h2, read_hidden[...], precision=HIGH)
    sig = 1.0 / (1.0 + jnp.exp(-pre))
    inner = pre * sig
    seed = seed2[...]
    e2_o[...] = nt(jnp.ones((8, 16), F32), inner * seed, precision=HIGH)
    dpre = seed * sig * (1.0 + pre * (1.0 - sig))
    dh2 = nt(dpre, read_hidden[...], precision=HIGH)
    dh2_o[...] = dh2
    dp = nt(dh2, wmix[1], precision=HIGH)
    da_o[0:32] = dp.astype(BF16)
    for order in (1, 2):
        weight = 2.0 * lam[1, order - 1 : order] * dp
        a = spans[order][0]
        for m in range(2 * order + 1):
            piece = weight * sums[order][32 * m : 32 * m + 32]
            da_o[a + 32 * m : a + 32 * m + 32] = piece.astype(BF16)
    dlift = None
    for order, (a, b) in enumerate(spans):
        g = tn(da_o[a:b], pool[a:b])
        drad_o[128 * order : 128 * order + 128] = (lift * g).astype(BF16)
        term = rad[128 * order : 128 * order + 128] * g
        dlift = term if dlift is None else dlift + term
    hi, lo = split(dlift)
    back = nt(hotref[...], jnp.concatenate([hi, lo], axis=0))
    back = back[:, 0:128] + back[:, 128:256]
    dleft_o[...] = back[0:288].astype(BF16)
    down_o[...] = back[288:576]
    dright_o[...] = back[576:864].astype(BF16)


def slope_kernel(edges, geo, slope, drad, base, da, woutb, drel_o):
    x, y, z = geo[0:1], geo[1:2], geo[2:3]
    recv8 = ones_at(edges[1:2], 32) * 0.125
    dhidden = nn(woutb[1], drad[...])
    dd2 = 2.0 * jnp.sum(dhidden * slope[...], axis=0, keepdims=True)
    q1 = nn(da[32:128], base[128:256])
    q2 = nn(da[128:288], base[256:384])
    one = [
        jnp.sum(q1[32 * m : 32 * m + 32] * recv8, axis=0, keepdims=True) * S3 for m in range(3)
    ]
    two = [jnp.sum(q2[32 * m : 32 * m + 32] * recv8, axis=0, keepdims=True) for m in range(5)]
    dx = dd2 * x + one[0] + S15 * (two[0] * y + two[2] * z + two[3] * x) - S5 * two[4] * x
    dy = dd2 * y + one[1] + S15 * (two[0] * x + two[1] * z - two[3] * y) - S5 * two[4] * y
    dz = dd2 * z + one[2] + S15 * (two[1] * y + two[2] * x) + 2.0 * S5 * two[4] * z
    none = jnp.zeros_like(dx)
    drel_o[...] = jnp.concatenate([dx, dy, dz, none, none, none, none, none], axis=0)


def force_kernel(edges, folded, dh2, seed1, e1, e2, wup, wmix, v, drel2, left_o, own_o, right_o, rows):
    dh1 = dh2[...] + seed1[...] + nt(folded[...], wup[1], precision=HIGH)
    dp = nt(dh1, wmix[0], precision=HIGH)
    hi, lo = split(dp)
    dp2 = jnp.concatenate([hi, lo], axis=0)
    sender = edges[0:1]
    recv = ones_at(edges[1:2], 32)
    slot = ones_at(jnp.bitwise_and(sender, 31), 32).astype(BF16)
    block = ones_at(jnp.right_shift(sender, 5), 32)
    spread, pulled = [], []
    for k in range(3):
        q = nn(dp2, v[128 * k : 128 * k + 128])
        q = q[0:32] + q[32:64]
        drel = jnp.sum(q * recv, axis=0, keepdims=True) + drel2[k : k + 1]
        force = drel * (-1.0 / cutoff_radius)
        hi, lo = split(force)
        hi, lo = hi.astype(F32), lo.astype(F32)
        spread += [block * hi, block * lo]
        pulled += [hi, lo]
    pushed = nt(jnp.concatenate(spread, axis=0).astype(BF16), slot)
    pulled = jnp.concatenate(pulled + [jnp.zeros_like(hi)] * 2, axis=0).astype(BF16)
    pulled = nt(pulled, recv.astype(BF16))
    rows[...] = jnp.zeros_like(rows)
    for k in range(3):
        rows[:, 32 * k : 32 * k + 32] = pushed[64 * k : 64 * k + 32] + pushed[64 * k + 32 : 64 * k + 64]
        rows[13:14, 32 * k : 32 * k + 32] = (
            rows[13:14, 32 * k : 32 * k + 32] - pulled[2 * k : 2 * k + 1] - pulled[2 * k + 1 : 2 * k + 2]
        )
    rows[13:14, 96:128] = e1[...] + e2[0:1]
    left_o[...] = rows[0:9]
    own_o[...] = rows[9:18]
    right_o[...] = rows[18:27]


def local(
    positions, species, atom_count, edge_count, sender, receiver, image_shift,
    embed, radial_in, radial_out, w_up, lam, w_mix, read_one, read_hidden, read_out,
):
    atoms = positions.shape[-1]
    count = sender.shape[-1]
    box = (SIDE * 4 * lattice_step, SIDE * 4 * lattice_step, SIDE * (atoms // 16) * lattice_step)

    owned = jnp.arange(atoms, dtype=jnp.int32) < atom_count[0, 0, 0]
    kinds = jnp.where(owned, species[0, 0, 0], -1).astype(F32)
    row = jnp.concatenate([positions.reshape(3 * atoms), kinds])[None]
    s, r = sender[0, 0, 0], receiver[0, 0, 0]
    block, slot = s // atoms, s % atoms
    block = (block % 3) * 9 + (block // 3 % 3) * 3 + block // 9
    live = jnp.arange(count, dtype=jnp.int32) < edge_count[0, 0, 0]
    edges = jnp.stack([jnp.where(live, block * atoms + slot, 1023), jnp.where(live, r, 99)])

    padded = jnp.pad(embed, ((0, 128 - embed.shape[0]), (0, 0)))
    emb, t0, win, wout, woutb, wup = call(
        weights_kernel,
        [((128, 128), BF16), ((128, 256), BF16), ((2, 64, 32), BF16), ((2, 384, 192), BF16),
         ((2, 64, 384), BF16), ((128, 256), BF16)],
        padded, radial_in, radial_out, w_up,
    )

    line = jnp.concatenate([move(row, bring_home(d)) for d in (-1, 0, 1)], axis=0)
    edges = move(edges, bring_home(0))
    plane = jnp.concatenate(widen(line, 1), axis=0)
    left, own, right = widen(plane, 2)

    h1, e1, seed1, seed2, geo, pool, at, lift, base = pl.pallas_call(
        functools.partial(first_kernel, box),
        out_shape=tuple(
            jax.ShapeDtypeStruct(s, d)
            for s, d in (
                ((32, 128), BF16), ((1, 32), F32), ((32, 128), F32), ((32, 16), F32), ((8, count), F32),
                ((288, count), BF16), ((256, 128), BF16), ((128, count), BF16), ((384, count), BF16),
            )
        ),
        scratch_shapes=[pltpu.VMEM((32, 128), F32)],
        compiler_params=pltpu.CompilerParams(vmem_limit_bytes=40 * 1024 * 1024),
        cost_estimate=pl.CostEstimate(flops=1_000_000, bytes_accessed=1_000_000, transcendentals=0),
    )(left, own, right, edges, emb, t0, win, wout, lam, w_mix, read_one[None], read_out[None])

    line = jnp.concatenate(widen(h1, 0), axis=0)
    plane = jnp.concatenate(widen(line, 1), axis=0)
    left, own, right = widen(plane, 2)

    hotref, rad, slope = call(
        radial_kernel,
        [((864, count), BF16), ((384, count), F32), ((64, count), F32)],
        edges, geo, win, wout, flops=1_000_000_000,
    )
    (v,) = call(
        direction_kernel, [((384, count), BF16)], edges, geo, pool, at, lift, base, win, wout,
        flops=1_000_000_000,
    )

    dleft, down, dright, dh2, e2, drad, base2, da = call(
        second_kernel,
        [((288, 128), BF16), ((288, 128), F32), ((288, 128), BF16), ((32, 128), F32), ((8, 32), F32),
         ((384, count), BF16), ((384, count), BF16), ((288, 128), BF16)],
        left, own, right, hotref, rad, pool, wup, lam, w_mix, read_hidden, seed2,
    )

    plane = down + move(dleft, shift(2, 1)).astype(F32) + move(dright, shift(2, -1)).astype(F32)
    line = (
        plane[96:192]
        + move(plane[0:96].astype(BF16), shift(1, 1)).astype(F32)
        + move(plane[192:288].astype(BF16), shift(1, -1)).astype(F32)
    )
    folded = (
        line[32:64]
        + move(line[0:32].astype(BF16), shift(0, 1)).astype(F32)
        + move(line[64:96].astype(BF16), shift(0, -1)).astype(F32)
    )

    (drel2,) = call(
        slope_kernel, [((8, count), F32)], edges, geo, slope, drad, base2, da, woutb,
        flops=1_000_000_000,
    )

    left, own, right = pl.pallas_call(
        force_kernel,
        out_shape=tuple(jax.ShapeDtypeStruct((9, 128), F32) for _ in range(3)),
        scratch_shapes=[pltpu.VMEM((32, 128), F32)],
        compiler_params=pltpu.CompilerParams(vmem_limit_bytes=40 * 1024 * 1024),
        cost_estimate=pl.CostEstimate(flops=1_000_000, bytes_accessed=1_000_000, transcendentals=0),
    )(edges, folded, dh2, seed1, e1, e2, w_up, w_mix, v, drel2)

    plane = own + move(left, shift(2, 1)) + move(right, shift(2, -1))
    line = plane[3:6] + move(plane[0:3], shift(1, 1)) + move(plane[6:9], shift(1, -1))
    row = sum(move(line[d + 1 : d + 2], send_back(d)) for d in (-1, 0, 1))
    forces = row[0, : 3 * atoms].reshape(3, 1, 1, 1, atoms)
    site_energy = row[0, 3 * atoms :].reshape(1, 1, 1, atoms)
    return (site_energy, forces)


def solution(mesh):
    cell = P("gx", "gy", "gz")
    in_specs = (
        P(None, "gx", "gy", "gz", None),
        P("gx", "gy", "gz", None),
        cell,
        cell,
        P("gx", "gy", "gz", None),
        P("gx", "gy", "gz", None),
        P(None, "gx", "gy", "gz", None),
    ) + (P(),) * 9
    out_specs = (P("gx", "gy", "gz", None), P(None, "gx", "gy", "gz", None))
    return jax.shard_map(local, mesh=mesh, in_specs=in_specs, out_specs=out_specs, check_vma=False)
```

time: 375 us -> 138 us (0.37)
  the two profiles are of different devices: /device:TPU:4 before, /device:TPU:1 now
where the time goes in v1:
time: 138 us; the launch traced here: 137 us
  starting transfers between devices  88.3 us (64%)
  waiting for transfers between devices  17.9 us (13%)
  local copies, waits for them, and re-layouts  13.2 us (10%)
  Pallas kernels  12.4 us (9%)
  other arithmetic  2.43 us (2%)
  between operations  2.42 us (2%)
    ppermute x27, starting transfers between devices, move(): return lax.ppermute(x, AXES, pairs)  88.3 us
    ppermute x27, waiting for transfers between devices, move(): return lax.ppermute(x, AXES, pairs)  17.9 us
    unnamed x43, local copies, waits for them, and re-layouts  10.4 us
    pallas_call x5, Pallas kernels, call(): pl.pallas_call(kernel, out_shape=tuple((jax.ShapeDtypeStruct(s, d) for s,...  8.77 us
  transfers between devices with their start and end apart: 27, of which 10 were waited for; matrix products, arithmetic and copies ran while one was open for 4% of the time, Pallas kernels for 3%

profile of v1, /device:TPU:1, one launch (start us, length us, event | category | flops | bytes accessed | tf_op | source)
XLA Modules:
  0.0 136.7 jit_solution(14288388857585288524)
XLA Ops:
  1.3 0.7 reduce
  2.8 8.8 %collective-permute-start.3 = (f32[1,128]{1,0:T(1,128)S(1)}, f32[1,128]{1,0:T(1,128)S(1)}, u32[]{:S(2)}, u32[]{:S(2)}) collective-permute-start(f32[1,128]{1,0:T(1,128)S(1)} %maximum_bitcast_fusion), channel_id=1, source_target_pairs={{64,0},{65,64},{66,2},{67,66},{68,4},{69,68},{70,6},{71,70},{72,8}... | collective-permute-start | bytes 1544 | tf_op jit(solution)/shard_map/ppermute | solution.py:36
  11.6 1.9 %collective-permute-start.2 = (f32[1,128]{1,0:T(1,128)S(1)}, f32[1,128]{1,0:T(1,128)S(1)}, u32[]{:S(2)}, u32[]{:S(2)}) collective-permute-start(f32[1,128]{1,0:T(1,128)S(1)} %maximum_bitcast_fusion), channel_id=1, source_target_pairs={{0,0},{1,64},{2,2},{3,66},{4,4},{5,68},{6,6},{7,70},{8,8},{9,72},{... | collective-permute-start | bytes 1544 | tf_op jit(solution)/shard_map/ppermute | solution.py:36
  13.5 8.4 %collective-permute-start.1 = (f32[1,128]{1,0:T(1,128)S(1)}, f32[1,128]{1,0:T(1,128)S(1)}, u32[]{:S(2)}, u32[]{:S(2)}) collective-permute-start(f32[1,128]{1,0:T(1,128)S(1)} %maximum_bitcast_fusion), channel_id=1, source_target_pairs={{448,0},{449,64},{450,2},{451,66},{452,4},{453,68},{454,6},{455,70... | collective-permute-start | bytes 1544 | tf_op jit(solution)/shard_map/ppermute | solution.py:36
  22.6 0.9 compare_select_fusion.3
  23.5 1.9 %collective-permute-start = (s32[2,1792]{1,0:T(2,128)S(1)}, s32[2,1792]{1,0:T(2,128)S(1)}, u32[]{:S(2)}, u32[]{:S(2)}) collective-permute-start(s32[2,1792]{1,0:T(2,128)S(1)} %pad_add_fusion), channel_id=1, source_target_pairs={{0,0},{1,64},{2,2},{3,66},{4,4},{5,68},{6,6},{7,70},{8,8},{9,72},{... | collective-permute-start | bytes 43016 | tf_op jit(solution)/shard_map/ppermute | solution.py:36
  25.5 5.1 %collective-permute-start.5 = (f32[3,128]{1,0:T(4,128)S(1)}, f32[3,128]{1,0:T(4,128)S(1)}, u32[]{:S(2)}, u32[]{:S(2)}) collective-permute-start(f32[3,128]{1,0:T(4,128)S(1)} %pad_maximum_fusion), channel_id=1, source_target_pairs={{8,0},{72,64},{10,2},{74,66},{12,4},{76,68},{14,6},{78,70},{16,8},... | collective-permute-start | bytes 4616 | tf_op jit(solution)/shard_map/ppermute | solution.py:36
  30.6 1.9 %collective-permute-start.4 = (f32[3,128]{1,0:T(4,128)S(1)}, f32[3,128]{1,0:T(4,128)S(1)}, u32[]{:S(2)}, u32[]{:S(2)}) collective-permute-start(f32[3,128]{1,0:T(4,128)S(1)} %pad_maximum_fusion), channel_id=1, source_target_pairs={{56,0},{120,64},{58,2},{122,66},{60,4},{124,68},{62,6},{126,70},{0... | collective-permute-start | bytes 4616 | tf_op jit(solution)/shard_map/ppermute | solution.py:36
  32.5 3.6 %collective-permute-done.4 = f32[3,128]{1,0:T(4,128)S(1)} collective-permute-done((f32[3,128]{1,0:T(4,128)S(1)}, f32[3,128]{1,0:T(4,128)S(1)}, u32[]{:S(2)}, u32[]{:S(2)}) %collective-permute-start.4) | collective-permute-done | bytes 1568 | tf_op jit(solution)/shard_map/ppermute | solution.py:36
  36.3 1.7 %collective-permute-start.6 = (f32[9,128]{1,0:T(8,128)S(1)}, f32[9,128]{1,0:T(8,128)S(1)}, u32[]{:S(2)}, u32[]{:S(2)}) collective-permute-start(f32[9,128]{1,0:T(8,128)S(1)} %concatenate.19.own), channel_id=1, source_target_pairs={{70,0},{0,64},{64,2},{2,66},{66,4},{4,68},{68,6},{6,70},{78,8},{8,... | collective-permute-start | bytes 13832 | tf_op jit(solution)/shard_map/ppermute | solution.py:36
  38.0 0.8 pad.4.embed
  38.8 0.9 copy-done.2
  39.7 0.9 copy-done.4
  40.6 0.7 copy-done.10
  41.7 0.9 copy-done
  44.6 2.3 %shard_map.159 = (bf16[32,128]{1,0:T(8,128)(2,1)S(1)}, f32[1,32]{1,0:T(1,128)S(1)}, f32[32,128]{1,0:T(8,128)S(1)}, f32[32,16]{1,0:T(8,128)S(1)}, f32[8,1792]{1,0...) custom-call(f32[9,128]{1,0:T(8,128)S(1)} %collective-permute-done.6., ...), custom_call_target="tpu_custom_call" | custom-call | flops 1000000 | bytes 1000000 | tf_op jit(solution)/shard_map/pallas_call | solution.py:401
  47.6 5.4 %collective-permute-start.8 = (bf16[32,128]{1,0:T(8,128)(2,1)S(1)}, bf16[32,128]{1,0:T(8,128)(2,1)S(1)}, u32[]{:S(2)}, u32[]{:S(2)}) collective-permute-start(bf16[32,128]{1,0:T(8,128)(2,1)S(1)} %get-tuple-element.35), channel_id=1, source_target_pairs={{385,0},{449,64},{387,2},{451,66},{389,4},{453,68},{391,6},{455,70... | collective-permute-start | bytes 24584 | tf_op jit(solution)/shard_map/ppermute | solution.py:36
  53.0 1.9 %collective-permute-start.9 = (bf16[32,128]{1,0:T(8,128)(2,1)S(1)}, bf16[32,128]{1,0:T(8,128)(2,1)S(1)}, u32[]{:S(2)}, u32[]{:S(2)}) collective-permute-start(bf16[32,128]{1,0:T(8,128)(2,1)S(1)} %get-tuple-element.35), channel_id=1, source_target_pairs={{128,0},{192,64},{130,2},{194,66},{132,4},{196,68},{134,6},{198,70... | collective-permute-start | bytes 24584 | tf_op jit(solution)/shard_map/ppermute | solution.py:36
  56.1 1.2 collective-permute-done.9
  58.0 1.9 %collective-permute-start.10 = (bf16[96,128]{1,0:T(8,128)(2,1)}, bf16[96,128]{1,0:T(8,128)(2,1)}, u32[]{:S(2)}, u32[]{:S(2)}) collective-permute-start(bf16[96,128]{1,0:T(8,128)(2,1)} %constant_dynamic-update-slice_fusion), channel_id=1, source_target_pairs={{56,0},{120,64},{58,2},{122,66},{60,4},{124,68},{62,6},{126,70},{0... | collective-permute-start | bytes 73736 | tf_op jit(solution)/shard_map/ppermute | solution.py:36
  59.9 0.8 copy.19.read_hidden
  60.7 4.6 %collective-permute-start.11 = (bf16[96,128]{1,0:T(8,128)(2,1)}, bf16[96,128]{1,0:T(8,128)(2,1)S(1)}, u32[]{:S(2)}, u32[]{:S(2)}) collective-permute-start(bf16[96,128]{1,0:T(8,128)(2,1)} %constant_dynamic-update-slice_fusion), channel_id=1, source_target_pairs={{8,0},{72,64},{10,2},{74,66},{12,4},{76,68},{14,6},{78,70},{16,8},... | collective-permute-start | bytes 73736 | tf_op jit(solution)/shard_map/ppermute | solution.py:36
  65.3 0.7 constant_dynamic-update-slice_fusion.7
  66.0 0.7 constant_dynamic-update-slice_fusion.6
  66.7 2.5 %collective-permute-start.13 = (bf16[288,128]{1,0:T(8,128)(2,1)S(1)}, bf16[288,128]{1,0:T(8,128)(2,1)S(1)}, u32[]{:S(2)}, u32[]{:S(2)}) collective-permute-start(bf16[288,128]{1,0:T(8,128)(2,1)S(1)} %constant_dynamic-update-slice_fusion.3.own), channel_id=1, source_target_pairs={{64,0},{2,64},{66,2},{4,66},{68,4},{6,68},{70,6},{0,70},{72,8},{10... | collective-permute-start | bytes 221192 | tf_op jit(solution)/shard_map/ppermute | solution.py:36
  69.5 0.8 copy-done.6
  70.3 1.5 %shard_map.160 = (bf16[864,1792]{1,0:T(8,128)(2,1)S(1)}, f32[384,1792]{1,0:T(8,128)S(1)}, f32[64,1792]{1,0:T(8,128)S(1)}) custom-call(s32[2,1792]{1,0:T(2,128)S(1)} %collective-permute-done.edges, f32[8,1792]{1,0:T(8,128)S(1)} %copy-done.6, bf16[2,64,32]{2,1,0:T(8,128)(2,1)S(1)} %get-tuple-element.33.win, bf16[2,384,192]{2,1,0:T(8,128)(2,1)S(1)} %get-tuple-element.34.wout), custom_call_target="tpu_custom_call" | custom-call | flops 1000000000 | bytes 1000000 | tf_op jit(solution)/shard_map/pallas_call | solution.py:112
  71.8 4.1 %shard_map.161 = (bf16[288,128]{1,0:T(8,128)(2,1)S(1)}, f32[288,128]{1,0:T(8,128)S(1)}, bf16[288,128]{1,0:T(8,128)(2,1)S(1)}, f32[32,128]{1,0:T(8,128)S(1)}, f32...) custom-call(bf16[288,128]{1,0:T(8,128)(2,1)S(1)} %collective-permute, ...), custom_call_target="tpu_custom_call" | custom-call | flops 1000000 | bytes 1000000 | tf_op jit(solution)/shard_map/pallas_call | solution.py:112
  76.0 3.2 %collective-permute-start.14 = (bf16[288,128]{1,0:T(8,128)(2,1)S(1)}, bf16[288,128]{1,0:T(8,128)(2,1)S(1)}, u32[]{:S(2)}, u32[]{:S(2)}) collective-permute-start(bf16[288,128]{1,0:T(8,128)(2,1)S(1)} %get-tuple-element.43), channel_id=1, source_target_pairs={{64,0},{2,64},{66,2},{4,66},{68,4},{6,68},{70,6},{0,70},{72,8},{10... | collective-permute-start | bytes 221192 | tf_op jit(solution)/shard_map/ppermute | solution.py:36
  79.2 0.9 collective-permute-done.14
  80.7 4.5 %collective-permute-start.16 = (bf16[96,128]{1,0:T(8,128)(2,1)S(1)}, bf16[96,128]{1,0:T(8,128)(2,1)S(1)}, u32[]{:S(2)}, u32[]{:S(2)}) collective-permute-start(bf16[96,128]{1,0:T(8,128)(2,1)S(1)} %get-tuple-element.68), channel_id=1, source_target_pairs={{8,0},{72,64},{10,2},{74,66},{12,4},{76,68},{14,6},{78,70},{16,8},... | collective-permute-start | bytes 73736 | tf_op jit(solution)/shard_map/ppermute | solution.py:36
  85.2 1.9 %collective-permute-start.17 = (bf16[96,128]{1,0:T(8,128)(2,1)S(1)}, bf16[96,128]{1,0:T(8,128)(2,1)S(1)}, u32[]{:S(2)}, u32[]{:S(2)}) collective-permute-start(bf16[96,128]{1,0:T(8,128)(2,1)S(1)} %get-tuple-element.69), channel_id=1, source_target_pairs={{56,0},{120,64},{58,2},{122,66},{60,4},{124,68},{62,6},{126,70},{0... | collective-permute-start | bytes 73736 | tf_op jit(solution)/shard_map/ppermute | solution.py:36
  87.2 2.1 %shard_map.162.v = bf16[384,1792]{1,0:T(8,128)(2,1)S(1)} custom-call(s32[2,1792]{1,0:T(2,128)S(1)} %collective-permute-done.edges, f32[8,1792]{1,0:T(8,128)S(1)} %copy-done.6, bf16[288,1792]{1,0:T(8,128)(2,1)S(1)} %get-tuple-element.39.pool, bf16[256,128]{1,0:T(8,128)(2,1)S(1)} %get-tuple-element.49.at, bf16[128,1792]{1,0:T(8,128)(2,1)S(1)} %get-tuple-element.50.lift, ...), custom_call_target="tpu_custom_call" | custom-call | flops 1000000000 | bytes 1000000 | tf_op jit(solution)/shard_map/pallas_call | solution.py:112
  89.2 1.8 %collective-permute-done.17 = bf16[96,128]{1,0:T(8,128)(2,1)S(1)} collective-permute-done((bf16[96,128]{1,0:T(8,128)(2,1)S(1)}, bf16[96,128]{1,0:T(8,128)(2,1)S(1)}, u32[]{:S(2)}, u32[]{:S(2)}) %collective-permute-start.17) | collective-permute-done | bytes 24608 | tf_op jit(solution)/shard_map/ppermute | solution.py:36
  91.0 3.5 %collective-permute-start.18 = (bf16[32,128]{1,0:T(8,128)(2,1)S(1)}, bf16[32,128]{1,0:T(8,128)(2,1)S(1)}, u32[]{:S(2)}, u32[]{:S(2)}) collective-permute-start(bf16[32,128]{1,0:T(8,128)(2,1)S(1)} %get-tuple-element.70), channel_id=1, source_target_pairs={{128,0},{192,64},{130,2},{194,66},{132,4},{196,68},{134,6},{198,70... | collective-permute-start | bytes 24584 | tf_op jit(solution)/shard_map/ppermute | solution.py:36
  94.5 1.9 %collective-permute-start.19 = (bf16[32,128]{1,0:T(8,128)(2,1)S(1)}, bf16[32,128]{1,0:T(8,128)(2,1)S(1)}, u32[]{:S(2)}, u32[]{:S(2)}) collective-permute-start(bf16[32,128]{1,0:T(8,128)(2,1)S(1)} %get-tuple-element.71), channel_id=1, source_target_pairs={{385,0},{449,64},{387,2},{451,66},{389,4},{453,68},{391,6},{455,70... | collective-permute-start | bytes 24584 | tf_op jit(solution)/shard_map/ppermute | solution.py:36
  96.5 0.7 shard_map.163.drel2
  97.3 2.9 %collective-permute-done.19 = bf16[32,128]{1,0:T(8,128)(2,1)S(1)} collective-permute-done((bf16[32,128]{1,0:T(8,128)(2,1)S(1)}, bf16[32,128]{1,0:T(8,128)(2,1)S(1)}, u32[]{:S(2)}, u32[]{:S(2)}) %collective-permute-start.19) | collective-permute-done | bytes 8224 | tf_op jit(solution)/shard_map/ppermute | solution.py:36
  100.2 1.4 shard_map.164
  101.5 6.8 %collective-permute-start.20 = (f32[9,128]{1,0:T(8,128)S(1)}, f32[9,128]{1,0:T(8,128)S(1)}, u32[]{:S(2)}, u32[]{:S(2)}) collective-permute-start(f32[9,128]{1,0:T(8,128)S(1)} %get-tuple-element.58), channel_id=1, source_target_pairs={{64,0},{2,64},{66,2},{4,66},{68,4},{6,68},{70,6},{0,70},{72,8},{10... | collective-permute-start | bytes 13832 | tf_op jit(solution)/shard_map/ppermute | solution.py:36
  108.3 0.8 collective-permute-done.20
  109.5 2.0 %collective-permute-start.22 = (f32[3,128]{1,0:T(4,128)S(1)}, f32[3,128]{1,0:T(4,128)S(1)}, u32[]{:S(2)}, u32[]{:S(2)}) collective-permute-start(f32[3,128]{1,0:T(4,128)S(1)} %get-tuple-element.72), channel_id=1, source_target_pairs={{8,0},{72,64},{10,2},{74,66},{12,4},{76,68},{14,6},{78,70},{16,8},... | collective-permute-start | bytes 4616 | tf_op jit(solution)/shard_map/ppermute | solution.py:36
  111.5 3.3 %collective-permute-start.23 = (f32[3,128]{1,0:T(4,128)S(1)}, f32[3,128]{1,0:T(4,128)S(1)}, u32[]{:S(2)}, u32[]{:S(2)}) collective-permute-start(f32[3,128]{1,0:T(4,128)S(1)} %get-tuple-element.73), channel_id=1, source_target_pairs={{56,0},{120,64},{58,2},{122,66},{60,4},{124,68},{62,6},{126,70},{0... | collective-permute-start | bytes 4616 | tf_op jit(solution)/shard_map/ppermute | solution.py:36
  114.8 2.2 %collective-permute-done.23 = f32[3,128]{1,0:T(4,128)S(1)} collective-permute-done((f32[3,128]{1,0:T(4,128)S(1)}, f32[3,128]{1,0:T(4,128)S(1)}, u32[]{:S(2)}, u32[]{:S(2)}) %collective-permute-start.23) | collective-permute-done | bytes 1568 | tf_op jit(solution)/shard_map/ppermute | solution.py:36
  117.0 10.7 %collective-permute-start.25 = (f32[1,128]{1,0:T(1,128)S(1)}, f32[1,128]{1,0:T(1,128)S(1)}, u32[]{:S(2)}, u32[]{:S(2)}) collective-permute-start(f32[1,128]{1,0:T(1,128)S(1)} %get-tuple-element.74), channel_id=1, source_target_pairs={{0,0},{64,1},{2,2},{66,3},{4,4},{68,5},{6,6},{70,7},{8,8},{72,9},{... | collective-permute-start | bytes 1544 | tf_op jit(solution)/shard_map/ppermute | solution.py:36
  127.7 1.9 %collective-permute-start.26 = (f32[1,128]{1,0:T(1,128)S(1)}, f32[1,128]{1,0:T(1,128)S(1)}, u32[]{:S(2)}, u32[]{:S(2)}) collective-permute-start(f32[1,128]{1,0:T(1,128)S(1)} %get-tuple-element.75), channel_id=1, source_target_pairs={{0,64},{64,65},{2,66},{66,67},{4,68},{68,69},{6,70},{70,71},{8,72}... | collective-permute-start | bytes 1544 | tf_op jit(solution)/shard_map/ppermute | solution.py:36
  129.7 2.2 %collective-permute-start.24 = (f32[1,128]{1,0:T(1,128)S(1)}, f32[1,128]{1,0:T(1,128)S(1)}, u32[]{:S(2)}, u32[]{:S(2)}) collective-permute-start(f32[1,128]{1,0:T(1,128)S(1)} %get-tuple-element.76), channel_id=1, source_target_pairs={{0,448},{64,449},{2,450},{66,451},{4,452},{68,453},{6,454},{70,455... | collective-permute-start | bytes 1544 | tf_op jit(solution)/shard_map/ppermute | solution.py:36
  131.9 3.5 %collective-permute-done.24 = f32[1,128]{1,0:T(1,128)S(1)} collective-permute-done((f32[1,128]{1,0:T(1,128)S(1)}, f32[1,128]{1,0:T(1,128)S(1)}, u32[]{:S(2)}, u32[]{:S(2)}) %collective-permute-start.24) | collective-permute-done | bytes 544 | tf_op jit(solution)/shard_map/ppermute | solution.py:36
  (80 shorter events, 8.2 us)
Async XLA Ops:
  2.8 22.7 %collective-permute-start.3 = (f32[1,128]{1,0:T(1,128)S(1)}, f32[1,128]{1,0:T(1,128)S(1)}, u32[]{:S(2)}, u32[]{:S(2)}) collective-permute-start(f32[1,128]{1,0:T(1,128)S(1)} %maximum_bitcast_fusion), channel_id=1, source_target_pairs={{64,0},{65,64},{66,2},{67,66},{68,4},{69,68},{70,6},{71,70},{72,8}... | collective-permute-start | bytes 1544 | tf_op jit(solution)/shard_map/ppermute | solution.py:36
  11.6 13.9 %collective-permute-start.2 = (f32[1,128]{1,0:T(1,128)S(1)}, f32[1,128]{1,0:T(1,128)S(1)}, u32[]{:S(2)}, u32[]{:S(2)}) collective-permute-start(f32[1,128]{1,0:T(1,128)S(1)} %maximum_bitcast_fusion), channel_id=1, source_target_pairs={{0,0},{1,64},{2,2},{3,66},{4,4},{5,68},{6,6},{7,70},{8,8},{9,72},{... | collective-permute-start | bytes 1544 | tf_op jit(solution)/shard_map/ppermute | solution.py:36
  13.5 12.0 %collective-permute-start.1 = (f32[1,128]{1,0:T(1,128)S(1)}, f32[1,128]{1,0:T(1,128)S(1)}, u32[]{:S(2)}, u32[]{:S(2)}) collective-permute-start(f32[1,128]{1,0:T(1,128)S(1)} %maximum_bitcast_fusion), channel_id=1, source_target_pairs={{448,0},{449,64},{450,2},{451,66},{452,4},{453,68},{454,6},{455,70... | collective-permute-start | bytes 1544 | tf_op jit(solution)/shard_map/ppermute | solution.py:36
  23.5 18.2 %collective-permute-start = (s32[2,1792]{1,0:T(2,128)S(1)}, s32[2,1792]{1,0:T(2,128)S(1)}, u32[]{:S(2)}, u32[]{:S(2)}) collective-permute-start(s32[2,1792]{1,0:T(2,128)S(1)} %pad_add_fusion), channel_id=1, source_target_pairs={{0,0},{1,64},{2,2},{3,66},{4,4},{5,68},{6,6},{7,70},{8,8},{9,72},{... | collective-permute-start | bytes 43016 | tf_op jit(solution)/shard_map/ppermute | solution.py:36
  25.5 7.0 %collective-permute-start.5 = (f32[3,128]{1,0:T(4,128)S(1)}, f32[3,128]{1,0:T(4,128)S(1)}, u32[]{:S(2)}, u32[]{:S(2)}) collective-permute-start(f32[3,128]{1,0:T(4,128)S(1)} %pad_maximum_fusion), channel_id=1, source_target_pairs={{8,0},{72,64},{10,2},{74,66},{12,4},{76,68},{14,6},{78,70},{16,8},... | collective-permute-start | bytes 4616 | tf_op jit(solution)/shard_map/ppermute | solution.py:36
  30.6 5.5 %collective-permute-start.4 = (f32[3,128]{1,0:T(4,128)S(1)}, f32[3,128]{1,0:T(4,128)S(1)}, u32[]{:S(2)}, u32[]{:S(2)}) collective-permute-start(f32[3,128]{1,0:T(4,128)S(1)} %pad_maximum_fusion), channel_id=1, source_target_pairs={{56,0},{120,64},{58,2},{122,66},{60,4},{124,68},{62,6},{126,70},{0... | collective-permute-start | bytes 4616 | tf_op jit(solution)/shard_map/ppermute | solution.py:36
  36.3 5.4 %collective-permute-start.7 = (f32[9,128]{1,0:T(8,128)S(1)}, f32[9,128]{1,0:T(8,128)S(1)}, u32[]{:S(2)}, u32[]{:S(2)}) collective-permute-start(f32[9,128]{1,0:T(8,128)S(1)} %concatenate.19.own), channel_id=1, source_target_pairs={{64,0},{2,64},{66,2},{4,66},{68,4},{6,68},{70,6},{0,70},{72,8},{10... | collective-permute-start | bytes 13832 | tf_op jit(solution)/shard_map/ppermute | solution.py:36
  36.3 5.4 %collective-permute-start.6 = (f32[9,128]{1,0:T(8,128)S(1)}, f32[9,128]{1,0:T(8,128)S(1)}, u32[]{:S(2)}, u32[]{:S(2)}) collective-permute-start(f32[9,128]{1,0:T(8,128)S(1)} %concatenate.19.own), channel_id=1, source_target_pairs={{70,0},{0,64},{64,2},{2,66},{66,4},{4,68},{68,6},{6,70},{78,8},{8,... | collective-permute-start | bytes 13832 | tf_op jit(solution)/shard_map/ppermute | solution.py:36
  38.8 0.9 copy-start.2
  39.7 0.9 copy-start.4
  40.6 0.7 copy-start.10
  41.7 16.3 %copy-start.15 = (bf16[2,64,384]{2,1,0:T(8,128)(2,1)}, bf16[2,64,384]{2,1,0:T(8,128)(2,1)S(1)}, u32[]{:S(2)}) copy-start(bf16[2,64,384]{2,1,0:T(8,128)(2,1)S(1)} %get-tuple-element.56.woutb) | copy-start | bytes 294916
  41.7 0.9 copy-start
  42.6 0.7 copy-start.8
  43.3 0.7 copy-start.13
  44.0 0.7 copy-start.14
  46.9 0.6 copy-start.5
  47.6 10.4 %copy-start.11 = (f32[1,32]{1,0:T(1,128)}, f32[1,32]{1,0:T(1,128)S(1)}, u32[]{:S(2)}) copy-start(f32[1,32]{1,0:T(1,128)S(1)} %get-tuple-element.47.e1) | copy-start | bytes 388
  47.6 7.3 %collective-permute-start.8 = (bf16[32,128]{1,0:T(8,128)(2,1)S(1)}, bf16[32,128]{1,0:T(8,128)(2,1)S(1)}, u32[]{:S(2)}, u32[]{:S(2)}) collective-permute-start(bf16[32,128]{1,0:T(8,128)(2,1)S(1)} %get-tuple-element.35), channel_id=1, source_target_pairs={{385,0},{449,64},{387,2},{451,66},{389,4},{453,68},{391,6},{455,70... | collective-permute-start | bytes 24584 | tf_op jit(solution)/shard_map/ppermute | solution.py:36
  53.0 4.4 %collective-permute-start.9 = (bf16[32,128]{1,0:T(8,128)(2,1)S(1)}, bf16[32,128]{1,0:T(8,128)(2,1)S(1)}, u32[]{:S(2)}, u32[]{:S(2)}) collective-permute-start(bf16[32,128]{1,0:T(8,128)(2,1)S(1)} %get-tuple-element.35), channel_id=1, source_target_pairs={{128,0},{192,64},{130,2},{194,66},{132,4},{196,68},{134,6},{198,70... | collective-permute-start | bytes 24584 | tf_op jit(solution)/shard_map/ppermute | solution.py:36
  54.9 3.1 %copy-start.17 = (bf16[32,128]{1,0:T(8,128)(2,1)}, bf16[32,128]{1,0:T(8,128)(2,1)S(1)}, u32[]{:S(2)}) copy-start(bf16[32,128]{1,0:T(8,128)(2,1)S(1)} %collective-permute-done.8) | copy-start | bytes 24580
  58.0 7.3 %collective-permute-start.10 = (bf16[96,128]{1,0:T(8,128)(2,1)}, bf16[96,128]{1,0:T(8,128)(2,1)}, u32[]{:S(2)}, u32[]{:S(2)}) collective-permute-start(bf16[96,128]{1,0:T(8,128)(2,1)} %constant_dynamic-update-slice_fusion), channel_id=1, source_target_pairs={{56,0},{120,64},{58,2},{122,66},{60,4},{124,68},{62,6},{126,70},{0... | collective-permute-start | bytes 73736 | tf_op jit(solution)/shard_map/ppermute | solution.py:36
  60.7 6.0 %collective-permute-start.11 = (bf16[96,128]{1,0:T(8,128)(2,1)}, bf16[96,128]{1,0:T(8,128)(2,1)S(1)}, u32[]{:S(2)}, u32[]{:S(2)}) collective-permute-start(bf16[96,128]{1,0:T(8,128)(2,1)} %constant_dynamic-update-slice_fusion), channel_id=1, source_target_pairs={{8,0},{72,64},{10,2},{74,66},{12,4},{76,68},{14,6},{78,70},{16,8},... | collective-permute-start | bytes 73736 | tf_op jit(solution)/shard_map/ppermute | solution.py:36
  66.7 5.1 %collective-permute-start.13 = (bf16[288,128]{1,0:T(8,128)(2,1)S(1)}, bf16[288,128]{1,0:T(8,128)(2,1)S(1)}, u32[]{:S(2)}, u32[]{:S(2)}) collective-permute-start(bf16[288,128]{1,0:T(8,128)(2,1)S(1)} %constant_dynamic-update-slice_fusion.3.own), channel_id=1, source_target_pairs={{64,0},{2,64},{66,2},{4,66},{68,4},{6,68},{70,6},{0,70},{72,8},{10... | collective-permute-start | bytes 221192 | tf_op jit(solution)/shard_map/ppermute | solution.py:36
  69.3 2.5 %collective-permute-start.12 = (bf16[288,128]{1,0:T(8,128)(2,1)S(1)}, bf16[288,128]{1,0:T(8,128)(2,1)S(1)}, u32[]{:S(2)}, u32[]{:S(2)}) collective-permute-start(bf16[288,128]{1,0:T(8,128)(2,1)S(1)} %constant_dynamic-update-slice_fusion.3.own), channel_id=1, source_target_pairs={{70,0},{0,64},{64,2},{2,66},{66,4},{4,68},{68,6},{6,70},{78,8},{8,... | collective-permute-start | bytes 221192 | tf_op jit(solution)/shard_map/ppermute | solution.py:36
  69.5 0.8 copy-start.6
  70.3 1.6 %copy-start.1 = (f32[2,128,128]{2,1,0:T(8,128)S(1)}, f32[2,128,128]{2,1,0:T(8,128)}, u32[]{:S(2)}) copy-start(f32[2,128,128]{2,1,0:T(8,128)} %wmix.5) | copy-start | bytes 393220
  70.3 1.6 %copy-start.9 = (f32[2,2,128]{2,1,0:T(2,128)S(1)}, f32[2,2,128]{2,1,0:T(2,128)}, u32[]{:S(2)}) copy-start(f32[2,2,128]{2,1,0:T(2,128)} %lam.3) | copy-start | bytes 6148
  76.0 4.2 %collective-permute-start.14 = (bf16[288,128]{1,0:T(8,128)(2,1)S(1)}, bf16[288,128]{1,0:T(8,128)(2,1)S(1)}, u32[]{:S(2)}, u32[]{:S(2)}) collective-permute-start(bf16[288,128]{1,0:T(8,128)(2,1)S(1)} %get-tuple-element.43), channel_id=1, source_target_pairs={{64,0},{2,64},{66,2},{4,66},{68,4},{6,68},{70,6},{0,70},{72,8},{10... | collective-permute-start | bytes 221192 | tf_op jit(solution)/shard_map/ppermute | solution.py:36
  79.2 1.4 %collective-permute-start.15 = (bf16[288,128]{1,0:T(8,128)(2,1)S(1)}, bf16[288,128]{1,0:T(8,128)(2,1)S(1)}, u32[]{:S(2)}, u32[]{:S(2)}) collective-permute-start(bf16[288,128]{1,0:T(8,128)(2,1)S(1)} %get-tuple-element.44), channel_id=1, source_target_pairs={{70,0},{0,64},{64,2},{2,66},{66,4},{4,68},{68,6},{6,70},{78,8},{8,... | collective-permute-start | bytes 221192 | tf_op jit(solution)/shard_map/ppermute | solution.py:36
  80.7 8.5 %collective-permute-start.16 = (bf16[96,128]{1,0:T(8,128)(2,1)S(1)}, bf16[96,128]{1,0:T(8,128)(2,1)S(1)}, u32[]{:S(2)}, u32[]{:S(2)}) collective-permute-start(bf16[96,128]{1,0:T(8,128)(2,1)S(1)} %get-tuple-element.68), channel_id=1, source_target_pairs={{8,0},{72,64},{10,2},{74,66},{12,4},{76,68},{14,6},{78,70},{16,8},... | collective-permute-start | bytes 73736 | tf_op jit(solution)/shard_map/ppermute | solution.py:36
  85.2 5.8 %collective-permute-start.17 = (bf16[96,128]{1,0:T(8,128)(2,1)S(1)}, bf16[96,128]{1,0:T(8,128)(2,1)S(1)}, u32[]{:S(2)}, u32[]{:S(2)}) collective-permute-start(bf16[96,128]{1,0:T(8,128)(2,1)S(1)} %get-tuple-element.69), channel_id=1, source_target_pairs={{56,0},{120,64},{58,2},{122,66},{60,4},{124,68},{62,6},{126,70},{0... | collective-permute-start | bytes 73736 | tf_op jit(solution)/shard_map/ppermute | solution.py:36
  87.1 9.3 %copy-start.7 = (f32[8,1792]{1,0:T(8,128)S(1)}, f32[8,1792]{1,0:T(8,128)}, u32[]{:S(2)}) copy-start(f32[8,1792]{1,0:T(8,128)} %copy-done.5) | copy-start | bytes 172036
  87.1 9.3 %copy-start.16 = (bf16[2,64,384]{2,1,0:T(8,128)(2,1)S(1)}, bf16[2,64,384]{2,1,0:T(8,128)(2,1)}, u32[]{:S(2)}) copy-start(bf16[2,64,384]{2,1,0:T(8,128)(2,1)} %copy-done.15) | copy-start | bytes 294916
  91.0 6.2 %collective-permute-start.18 = (bf16[32,128]{1,0:T(8,128)(2,1)S(1)}, bf16[32,128]{1,0:T(8,128)(2,1)S(1)}, u32[]{:S(2)}, u32[]{:S(2)}) collective-permute-start(bf16[32,128]{1,0:T(8,128)(2,1)S(1)} %get-tuple-element.70), channel_id=1, source_target_pairs={{128,0},{192,64},{130,2},{194,66},{132,4},{196,68},{134,6},{198,70... | collective-permute-start | bytes 24584 | tf_op jit(solution)/shard_map/ppermute | solution.py:36
  94.5 5.6 %collective-permute-start.19 = (bf16[32,128]{1,0:T(8,128)(2,1)S(1)}, bf16[32,128]{1,0:T(8,128)(2,1)S(1)}, u32[]{:S(2)}, u32[]{:S(2)}) collective-permute-start(bf16[32,128]{1,0:T(8,128)(2,1)S(1)} %get-tuple-element.71), channel_id=1, source_target_pairs={{385,0},{449,64},{387,2},{451,66},{389,4},{453,68},{391,6},{455,70... | collective-permute-start | bytes 24584 | tf_op jit(solution)/shard_map/ppermute | solution.py:36
  96.5 3.7 %copy-start.3 = (f32[2,128,128]{2,1,0:T(8,128)S(1)}, f32[2,128,128]{2,1,0:T(8,128)}, u32[]{:S(2)}) copy-start(f32[2,128,128]{2,1,0:T(8,128)} %wup.3) | copy-start | bytes 393220
  96.5 3.7 %copy-start.12 = (f32[1,32]{1,0:T(1,128)S(1)}, f32[1,32]{1,0:T(1,128)}, u32[]{:S(2)}) copy-start(f32[1,32]{1,0:T(1,128)} %copy-done.11) | copy-start | bytes 388
  101.5 7.6 %collective-permute-start.20 = (f32[9,128]{1,0:T(8,128)S(1)}, f32[9,128]{1,0:T(8,128)S(1)}, u32[]{:S(2)}, u32[]{:S(2)}) collective-permute-start(f32[9,128]{1,0:T(8,128)S(1)} %get-tuple-element.58), channel_id=1, source_target_pairs={{64,0},{2,64},{66,2},{4,66},{68,4},{6,68},{70,6},{0,70},{72,8},{10... | collective-permute-start | bytes 13832 | tf_op jit(solution)/shard_map/ppermute | solution.py:36
  108.3 1.2 collective-permute-start.21
  109.5 5.3 %collective-permute-start.22 = (f32[3,128]{1,0:T(4,128)S(1)}, f32[3,128]{1,0:T(4,128)S(1)}, u32[]{:S(2)}, u32[]{:S(2)}) collective-permute-start(f32[3,128]{1,0:T(4,128)S(1)} %get-tuple-element.72), channel_id=1, source_target_pairs={{8,0},{72,64},{10,2},{74,66},{12,4},{76,68},{14,6},{78,70},{16,8},... | collective-permute-start | bytes 4616 | tf_op jit(solution)/shard_map/ppermute | solution.py:36
  111.5 5.5 %collective-permute-start.23 = (f32[3,128]{1,0:T(4,128)S(1)}, f32[3,128]{1,0:T(4,128)S(1)}, u32[]{:S(2)}, u32[]{:S(2)}) collective-permute-start(f32[3,128]{1,0:T(4,128)S(1)} %get-tuple-element.73), channel_id=1, source_target_pairs={{56,0},{120,64},{58,2},{122,66},{60,4},{124,68},{62,6},{126,70},{0... | collective-permute-start | bytes 4616 | tf_op jit(solution)/shard_map/ppermute | solution.py:36
  117.0 14.8 %collective-permute-start.25 = (f32[1,128]{1,0:T(1,128)S(1)}, f32[1,128]{1,0:T(1,128)S(1)}, u32[]{:S(2)}, u32[]{:S(2)}) collective-permute-start(f32[1,128]{1,0:T(1,128)S(1)} %get-tuple-element.74), channel_id=1, source_target_pairs={{0,0},{64,1},{2,2},{66,3},{4,4},{68,5},{6,6},{70,7},{8,8},{72,9},{... | collective-permute-start | bytes 1544 | tf_op jit(solution)/shard_map/ppermute | solution.py:36
  127.7 4.1 %collective-permute-start.26 = (f32[1,128]{1,0:T(1,128)S(1)}, f32[1,128]{1,0:T(1,128)S(1)}, u32[]{:S(2)}, u32[]{:S(2)}) collective-permute-start(f32[1,128]{1,0:T(1,128)S(1)} %get-tuple-element.75), channel_id=1, source_target_pairs={{0,64},{64,65},{2,66},{66,67},{4,68},{68,69},{6,70},{70,71},{8,72}... | collective-permute-start | bytes 1544 | tf_op jit(solution)/shard_map/ppermute | solution.py:36
  129.7 5.8 %collective-permute-start.24 = (f32[1,128]{1,0:T(1,128)S(1)}, f32[1,128]{1,0:T(1,128)S(1)}, u32[]{:S(2)}, u32[]{:S(2)}) collective-permute-start(f32[1,128]{1,0:T(1,128)S(1)} %get-tuple-element.76), channel_id=1, source_target_pairs={{0,448},{64,449},{2,450},{66,451},{4,452},{68,453},{6,454},{70,455... | collective-permute-start | bytes 1544 | tf_op jit(solution)/shard_map/ppermute | solution.py:36

commit v2 on v1

--- a/solution.py
+++ b/solution.py
@@ -36,12 +36,20 @@
     return lax.ppermute(x, AXES, pairs)
 
 
-def bring_home(step):
-    return [(place((a + step) % SIDE, b, d), home(a, b, d)) for a, b, d in bricks()]
-
-
-def send_back(step):
-    return [(home(a, b, d), place((a + step) % SIDE, b, d)) for a, b, d in bricks()]
+def bring_home():
+    return [(place(a, b, d), home(a, b, d)) for a, b, d in bricks()]
+
+
+def around():
+    gx, gz = lax.axis_index("gx"), lax.axis_index("gz")
+    a, d = (gz % 2) * 4 + gx // 2, (gz // 2) * 2 + gx % 2
+    step = np.arange(-1, 2, dtype=np.int32)
+    dz, dx = jnp.asarray(np.repeat(step, 3)), jnp.asarray(np.tile(step, 3))
+    return ((a + dx) % SIDE) * SIDE + (d + dz) % SIDE
+
+
+def exchange(x):
+    return lax.all_to_all(x, ("gx", "gz"), 0, 0, tiled=True)
 
 
 def shift(axis, step):
@@ -108,19 +116,77 @@
     return act * env, dact * env + act * denv
 
 
-def call(kernel, outs, *args, flops=1_000_000, limit=40):
+def call(kernel, outs, *args, flops=1_000_000, limit=16, scratch=(), far=False, index=False):
+    params = {}
+    if index:
+        params["in_specs"] = [pl.BlockSpec(memory_space=pltpu.SMEM)] + [
+            pl.BlockSpec(memory_space=pltpu.VMEM)
+        ] * (len(args) - 1)
+    if far:
+        spaces = [pltpu.SMEM if a.size == 1 else pltpu.HBM for a in args]
+        args = [
+            a if s is pltpu.SMEM else pltpu.with_memory_space_constraint(a, s)
+            for a, s in zip(args, spaces)
+        ]
+        params["in_specs"] = [pl.BlockSpec(memory_space=s) for s in spaces]
+        scratch = list(scratch) + [pltpu.SemaphoreType.DMA((len(args),))]
     return pl.pallas_call(
         kernel,
         out_shape=tuple(jax.ShapeDtypeStruct(s, d) for s, d in outs),
+        scratch_shapes=scratch,
         compiler_params=pltpu.CompilerParams(vmem_limit_bytes=limit * 1024 * 1024),
         cost_estimate=pl.CostEstimate(flops=flops, bytes_accessed=1_000_000, transcendentals=0),
+        **params,
     )(*args)
 
 
-def weights_kernel(embed, rin, rout, wup, emb_o, t0_o, win_o, wout_o, woutb_o, wup_o):
-    emb = embed[...].astype(BF16)
-    emb_o[...] = emb
-    table = nn(emb.astype(F32), wup[0], precision=HIGH)
+def fetch(sources, targets, sems):
+    copies = [
+        pltpu.make_async_copy(s, t, sems.at[i]) for i, (s, t) in enumerate(zip(sources, targets))
+    ]
+    for copy in copies:
+        copy.start()
+    for copy in copies:
+        copy.wait()
+
+
+def like(*args):
+    return [pltpu.VMEM(a.shape, a.dtype) for a in args]
+
+
+def pack_kernel(*refs):
+    (atom_count, edge_count), far, (rows_o, edges_o) = refs[:2], refs[2:6], refs[6:8]
+    near, sems = refs[8:12], refs[12]
+    fetch(far, near, sems)
+    positions, species, sender, receiver = near
+    atoms, count = species.shape[-1], sender.shape[-1]
+    owned = lax.broadcasted_iota(jnp.int32, (1, atoms), 1) < atom_count[0, 0, 0]
+    kinds = jnp.where(owned, species[0, 0], -1).astype(F32)
+    for c, part in enumerate([positions[k, 0, 0] for k in range(3)] + [kinds]):
+        rows_o[0, :, atoms * c : atoms * c + atoms] = part
+    rows_o[1:] = jnp.broadcast_to(rows_o[0:1], (rows_o.shape[0] - 1, 1, 4 * atoms))
+    live = lax.broadcasted_iota(jnp.int32, (1, count), 1) < edge_count[0, 0, 0]
+    s, r = sender[0, 0], receiver[0, 0]
+    block, slot = jnp.right_shift(s, 5), jnp.bitwise_and(s, 31)
+    one = lambda flag: jnp.where(flag, 1, 0)
+    bx = one(block >= 9) + one(block >= 18)
+    block = block - 9 * bx
+    by = one(block >= 3) + one(block >= 6)
+    bz = block - 3 * by
+    s = (bz * 9 + by * 3 + bx) * 32 + slot
+    edges_o[0:1] = jnp.where(live, s, 1023)
+    edges_o[1:2] = jnp.where(live, r, 99)
+
+
+def weights_kernel(*refs):
+    far, outs, near, sems = refs[:9], refs[9:21], refs[21:25], refs[25]
+    emb_o, t0_o, win_o, wout_o, woutb_o, wup_o, wupt_o, lam_o, wmix_o, one_o, hidden_o, out_o = outs
+    fetch(far, list(near) + [lam_o, wmix_o, one_o, hidden_o, out_o], sems)
+    embed, rin, rout, wup = near
+    wupt_o[...] = wup[1]
+    emb_o[...] = jnp.zeros_like(emb_o)
+    emb_o[0 : embed.shape[0]] = embed[...].astype(BF16).astype(F32)
+    table = nn(emb_o[...], wup[0], precision=HIGH)
     hi, lo = split(table.T)
     t0_o[...] = jnp.concatenate([hi, lo], axis=1)
     for t in range(2):
@@ -138,14 +204,14 @@
 
 
 def first_kernel(
-    box, left, own, right, edges, emb, t0, win, wout, lam, wmix, read_one, read_out,
+    box, places, below, level, above, edges, emb, t0, win, wout, lam, wmix, read_one, read_out,
     h1_o, e1_o, seed1_o, seed2_o, geo_o, pool_o, at_o, lift_o, base_o, table,
 ):
-    count = edges.shape[1]
     table[...] = jnp.zeros_like(table)
-    table[0:9] = left[...]
-    table[9:18] = own[...]
-    table[18:27] = right[...]
+    for k in range(9):
+        for dy, plane in enumerate((below, level, above)):
+            at = k // 3 * 9 + dy * 3 + k % 3
+            table[at : at + 1] = plane[places[k]]
     rows = table[...]
     hi = rows.astype(BF16).astype(F32)
     rest = rows - hi
@@ -211,12 +277,12 @@
         product = product + weight * square
         first = 0 if order == 1 else 96
         at_o[first : first + 32 * (2 * order + 1)] = (2.0 * weight * total).astype(BF16)
-    kinds = own[4:5, 96:128]
+    kinds = rows[13:14, 96:128]
     mask = jnp.where(kinds >= 0.0, 1.0, 0.0)
     own_kind = jnp.where(
         lax.broadcasted_iota(jnp.int32, (128, 32), 0) == kinds.astype(jnp.int32), 1.0, 0.0
     ).astype(BF16)
-    h0 = tn(own_kind, emb[...])
+    h0 = tn(own_kind, emb[...].astype(BF16))
     h1 = h0 + nn(product, wmix[0], precision=HIGH)
     h1_o[...] = h1.astype(BF16)
     e1_o[...] = nt(read_one[...], h1, precision=HIGH) * mask
@@ -286,13 +352,13 @@
         )
         product = product + lam[1, order - 1 : order] * square
     h2 = own[128:160].astype(F32) + nn(product, wmix[1], precision=HIGH)
-    pre = nn(h2, read_hidden[...], precision=HIGH)
+    pre = nt(h2, read_hidden[...], precision=HIGH)
     sig = 1.0 / (1.0 + jnp.exp(-pre))
     inner = pre * sig
     seed = seed2[...]
     e2_o[...] = nt(jnp.ones((8, 16), F32), inner * seed, precision=HIGH)
     dpre = seed * sig * (1.0 + pre * (1.0 - sig))
-    dh2 = nt(dpre, read_hidden[...], precision=HIGH)
+    dh2 = nn(dpre, read_hidden[...], precision=HIGH)
     dh2_o[...] = dh2
     dp = nt(dh2, wmix[1], precision=HIGH)
     da_o[0:32] = dp.astype(BF16)
@@ -334,8 +400,8 @@
     drel_o[...] = jnp.concatenate([dx, dy, dz, none, none, none, none, none], axis=0)
 
 
-def force_kernel(edges, folded, dh2, seed1, e1, e2, wup, wmix, v, drel2, left_o, own_o, right_o, rows):
-    dh1 = dh2[...] + seed1[...] + nt(folded[...], wup[1], precision=HIGH)
+def force_kernel(edges, folded, dh2, seed1, e1, e2, wup, wmix, v, drel2, below_o, level_o, above_o, rows):
+    dh1 = dh2[...] + seed1[...] + nt(folded[...], wup[...], precision=HIGH)
     dp = nt(dh1, wmix[0], precision=HIGH)
     hi, lo = split(dp)
     dp2 = jnp.concatenate([hi, lo], axis=0)
@@ -363,9 +429,24 @@
             rows[13:14, 32 * k : 32 * k + 32] - pulled[2 * k : 2 * k + 1] - pulled[2 * k + 1 : 2 * k + 2]
         )
     rows[13:14, 96:128] = e1[...] + e2[0:1]
-    left_o[...] = rows[0:9]
-    own_o[...] = rows[9:18]
-    right_o[...] = rows[18:27]
+    for dz in range(3):
+        for dy, out in enumerate((below_o, level_o, above_o)):
+            out[3 * dz : 3 * dz + 3] = rows[9 * dz + 3 * dy : 9 * dz + 3 * dy + 3]
+
+
+def spread_kernel(places, a, b, c, out):
+    out[...] = jnp.zeros_like(out)
+    total = a[...] + b[...] + c[...]
+    for k in range(9):
+        out[places[k]] = total[k : k + 1]
+
+
+def last_kernel(rows, energy_o, forces_o):
+    atoms = energy_o.shape[-1]
+    total = jnp.sum(rows[...], axis=0)
+    energy_o[0, 0] = total[:, 3 * atoms : 4 * atoms]
+    for k in range(3):
+        forces_o[k, 0, 0] = total[:, atoms * k : atoms * k + atoms]
 
 
 def local(
@@ -376,55 +457,48 @@
     count = sender.shape[-1]
     box = (SIDE * 4 * lattice_step, SIDE * 4 * lattice_step, SIDE * (atoms // 16) * lattice_step)
 
-    owned = jnp.arange(atoms, dtype=jnp.int32) < atom_count[0, 0, 0]
-    kinds = jnp.where(owned, species[0, 0, 0], -1).astype(F32)
-    row = jnp.concatenate([positions.reshape(3 * atoms), kinds])[None]
-    s, r = sender[0, 0, 0], receiver[0, 0, 0]
-    block, slot = s // atoms, s % atoms
-    block = (block % 3) * 9 + (block // 3 % 3) * 3 + block // 9
-    live = jnp.arange(count, dtype=jnp.int32) < edge_count[0, 0, 0]
-    edges = jnp.stack([jnp.where(live, block * atoms + slot, 1023), jnp.where(live, r, 99)])
-
-    padded = jnp.pad(embed, ((0, 128 - embed.shape[0]), (0, 0)))
-    emb, t0, win, wout, woutb, wup = call(
+    places = around()
+    rows, edges = call(
+        pack_kernel, [((SIDE * SIDE, 1, 4 * atoms), F32), ((2, count), jnp.int32)],
+        atom_count, edge_count, positions, species, sender, receiver, far=True,
+        scratch=like(positions, species, sender, receiver),
+    )
+    level = exchange(rows)
+    below, level, above = widen(level, 1)
+    edges = move(edges, bring_home())
+
+    weights = call(
         weights_kernel,
-        [((128, 128), BF16), ((128, 256), BF16), ((2, 64, 32), BF16), ((2, 384, 192), BF16),
-         ((2, 64, 384), BF16), ((128, 256), BF16)],
-        padded, radial_in, radial_out, w_up,
-    )
-
-    line = jnp.concatenate([move(row, bring_home(d)) for d in (-1, 0, 1)], axis=0)
-    edges = move(edges, bring_home(0))
-    plane = jnp.concatenate(widen(line, 1), axis=0)
-    left, own, right = widen(plane, 2)
-
-    h1, e1, seed1, seed2, geo, pool, at, lift, base = pl.pallas_call(
+        [((128, 128), F32), ((128, 256), BF16), ((2, 64, 32), BF16), ((2, 384, 192), BF16),
+         ((2, 64, 384), BF16), ((128, 256), BF16), ((128, 128), F32), ((2, 2, 128), F32), ((2, 128, 128), F32),
+         ((1, 128), F32), ((16, 128), F32), ((1, 16), F32)],
+        embed, radial_in, radial_out, w_up, lam, w_mix, read_one[None], read_hidden.T, read_out[None],
+        far=True, scratch=like(embed, radial_in, radial_out, w_up),
+    )
+    emb, t0, win, wout, woutb, wup, wup_t, lam, w_mix, read_one, read_hidden, read_out = weights
+
+    h1, e1, seed1, seed2, geo, pool, at, lift, base = call(
         functools.partial(first_kernel, box),
-        out_shape=tuple(
-            jax.ShapeDtypeStruct(s, d)
-            for s, d in (
-                ((32, 128), BF16), ((1, 32), F32), ((32, 128), F32), ((32, 16), F32), ((8, count), F32),
-                ((288, count), BF16), ((256, 128), BF16), ((128, count), BF16), ((384, count), BF16),
-            )
-        ),
-        scratch_shapes=[pltpu.VMEM((32, 128), F32)],
-        compiler_params=pltpu.CompilerParams(vmem_limit_bytes=40 * 1024 * 1024),
-        cost_estimate=pl.CostEstimate(flops=1_000_000, bytes_accessed=1_000_000, transcendentals=0),
-    )(left, own, right, edges, emb, t0, win, wout, lam, w_mix, read_one[None], read_out[None])
+        [((32, 128), BF16), ((1, 32), F32), ((32, 128), F32), ((32, 16), F32), ((8, count), F32),
+         ((288, count), BF16), ((256, 128), BF16), ((128, count), BF16), ((384, count), BF16)],
+        places, below, level, above, edges, emb, t0, win, wout, lam, w_mix, read_one, read_out,
+        scratch=[pltpu.VMEM((32, 128), F32)], index=True,
+    )
 
     line = jnp.concatenate(widen(h1, 0), axis=0)
-    plane = jnp.concatenate(widen(line, 1), axis=0)
-    left, own, right = widen(plane, 2)
-
-    hotref, rad, slope = call(
+    hidden = call(
         radial_kernel,
         [((864, count), BF16), ((384, count), F32), ((64, count), F32)],
         edges, geo, win, wout, flops=1_000_000_000,
     )
-    (v,) = call(
+    line, (hotref, rad, slope) = lax.optimization_barrier((line, hidden))
+    plane = jnp.concatenate(widen(line, 1), axis=0)
+    hidden = call(
         direction_kernel, [((384, count), BF16)], edges, geo, pool, at, lift, base, win, wout,
         flops=1_000_000_000,
     )
+    plane, (v,) = lax.optimization_barrier((plane, hidden))
+    left, own, right = widen(plane, 2)
 
     dleft, down, dright, dh2, e2, drad, base2, da = call(
         second_kernel,
@@ -450,20 +524,19 @@
         flops=1_000_000_000,
     )
 
-    left, own, right = pl.pallas_call(
-        force_kernel,
-        out_shape=tuple(jax.ShapeDtypeStruct((9, 128), F32) for _ in range(3)),
-        scratch_shapes=[pltpu.VMEM((32, 128), F32)],
-        compiler_params=pltpu.CompilerParams(vmem_limit_bytes=40 * 1024 * 1024),
-        cost_estimate=pl.CostEstimate(flops=1_000_000, bytes_accessed=1_000_000, transcendentals=0),
-    )(edges, folded, dh2, seed1, e1, e2, w_up, w_mix, v, drel2)
-
-    plane = own + move(left, shift(2, 1)) + move(right, shift(2, -1))
-    line = plane[3:6] + move(plane[0:3], shift(1, 1)) + move(plane[6:9], shift(1, -1))
-    row = sum(move(line[d + 1 : d + 2], send_back(d)) for d in (-1, 0, 1))
-    forces = row[0, : 3 * atoms].reshape(3, 1, 1, 1, atoms)
-    site_energy = row[0, 3 * atoms :].reshape(1, 1, 1, atoms)
-    return (site_energy, forces)
+    below, level, above = call(
+        force_kernel, [((9, 128), F32)] * 3,
+        edges, folded, dh2, seed1, e1, e2, wup_t, w_mix, v, drel2,
+        scratch=[pltpu.VMEM((32, 128), F32)],
+    )
+
+    (rows,) = call(
+        spread_kernel, [((SIDE * SIDE, 1, 4 * atoms), F32)],
+        places, level, move(below, shift(1, 1)), move(above, shift(1, -1)), index=True,
+    )
+    return call(
+        last_kernel, [((1, 1, 1, atoms), F32), ((3, 1, 1, 1, atoms), F32)], exchange(rows)
+    )
 
 
 def solution(mesh):

time: 138 us -> 120 us (0.87)
  starting transfers between devices: 88.3 us -> 58.8 us
  blocking collectives: 0 us -> 21 us
  local copies, waits for them, and re-layouts: 13.2 us -> 0.01 us
  Pallas kernels: 12.4 us -> 16.9 us
  other arithmetic: 2.43 us -> 0.75 us
  waiting for transfers between devices: 17.9 us -> 19.5 us
    ppermute x27 -> x17, starting transfers between devices: 88.3 us -> 43.9 us  [move(): return lax.ppermute(x, AXES, pairs)]
    all_to_all x0 -> x1, blocking collectives: none -> 21 us  [exchange(): return lax.all_to_all(x, ('gx', 'gz'), 0, 0, tiled=True)]
    all_to_all x0 -> x1, starting transfers between devices: none -> 14.9 us  [exchange(): return lax.all_to_all(x, ('gx', 'gz'), 0, 0, tiled=True)]
    unnamed x43 -> x0, local copies, waits for them, and re-layouts: 10.4 us -> none
    pallas_call x5 -> x10, Pallas kernels: 8.77 us -> 16.9 us  [call(): pl.pallas_call(kernel, out_shape=tuple((jax.ShapeDtypeStruct(s, d) for s,...]
    all_to_all x0 -> x1, waiting for transfers between devices: none -> 5.63 us  [exchange(): return lax.all_to_all(x, ('gx', 'gz'), 0, 0, tiled=True)]
    ppermute x27 -> x17, waiting for transfers between devices: 17.9 us -> 13.8 us  [move(): return lax.ppermute(x, AXES, pairs)]
    pallas_call x2 -> x0, Pallas kernels: 3.64 us -> none  [the longest x1 2.29 us: local(): pl.pallas_call(functools.partial(first_kernel, box), out_shape=tuple((jax...]
  transfers between devices with their start and end apart: 27 -> 18, of which waited for: 10 -> 10; matrix products, arithmetic and copies ran while one was open for 4% -> 1% of each run, Pallas kernels for 3% -> 5%
where the time goes in v2:
time: 120 us; the launch traced here: 119 us
  starting transfers between devices  58.8 us (49%)
  blocking collectives  21 us (18%)
  waiting for transfers between devices  19.5 us (16%)
  Pallas kernels  16.9 us (14%)
  between operations  2.21 us (2%)
    ppermute x17, starting transfers between devices, move(): return lax.ppermute(x, AXES, pairs)  43.9 us
    all_to_all x1, blocking collectives, exchange(): return lax.all_to_all(x, ('gx', 'gz'), 0, 0, tiled=True)  21 us
    pallas_call x10, Pallas kernels, call(): pl.pallas_call(kernel, out_shape=tuple((jax.ShapeDtypeStruct(s, d) for s,...  16.9 us
    all_to_all x1, starting transfers between devices, exchange(): return lax.all_to_all(x, ('gx', 'gz'), 0, 0, tiled=True)  14.9 us
    ppermute x17, waiting for transfers between devices, move(): return lax.ppermute(x, AXES, pairs)  13.8 us
    all_to_all x1, waiting for transfers between devices, exchange(): return lax.all_to_all(x, ('gx', 'gz'), 0, 0, tiled=True)  5.63 us
  transfers between devices with their start and end apart: 18, of which 10 were waited for; matrix products, arithmetic and copies ran while one was open for 1% of the time, Pallas kernels for 5%

profile of v2, /device:TPU:1, one launch (start us, length us, event | category | flops | bytes accessed | tf_op | source)
XLA Modules:
  0.0 119.1 jit_solution(17448310603430387524)
XLA Ops:
  1.9 1.5 %shard_map.176 = (f32[64,1,128]{2,1,0:T(1,128)}, s32[2,1792]{1,0:T(2,128)S(1)}) custom-call(s32[1,1,1]{2,1,0:T(1,128)S(6)} %copy.19.refs_0_, s32[1,1,1]{2,1,0:T(1,128)S(6)} %copy.20.refs_1_, f32[3,1,1,1,32]{4,3,2,1,0:T(1,128)} %refs_2_.2, s32[1,1,1,32]{3,2,1,0:T(1,128)} %refs_3_.2, s32[1,1,1,1792]{3,2,1,0:T(1,128)} %refs_4_.2, s32[1,1,1,1792]{3,2,1,0:T(1,128)} %refs_5_.2), custom_call_target="tpu_custom_call" | custom-call | flops 1000000 | bytes 1000000 | tf_op jit(solution)/shard_map/pallas_call | solution.py:133
  3.4 14.9 %all-to-all-start = ((f32[64,1,128]{2,1,0:T(1,128)}), f32[64,1,128]{2,1,0:T(1,128)S(1)}, u32[]{:S(2)}, u32[]{:S(2)}) async-start(f32[64,1,128]{2,1,0:T(1,128)} %get-tuple-element.46), calls=%async_computation | async-start | bytes 65536 | tf_op jit(solution)/shard_map/all_to_all | solution.py:52
  18.3 3.5 %collective-permute-start = (s32[2,1792]{1,0:T(2,128)S(1)}, s32[2,1792]{1,0:T(2,128)S(1)}, u32[]{:S(2)}, u32[]{:S(2)}) collective-permute-start(s32[2,1792]{1,0:T(2,128)S(1)} %get-tuple-element.45), channel_id=1, source_target_pairs={{0,0},{1,64},{2,2},{3,66},{4,4},{5,68},{6,6},{7,70},{8,8},{9,72},{... | collective-permute-start | bytes 43016 | tf_op jit(solution)/shard_map/ppermute | solution.py:36
  21.9 5.6 %all-to-all-done.level = f32[64,1,128]{2,1,0:T(1,128)S(1)} async-done(((f32[64,1,128]{2,1,0:T(1,128)}), f32[64,1,128]{2,1,0:T(1,128)S(1)}, u32[]{:S(2)}, u32[]{:S(2)}) %all-to-all-start) | async-done | bytes 32800 | tf_op jit(solution)/shard_map/all_to_all | solution.py:52
  27.5 5.1 %collective-permute-start.2 = (f32[64,1,128]{2,1,0:T(1,128)S(1)}, f32[64,1,128]{2,1,0:T(1,128)S(1)}, u32[]{:S(2)}, u32[]{:S(2)}) collective-permute-start(f32[64,1,128]{2,1,0:T(1,128)S(1)} %all-to-all-done.level), channel_id=1, source_target_pairs={{8,0},{72,64},{10,2},{74,66},{12,4},{76,68},{14,6},{78,70},{16,8},... | collective-permute-start | bytes 98312 | tf_op jit(solution)/shard_map/ppermute | solution.py:36
  32.6 1.9 %collective-permute-start.1 = (f32[64,1,128]{2,1,0:T(1,128)S(1)}, f32[64,1,128]{2,1,0:T(1,128)S(1)}, u32[]{:S(2)}, u32[]{:S(2)}) collective-permute-start(f32[64,1,128]{2,1,0:T(1,128)S(1)} %all-to-all-done.level), channel_id=1, source_target_pairs={{56,0},{120,64},{58,2},{122,66},{60,4},{124,68},{62,6},{126,70},{0... | collective-permute-start | bytes 98312 | tf_op jit(solution)/shard_map/ppermute | solution.py:36
  34.5 0.7 fusion.2.places
  35.2 1.5 %shard_map.177 = (f32[128,128]{1,0:T(8,128)S(1)}, bf16[128,256]{1,0:T(8,128)(2,1)S(1)}, bf16[2,64,32]{2,1,0:T(8,128)(2,1)S(1)}, bf16[2,384,192]{2,1,0:T(8,128)(2...) custom-call(f32[89,128]{1,0:T(8,128)} %refs_0_.2, ...), custom_call_target="tpu_custom_call" | custom-call | flops 1000000 | bytes 1000000 | tf_op jit(solution)/shard_map/pallas_call | solution.py:133
  36.8 0.0 collective-permute-done.edges
  36.8 0.0 collective-permute-done.2.above
  36.8 1.7 %collective-permute-done.1.below = f32[64,1,128]{2,1,0:T(1,128)S(1)} collective-permute-done((f32[64,1,128]{2,1,0:T(1,128)S(1)}, f32[64,1,128]{2,1,0:T(1,128)S(1)}, u32[]{:S(2)}, u32[]{:S(2)}) %collective-permute-start.1) | collective-permute-done | bytes 32800 | tf_op jit(solution)/shard_map/ppermute | solution.py:36
  38.5 2.8 %shard_map.178 = (bf16[32,128]{1,0:T(8,128)(2,1)S(1)}, f32[1,32]{1,0:T(1,128)S(1)}, f32[32,128]{1,0:T(8,128)S(1)}, f32[32,16]{1,0:T(8,128)S(1)}, f32[8,1792]{1,0...) custom-call(s32[9]{0:T(128)S(1)} %fusion.2.places, ...), custom_call_target="tpu_custom_call" | custom-call | flops 1000000 | bytes 1000000 | tf_op jit(solution)/shard_map/pallas_call | solution.py:133
  41.3 2.5 %collective-permute-start.4 = (bf16[32,128]{1,0:T(8,128)(2,1)S(1)}, bf16[32,128]{1,0:T(8,128)(2,1)S(1)}, u32[]{:S(2)}, u32[]{:S(2)}) collective-permute-start(bf16[32,128]{1,0:T(8,128)(2,1)S(1)} %get-tuple-element.55), channel_id=1, source_target_pairs={{128,0},{192,64},{130,2},{194,66},{132,4},{196,68},{134,6},{198,70... | collective-permute-start | bytes 24584 | tf_op jit(solution)/shard_map/ppermute | solution.py:36
  43.8 2.8 %collective-permute-start.3 = (bf16[32,128]{1,0:T(8,128)(2,1)S(1)}, bf16[32,128]{1,0:T(8,128)(2,1)S(1)}, u32[]{:S(2)}, u32[]{:S(2)}) collective-permute-start(bf16[32,128]{1,0:T(8,128)(2,1)S(1)} %get-tuple-element.55), channel_id=1, source_target_pairs={{385,0},{449,64},{387,2},{451,66},{389,4},{453,68},{391,6},{455,70... | collective-permute-start | bytes 24584 | tf_op jit(solution)/shard_map/ppermute | solution.py:36
  46.6 1.5 %shard_map.179 = (bf16[864,1792]{1,0:T(8,128)(2,1)S(1)}, f32[384,1792]{1,0:T(8,128)S(1)}, f32[64,1792]{1,0:T(8,128)S(1)}) custom-call(s32[2,1792]{1,0:T(2,128)S(1)} %collective-permute-done.edges, f32[8,1792]{1,0:T(8,128)S(1)} %get-tuple-element.56.geo, bf16[2,64,32]{2,1,0:T(8,128)(2,1)S(1)} %get-tuple-element.49.win, ...), custom_call_target="tpu_custom_call" | custom-call | flops 1000000000 | bytes 1000000 | tf_op jit(solution)/shard_map/pallas_call | solution.py:133
  48.2 0.0 collective-permute-done.4
  48.2 1.2 %collective-permute-done.3 = bf16[32,128]{1,0:T(8,128)(2,1)S(1)} collective-permute-done((bf16[32,128]{1,0:T(8,128)(2,1)S(1)}, bf16[32,128]{1,0:T(8,128)(2,1)S(1)}, u32[]{:S(2)}, u32[]{:S(2)}) %collective-permute-start.3) | collective-permute-done | bytes 8224 | tf_op jit(solution)/shard_map/ppermute | solution.py:36
  49.4 2.9 %collective-permute-start.6 = (bf16[96,128]{1,0:T(8,128)(2,1)S(1)}, bf16[96,128]{1,0:T(8,128)(2,1)S(1)}, u32[]{:S(2)}, u32[]{:S(2)}) collective-permute-start(bf16[96,128]{1,0:T(8,128)(2,1)S(1)} %pad_maximum_fusion.1), channel_id=1, source_target_pairs={{8,0},{72,64},{10,2},{74,66},{12,4},{76,68},{14,6},{78,70},{16,8},... | collective-permute-start | bytes 73736 | tf_op jit(solution)/shard_map/ppermute | solution.py:36
  52.3 2.4 %collective-permute-start.5 = (bf16[96,128]{1,0:T(8,128)(2,1)S(1)}, bf16[96,128]{1,0:T(8,128)(2,1)S(1)}, u32[]{:S(2)}, u32[]{:S(2)}) collective-permute-start(bf16[96,128]{1,0:T(8,128)(2,1)S(1)} %pad_maximum_fusion.1), channel_id=1, source_target_pairs={{56,0},{120,64},{58,2},{122,66},{60,4},{124,68},{62,6},{126,70},{0... | collective-permute-start | bytes 73736 | tf_op jit(solution)/shard_map/ppermute | solution.py:36
  54.7 2.1 %shard_map.180.v = bf16[384,1792]{1,0:T(8,128)(2,1)S(1)} custom-call(s32[2,1792]{1,0:T(2,128)S(1)} %collective-permute-done.edges, f32[8,1792]{1,0:T(8,128)S(1)} %get-tuple-element.56.geo, bf16[288,1792]{1,0:T(8,128)(2,1)S(1)} %get-tuple-element.61.pool, bf16[256,128]{1,0:T(8,128)(2,1)S(1)} %get-tuple-element.62.at, ...), custom_call_target="tpu_custom_call" | custom-call | flops 1000000000 | bytes 1000000 | tf_op jit(solution)/shard_map/pallas_call | solution.py:133
  56.8 0.0 collective-permute-done.6
  56.8 1.3 %collective-permute-done.5 = bf16[96,128]{1,0:T(8,128)(2,1)S(1)} collective-permute-done((bf16[96,128]{1,0:T(8,128)(2,1)S(1)}, bf16[96,128]{1,0:T(8,128)(2,1)S(1)}, u32[]{:S(2)}, u32[]{:S(2)}) %collective-permute-start.5) | collective-permute-done | bytes 24608 | tf_op jit(solution)/shard_map/ppermute | solution.py:36
  58.1 4.0 %collective-permute-start.8 = (bf16[288,128]{1,0:T(8,128)(2,1)S(1)}, bf16[288,128]{1,0:T(8,128)(2,1)S(1)}, u32[]{:S(2)}, u32[]{:S(2)}) collective-permute-start(bf16[288,128]{1,0:T(8,128)(2,1)S(1)} %pad_maximum_fusion.own), channel_id=1, source_target_pairs={{64,0},{2,64},{66,2},{4,66},{68,4},{6,68},{70,6},{0,70},{72,8},{10... | collective-permute-start | bytes 221192 | tf_op jit(solution)/shard_map/ppermute | solution.py:36
  62.1 0.2 collective-permute-start.7
  62.2 2.0 %collective-permute-done.8.right = bf16[288,128]{1,0:T(8,128)(2,1)S(1)} collective-permute-done((bf16[288,128]{1,0:T(8,128)(2,1)S(1)}, bf16[288,128]{1,0:T(8,128)(2,1)S(1)}, u32[]{:S(2)}, u32[]{:S(2)}) %collective-permute-start.8) | collective-permute-done | bytes 73760 | tf_op jit(solution)/shard_map/ppermute | solution.py:36
  64.3 0.0 collective-permute-done.7.left
  64.3 4.0 %shard_map.181 = (bf16[288,128]{1,0:T(8,128)(2,1)S(1)}, f32[288,128]{1,0:T(8,128)S(1)}, bf16[288,128]{1,0:T(8,128)(2,1)S(1)}, f32[32,128]{1,0:T(8,128)S(1)}, f32...) custom-call(bf16[288,128]{1,0:T(8,128)(2,1)S(1)} %collective-permute, ...), custom_call_target="tpu_custom_call" | custom-call | flops 1000000 | bytes 1000000 | tf_op jit(solution)/shard_map/pallas_call | solution.py:133
  68.3 2.8 %collective-permute-start.9 = (bf16[288,128]{1,0:T(8,128)(2,1)S(1)}, bf16[288,128]{1,0:T(8,128)(2,1)S(1)}, u32[]{:S(2)}, u32[]{:S(2)}) collective-permute-start(bf16[288,128]{1,0:T(8,128)(2,1)S(1)} %get-tuple-element.72), channel_id=1, source_target_pairs={{64,0},{2,64},{66,2},{4,66},{68,4},{6,68},{70,6},{0,70},{72,8},{10... | collective-permute-start | bytes 221192 | tf_op jit(solution)/shard_map/ppermute | solution.py:36
  71.1 0.0 collective-permute-start.10
  71.1 1.0 collective-permute-done.9
  72.1 0.4 collective-permute-done.10
  72.6 2.0 %collective-permute-start.11 = (bf16[96,128]{1,0:T(8,128)(2,1)S(1)}, bf16[96,128]{1,0:T(8,128)(2,1)S(1)}, u32[]{:S(2)}, u32[]{:S(2)}) collective-permute-start(bf16[96,128]{1,0:T(8,128)(2,1)S(1)} %get-tuple-element.92), channel_id=1, source_target_pairs={{8,0},{72,64},{10,2},{74,66},{12,4},{76,68},{14,6},{78,70},{16,8},... | collective-permute-start | bytes 73736 | tf_op jit(solution)/shard_map/ppermute | solution.py:36
  74.6 3.3 %collective-permute-start.12 = (bf16[96,128]{1,0:T(8,128)(2,1)S(1)}, bf16[96,128]{1,0:T(8,128)(2,1)S(1)}, u32[]{:S(2)}, u32[]{:S(2)}) collective-permute-start(bf16[96,128]{1,0:T(8,128)(2,1)S(1)} %get-tuple-element.93), channel_id=1, source_target_pairs={{56,0},{120,64},{58,2},{122,66},{60,4},{124,68},{62,6},{126,70},{0... | collective-permute-start | bytes 73736 | tf_op jit(solution)/shard_map/ppermute | solution.py:36
  77.9 0.0 collective-permute-done.11
  77.9 2.5 %collective-permute-done.12 = bf16[96,128]{1,0:T(8,128)(2,1)S(1)} collective-permute-done((bf16[96,128]{1,0:T(8,128)(2,1)S(1)}, bf16[96,128]{1,0:T(8,128)(2,1)S(1)}, u32[]{:S(2)}, u32[]{:S(2)}) %collective-permute-start.12) | collective-permute-done | bytes 24608 | tf_op jit(solution)/shard_map/ppermute | solution.py:36
  80.4 1.9 %collective-permute-start.13 = (bf16[32,128]{1,0:T(8,128)(2,1)S(1)}, bf16[32,128]{1,0:T(8,128)(2,1)S(1)}, u32[]{:S(2)}, u32[]{:S(2)}) collective-permute-start(bf16[32,128]{1,0:T(8,128)(2,1)S(1)} %get-tuple-element.94), channel_id=1, source_target_pairs={{128,0},{192,64},{130,2},{194,66},{132,4},{196,68},{134,6},{198,70... | collective-permute-start | bytes 24584 | tf_op jit(solution)/shard_map/ppermute | solution.py:36
  82.3 3.4 %collective-permute-start.14 = (bf16[32,128]{1,0:T(8,128)(2,1)S(1)}, bf16[32,128]{1,0:T(8,128)(2,1)S(1)}, u32[]{:S(2)}, u32[]{:S(2)}) collective-permute-start(bf16[32,128]{1,0:T(8,128)(2,1)S(1)} %get-tuple-element.95), channel_id=1, source_target_pairs={{385,0},{449,64},{387,2},{451,66},{389,4},{453,68},{391,6},{455,70... | collective-permute-start | bytes 24584 | tf_op jit(solution)/shard_map/ppermute | solution.py:36
  85.7 0.7 shard_map.182.drel2
  86.5 0.0 collective-permute-done.13
  86.5 1.5 %collective-permute-done.14 = bf16[32,128]{1,0:T(8,128)(2,1)S(1)} collective-permute-done((bf16[32,128]{1,0:T(8,128)(2,1)S(1)}, bf16[32,128]{1,0:T(8,128)(2,1)S(1)}, u32[]{:S(2)}, u32[]{:S(2)}) %collective-permute-start.14) | collective-permute-done | bytes 8224 | tf_op jit(solution)/shard_map/ppermute | solution.py:36
  88.0 1.4 %shard_map.183 = (f32[9,128]{1,0:T(8,128)S(1)}, f32[9,128]{1,0:T(8,128)S(1)}, f32[9,128]{1,0:T(8,128)S(1)}) custom-call(s32[2,1792]{1,0:T(2,128)S(1)} %collective-permute-done.edges, f32[32,128]{1,0:T(8,128)S(1)} %fusion.1.folded, f32[32,128]{1,0:T(8,128)S(1)} %get-tuple-element.74.dh2, f32[32,128]{1,0:T(8,128)S(1)} %get-tuple-element.75.seed1, ...), custom_call_target="tpu_custom_call" | custom-call | flops 1000000 | bytes 1000000 | tf_op jit(solution)/shard_map/pallas_call | solution.py:133
  89.3 1.9 %collective-permute-start.15 = (f32[9,128]{1,0:T(8,128)S(1)}, f32[9,128]{1,0:T(8,128)S(1)}, u32[]{:S(2)}, u32[]{:S(2)}) collective-permute-start(f32[9,128]{1,0:T(8,128)S(1)} %get-tuple-element.86), channel_id=1, source_target_pairs={{8,0},{72,64},{10,2},{74,66},{12,4},{76,68},{14,6},{78,70},{16,8},... | collective-permute-start | bytes 13832 | tf_op jit(solution)/shard_map/ppermute | solution.py:36
  91.2 3.4 %collective-permute-start.16 = (f32[9,128]{1,0:T(8,128)S(1)}, f32[9,128]{1,0:T(8,128)S(1)}, u32[]{:S(2)}, u32[]{:S(2)}) collective-permute-start(f32[9,128]{1,0:T(8,128)S(1)} %get-tuple-element.87), channel_id=1, source_target_pairs={{56,0},{120,64},{58,2},{122,66},{60,4},{124,68},{62,6},{126,70},{0... | collective-permute-start | bytes 13832 | tf_op jit(solution)/shard_map/ppermute | solution.py:36
  94.6 0.0 collective-permute-done.15.b
  94.6 2.2 %collective-permute-done.16.c = f32[9,128]{1,0:T(8,128)S(1)} collective-permute-done((f32[9,128]{1,0:T(8,128)S(1)}, f32[9,128]{1,0:T(8,128)S(1)}, u32[]{:S(2)}, u32[]{:S(2)}) %collective-permute-start.16) | collective-permute-done | bytes 4640 | tf_op jit(solution)/shard_map/ppermute | solution.py:36
  96.9 0.6 shard_map.184
  97.4 21.0 %all_to_all.10.rows = f32[64,1,128]{2,1,0:T(1,128)S(1)} all-to-all(f32[64,1,128]{2,1,0:T(1,128)S(1)} %shard_map.184), channel_id=1, replica_groups=mesh['gx'=8,'gy'=8,'gz'=8] {'gx','gz'}, dimensions={0} | all-to-all | bytes 65536 | tf_op jit(solution)/shard_map/all_to_all | solution.py:52
  118.4 0.7 shard_map.185
  (7 shorter events, 0.1 us)
Async XLA Ops:
  3.4 24.1 %all-to-all-start = ((f32[64,1,128]{2,1,0:T(1,128)}), f32[64,1,128]{2,1,0:T(1,128)S(1)}, u32[]{:S(2)}, u32[]{:S(2)}) async-start(f32[64,1,128]{2,1,0:T(1,128)} %get-tuple-element.46), calls=%async_computation | async-start | bytes 65536 | tf_op jit(solution)/shard_map/all_to_all | solution.py:52
  18.3 18.5 %collective-permute-start = (s32[2,1792]{1,0:T(2,128)S(1)}, s32[2,1792]{1,0:T(2,128)S(1)}, u32[]{:S(2)}, u32[]{:S(2)}) collective-permute-start(s32[2,1792]{1,0:T(2,128)S(1)} %get-tuple-element.45), channel_id=1, source_target_pairs={{0,0},{1,64},{2,2},{3,66},{4,4},{5,68},{6,6},{7,70},{8,8},{9,72},{... | collective-permute-start | bytes 43016 | tf_op jit(solution)/shard_map/ppermute | solution.py:36
  27.5 9.3 %collective-permute-start.2 = (f32[64,1,128]{2,1,0:T(1,128)S(1)}, f32[64,1,128]{2,1,0:T(1,128)S(1)}, u32[]{:S(2)}, u32[]{:S(2)}) collective-permute-start(f32[64,1,128]{2,1,0:T(1,128)S(1)} %all-to-all-done.level), channel_id=1, source_target_pairs={{8,0},{72,64},{10,2},{74,66},{12,4},{76,68},{14,6},{78,70},{16,8},... | collective-permute-start | bytes 98312 | tf_op jit(solution)/shard_map/ppermute | solution.py:36
  32.6 5.9 %collective-permute-start.1 = (f32[64,1,128]{2,1,0:T(1,128)S(1)}, f32[64,1,128]{2,1,0:T(1,128)S(1)}, u32[]{:S(2)}, u32[]{:S(2)}) collective-permute-start(f32[64,1,128]{2,1,0:T(1,128)S(1)} %all-to-all-done.level), channel_id=1, source_target_pairs={{56,0},{120,64},{58,2},{122,66},{60,4},{124,68},{62,6},{126,70},{0... | collective-permute-start | bytes 98312 | tf_op jit(solution)/shard_map/ppermute | solution.py:36
  41.3 6.9 %collective-permute-start.4 = (bf16[32,128]{1,0:T(8,128)(2,1)S(1)}, bf16[32,128]{1,0:T(8,128)(2,1)S(1)}, u32[]{:S(2)}, u32[]{:S(2)}) collective-permute-start(bf16[32,128]{1,0:T(8,128)(2,1)S(1)} %get-tuple-element.55), channel_id=1, source_target_pairs={{128,0},{192,64},{130,2},{194,66},{132,4},{196,68},{134,6},{198,70... | collective-permute-start | bytes 24584 | tf_op jit(solution)/shard_map/ppermute | solution.py:36
  43.8 5.6 %collective-permute-start.3 = (bf16[32,128]{1,0:T(8,128)(2,1)S(1)}, bf16[32,128]{1,0:T(8,128)(2,1)S(1)}, u32[]{:S(2)}, u32[]{:S(2)}) collective-permute-start(bf16[32,128]{1,0:T(8,128)(2,1)S(1)} %get-tuple-element.55), channel_id=1, source_target_pairs={{385,0},{449,64},{387,2},{451,66},{389,4},{453,68},{391,6},{455,70... | collective-permute-start | bytes 24584 | tf_op jit(solution)/shard_map/ppermute | solution.py:36
  49.4 7.4 %collective-permute-start.6 = (bf16[96,128]{1,0:T(8,128)(2,1)S(1)}, bf16[96,128]{1,0:T(8,128)(2,1)S(1)}, u32[]{:S(2)}, u32[]{:S(2)}) collective-permute-start(bf16[96,128]{1,0:T(8,128)(2,1)S(1)} %pad_maximum_fusion.1), channel_id=1, source_target_pairs={{8,0},{72,64},{10,2},{74,66},{12,4},{76,68},{14,6},{78,70},{16,8},... | collective-permute-start | bytes 73736 | tf_op jit(solution)/shard_map/ppermute | solution.py:36
  52.3 5.8 %collective-permute-start.5 = (bf16[96,128]{1,0:T(8,128)(2,1)S(1)}, bf16[96,128]{1,0:T(8,128)(2,1)S(1)}, u32[]{:S(2)}, u32[]{:S(2)}) collective-permute-start(bf16[96,128]{1,0:T(8,128)(2,1)S(1)} %pad_maximum_fusion.1), channel_id=1, source_target_pairs={{56,0},{120,64},{58,2},{122,66},{60,4},{124,68},{62,6},{126,70},{0... | collective-permute-start | bytes 73736 | tf_op jit(solution)/shard_map/ppermute | solution.py:36
  58.1 6.1 %collective-permute-start.8 = (bf16[288,128]{1,0:T(8,128)(2,1)S(1)}, bf16[288,128]{1,0:T(8,128)(2,1)S(1)}, u32[]{:S(2)}, u32[]{:S(2)}) collective-permute-start(bf16[288,128]{1,0:T(8,128)(2,1)S(1)} %pad_maximum_fusion.own), channel_id=1, source_target_pairs={{64,0},{2,64},{66,2},{4,66},{68,4},{6,68},{70,6},{0,70},{72,8},{10... | collective-permute-start | bytes 221192 | tf_op jit(solution)/shard_map/ppermute | solution.py:36
  62.1 2.2 %collective-permute-start.7 = (bf16[288,128]{1,0:T(8,128)(2,1)S(1)}, bf16[288,128]{1,0:T(8,128)(2,1)S(1)}, u32[]{:S(2)}, u32[]{:S(2)}) collective-permute-start(bf16[288,128]{1,0:T(8,128)(2,1)S(1)} %pad_maximum_fusion.own), channel_id=1, source_target_pairs={{70,0},{0,64},{64,2},{2,66},{66,4},{4,68},{68,6},{6,70},{78,8},{8,... | collective-permute-start | bytes 221192 | tf_op jit(solution)/shard_map/ppermute | solution.py:36
  68.3 3.8 %collective-permute-start.9 = (bf16[288,128]{1,0:T(8,128)(2,1)S(1)}, bf16[288,128]{1,0:T(8,128)(2,1)S(1)}, u32[]{:S(2)}, u32[]{:S(2)}) collective-permute-start(bf16[288,128]{1,0:T(8,128)(2,1)S(1)} %get-tuple-element.72), channel_id=1, source_target_pairs={{64,0},{2,64},{66,2},{4,66},{68,4},{6,68},{70,6},{0,70},{72,8},{10... | collective-permute-start | bytes 221192 | tf_op jit(solution)/shard_map/ppermute | solution.py:36
  71.1 1.4 %collective-permute-start.10 = (bf16[288,128]{1,0:T(8,128)(2,1)S(1)}, bf16[288,128]{1,0:T(8,128)(2,1)S(1)}, u32[]{:S(2)}, u32[]{:S(2)}) collective-permute-start(bf16[288,128]{1,0:T(8,128)(2,1)S(1)} %get-tuple-element.73), channel_id=1, source_target_pairs={{70,0},{0,64},{64,2},{2,66},{66,4},{4,68},{68,6},{6,70},{78,8},{8,... | collective-permute-start | bytes 221192 | tf_op jit(solution)/shard_map/ppermute | solution.py:36
  72.6 5.3 %collective-permute-start.11 = (bf16[96,128]{1,0:T(8,128)(2,1)S(1)}, bf16[96,128]{1,0:T(8,128)(2,1)S(1)}, u32[]{:S(2)}, u32[]{:S(2)}) collective-permute-start(bf16[96,128]{1,0:T(8,128)(2,1)S(1)} %get-tuple-element.92), channel_id=1, source_target_pairs={{8,0},{72,64},{10,2},{74,66},{12,4},{76,68},{14,6},{78,70},{16,8},... | collective-permute-start | bytes 73736 | tf_op jit(solution)/shard_map/ppermute | solution.py:36
  74.6 5.8 %collective-permute-start.12 = (bf16[96,128]{1,0:T(8,128)(2,1)S(1)}, bf16[96,128]{1,0:T(8,128)(2,1)S(1)}, u32[]{:S(2)}, u32[]{:S(2)}) collective-permute-start(bf16[96,128]{1,0:T(8,128)(2,1)S(1)} %get-tuple-element.93), channel_id=1, source_target_pairs={{56,0},{120,64},{58,2},{122,66},{60,4},{124,68},{62,6},{126,70},{0... | collective-permute-start | bytes 73736 | tf_op jit(solution)/shard_map/ppermute | solution.py:36
  80.4 6.0 %collective-permute-start.13 = (bf16[32,128]{1,0:T(8,128)(2,1)S(1)}, bf16[32,128]{1,0:T(8,128)(2,1)S(1)}, u32[]{:S(2)}, u32[]{:S(2)}) collective-permute-start(bf16[32,128]{1,0:T(8,128)(2,1)S(1)} %get-tuple-element.94), channel_id=1, source_target_pairs={{128,0},{192,64},{130,2},{194,66},{132,4},{196,68},{134,6},{198,70... | collective-permute-start | bytes 24584 | tf_op jit(solution)/shard_map/ppermute | solution.py:36
  82.3 5.6 %collective-permute-start.14 = (bf16[32,128]{1,0:T(8,128)(2,1)S(1)}, bf16[32,128]{1,0:T(8,128)(2,1)S(1)}, u32[]{:S(2)}, u32[]{:S(2)}) collective-permute-start(bf16[32,128]{1,0:T(8,128)(2,1)S(1)} %get-tuple-element.95), channel_id=1, source_target_pairs={{385,0},{449,64},{387,2},{451,66},{389,4},{453,68},{391,6},{455,70... | collective-permute-start | bytes 24584 | tf_op jit(solution)/shard_map/ppermute | solution.py:36
  89.3 5.3 %collective-permute-start.15 = (f32[9,128]{1,0:T(8,128)S(1)}, f32[9,128]{1,0:T(8,128)S(1)}, u32[]{:S(2)}, u32[]{:S(2)}) collective-permute-start(f32[9,128]{1,0:T(8,128)S(1)} %get-tuple-element.86), channel_id=1, source_target_pairs={{8,0},{72,64},{10,2},{74,66},{12,4},{76,68},{14,6},{78,70},{16,8},... | collective-permute-start | bytes 13832 | tf_op jit(solution)/shard_map/ppermute | solution.py:36
  91.2 5.6 %collective-permute-start.16 = (f32[9,128]{1,0:T(8,128)S(1)}, f32[9,128]{1,0:T(8,128)S(1)}, u32[]{:S(2)}, u32[]{:S(2)}) collective-permute-start(f32[9,128]{1,0:T(8,128)S(1)} %get-tuple-element.87), channel_id=1, source_target_pairs={{56,0},{120,64},{58,2},{122,66},{60,4},{124,68},{62,6},{126,70},{0... | collective-permute-start | bytes 13832 | tf_op jit(solution)/shard_map/ppermute | solution.py:36

commit v3 on v2

--- a/solution.py
+++ b/solution.py
@@ -40,16 +40,19 @@
     return [(place(a, b, d), home(a, b, d)) for a, b, d in bricks()]
 
 
-def around():
+def here():
     gx, gz = lax.axis_index("gx"), lax.axis_index("gz")
-    a, d = (gz % 2) * 4 + gx // 2, (gz // 2) * 2 + gx % 2
-    step = np.arange(-1, 2, dtype=np.int32)
-    dz, dx = jnp.asarray(np.repeat(step, 3)), jnp.asarray(np.tile(step, 3))
-    return ((a + dx) % SIDE) * SIDE + (d + dz) % SIDE
+    return jnp.stack([(gz % 2) * 4 + gx // 2, (gz // 2) * 2 + gx % 2])
+
+
+def around(brick, k):
+    a, d = brick[0] + (k // 3 - 2 + SIDE), brick[1] + (k % 3 - 1 + SIDE)
+    return jnp.bitwise_and(a, SIDE - 1) * SIDE + jnp.bitwise_and(d, SIDE - 1)
 
 
 def exchange(x):
-    return lax.all_to_all(x, ("gx", "gz"), 0, 0, tiled=True)
+    rows = x.reshape(x.shape[0], 1, x.shape[1])
+    return lax.all_to_all(rows, ("gx", "gz"), 0, 0, tiled=True).reshape(x.shape)
 
 
 def shift(axis, step):
@@ -85,6 +88,16 @@
 def stack3(x):
     hi, lo = split(x)
     return jnp.concatenate([hi, lo, hi], axis=0)
+
+
+def product3(x, stack):
+    hi, lo = split(x)
+    return nn(jnp.concatenate([hi, lo, hi], axis=1), stack)
+
+
+def rows3(w):
+    hi, lo = split(w)
+    return jnp.concatenate([hi, hi, lo], axis=0)
 
 
 def hot(index, rows):
@@ -163,27 +176,24 @@
     owned = lax.broadcasted_iota(jnp.int32, (1, atoms), 1) < atom_count[0, 0, 0]
     kinds = jnp.where(owned, species[0, 0], -1).astype(F32)
     for c, part in enumerate([positions[k, 0, 0] for k in range(3)] + [kinds]):
-        rows_o[0, :, atoms * c : atoms * c + atoms] = part
-    rows_o[1:] = jnp.broadcast_to(rows_o[0:1], (rows_o.shape[0] - 1, 1, 4 * atoms))
+        rows_o[0:1, atoms * c : atoms * c + atoms] = part
+    rows_o[...] = jnp.broadcast_to(rows_o[0:1], rows_o.shape)
     live = lax.broadcasted_iota(jnp.int32, (1, count), 1) < edge_count[0, 0, 0]
     s, r = sender[0, 0], receiver[0, 0]
-    block, slot = jnp.right_shift(s, 5), jnp.bitwise_and(s, 31)
-    one = lambda flag: jnp.where(flag, 1, 0)
-    bx = one(block >= 9) + one(block >= 18)
-    block = block - 9 * bx
-    by = one(block >= 3) + one(block >= 6)
-    bz = block - 3 * by
-    s = (bz * 9 + by * 3 + bx) * 32 + slot
     edges_o[0:1] = jnp.where(live, s, 1023)
     edges_o[1:2] = jnp.where(live, r, 99)
 
 
 def weights_kernel(*refs):
-    far, outs, near, sems = refs[:9], refs[9:21], refs[21:25], refs[25]
-    emb_o, t0_o, win_o, wout_o, woutb_o, wup_o, wupt_o, lam_o, wmix_o, one_o, hidden_o, out_o = outs
-    fetch(far, list(near) + [lam_o, wmix_o, one_o, hidden_o, out_o], sems)
-    embed, rin, rout, wup = near
-    wupt_o[...] = wup[1]
+    far, outs, near, sems = refs[:9], refs[9:23], refs[23:28], refs[28]
+    (emb_o, t0_o, win_o, wout_o, woutb_o, wup_o, mix_o, mixt_o, wupt_o, hw_o), kept = outs[:10], outs[10:]
+    fetch(far, list(near) + list(kept), sems)
+    embed, rin, rout, wup, wmix = near
+    wupt_o[...] = rows3(wup[1].T)
+    for t in range(2):
+        mix_o[t] = rows3(wmix[t])
+        mixt_o[t] = rows3(wmix[t].T)
+    hw_o[...] = rows3(kept[2][...].T)
     emb_o[...] = jnp.zeros_like(emb_o)
     emb_o[0 : embed.shape[0]] = embed[...].astype(BF16).astype(F32)
     table = nn(emb_o[...], wup[0], precision=HIGH)
@@ -203,26 +213,49 @@
     wup_o[...] = jnp.concatenate([hi, lo], axis=1)
 
 
-def first_kernel(
-    box, places, below, level, above, edges, emb, t0, win, wout, lam, wmix, read_one, read_out,
-    h1_o, e1_o, seed1_o, seed2_o, geo_o, pool_o, at_o, lift_o, base_o, table,
-):
+def own_kernel(box, *refs):
+    (brick, below, level, above, edges), weights = refs[:5], refs[5:13]
+    (e1_o, seed1_o, seed2_o, h1_o, parts, table), results = refs[13:19], refs[19:24]
+    read_one, read_out = weights[6:]
     table[...] = jnp.zeros_like(table)
-    for k in range(9):
+    for k in range(15):
+        at = pl.ds(around(brick, k), 1)
         for dy, plane in enumerate((below, level, above)):
-            at = k // 3 * 9 + dy * 3 + k % 3
-            table[at : at + 1] = plane[places[k]]
+            row = k // 3 * 9 + dy * 3 + k % 3
+            table[row : row + 1] = plane[at]
     rows = table[...]
     hi = rows.astype(BF16).astype(F32)
     rest = rows - hi
     mid = rest.astype(BF16).astype(F32)
     low = rest - mid
-    parts = [
-        jnp.concatenate([p[:, 32 * c : 32 * c + 32] for p in (hi, mid, low)], axis=1)
-        for c in range(4)
-    ]
-    lhs = jnp.concatenate(parts, axis=0).astype(BF16)
-    mine = jnp.concatenate([p[13:14] for p in parts] + [jnp.zeros((4, 96), F32)], axis=0)
+    for c in range(4):
+        parts[c] = jnp.concatenate([p[:, 32 * c : 32 * c + 32] for p in (hi, mid, low)], axis=1)
+    h1, mask = first_layer(box, 9, edges, *weights[:6], *results, table, parts)
+    h1_o[...] = h1.astype(BF16)
+    e1_o[...] = nt(read_one[...], h1, precision=HIGH) * mask
+    mask8 = jnp.concatenate([mask, jnp.zeros((7, 32), F32)], axis=0)
+    zero = lax.broadcasted_iota(jnp.int32, (8, 128), 0) == 0
+    seed1_o[...] = tn(mask8, jnp.where(zero, read_one[...], 0.0), precision=HIGH)
+    zero = lax.broadcasted_iota(jnp.int32, (8, 16), 0) == 0
+    seed2_o[...] = tn(mask8, jnp.where(zero, read_out[...], 0.0), precision=HIGH)
+
+
+def sides_kernel(box, before, after, parts, table, h1, *refs):
+    weights, h1_o, results = refs[:6], refs[6], refs[7:]
+    h1_o[32:64] = h1[...]
+    for brick, edges in ((0, before), (2, after)):
+        found = results[:5] if brick == 0 else results[5:]
+        value, _ = first_layer(box, 9 * brick, edges, *weights, *found, table, parts)
+        h1_o[32 * brick : 32 * brick + 32] = value.astype(BF16)
+
+
+def first_layer(
+    box, start, edges, emb, t0, win, wout, lam, mix, geo_o, pool_o, at_o, lift_o, base_o, table, parts
+):
+    lhs = jnp.concatenate([parts[c, start : start + 32] for c in range(4)], axis=0).astype(BF16)
+    middle = start + 13
+    mine = [parts[c, middle : middle + 1] for c in range(4)] + [jnp.zeros((4, 96), F32)]
+    mine = jnp.concatenate(mine, axis=0)
     sender = edges[0:1]
     receiver = edges[1:2]
     slot = ones_at(jnp.bitwise_and(sender, 31), 32).astype(BF16)
@@ -277,25 +310,25 @@
         product = product + weight * square
         first = 0 if order == 1 else 96
         at_o[first : first + 32 * (2 * order + 1)] = (2.0 * weight * total).astype(BF16)
-    kinds = rows[13:14, 96:128]
+    kinds = table[middle : middle + 1, 96:128]
     mask = jnp.where(kinds >= 0.0, 1.0, 0.0)
     own_kind = jnp.where(
         lax.broadcasted_iota(jnp.int32, (128, 32), 0) == kinds.astype(jnp.int32), 1.0, 0.0
     ).astype(BF16)
     h0 = tn(own_kind, emb[...].astype(BF16))
-    h1 = h0 + nn(product, wmix[0], precision=HIGH)
-    h1_o[...] = h1.astype(BF16)
-    e1_o[...] = nt(read_one[...], h1, precision=HIGH) * mask
-    pad = jnp.zeros((7, 32), F32)
-    mask8 = jnp.concatenate([mask, pad], axis=0)
-    zero = lax.broadcasted_iota(jnp.int32, (8, 128), 0) == 0
-    seed1_o[...] = tn(mask8, jnp.where(zero, read_one[...], 0.0), precision=HIGH)
-    zero = lax.broadcasted_iota(jnp.int32, (8, 16), 0) == 0
-    seed2_o[...] = tn(mask8, jnp.where(zero, read_out[...], 0.0), precision=HIGH)
+    return h0 + product3(product, mix[0]), mask
 
 
 def radial_kernel(edges, geo, win, wout, hot_o, rad_o, slope_o):
-    sender = edges[0:1]
+    s = edges[0:1]
+    block, slot = jnp.right_shift(s, 5), jnp.bitwise_and(s, 31)
+    one = lambda flag: jnp.where(flag, 1, 0)
+    bx = one(block >= 9) + one(block >= 18)
+    block = block - 9 * bx
+    by = one(block >= 3) + one(block >= 6)
+    bz = block - 3 * by
+    s = (bz * 9 + by * 3 + bx) * 32 + slot
+    sender = s
     for r in range(0, 864, 96):
         row = lax.broadcasted_iota(jnp.int32, (96, sender.shape[1]), 0) + r
         hot_o[r : r + 96] = jnp.where(row == sender, 1.0, 0.0).astype(BF16)
@@ -331,7 +364,7 @@
 
 
 def second_kernel(
-    left, own, right, hotref, rad, pool, wup, lam, wmix, read_hidden, seed2,
+    left, own, right, hotref, rad, pool, wup, lam, mix, mix_t, hidden_w, read_hidden, seed2,
     dleft_o, down_o, dright_o, dh2_o, e2_o, drad_o, base_o, da_o,
 ):
     feats = jnp.concatenate([left[...], own[...], right[...]], axis=0)
@@ -351,8 +384,8 @@
             for m in range(2 * order + 1)
         )
         product = product + lam[1, order - 1 : order] * square
-    h2 = own[128:160].astype(F32) + nn(product, wmix[1], precision=HIGH)
-    pre = nt(h2, read_hidden[...], precision=HIGH)
+    h2 = own[128:160].astype(F32) + product3(product, mix[1])
+    pre = product3(h2, hidden_w[...])
     sig = 1.0 / (1.0 + jnp.exp(-pre))
     inner = pre * sig
     seed = seed2[...]
@@ -360,7 +393,7 @@
     dpre = seed * sig * (1.0 + pre * (1.0 - sig))
     dh2 = nn(dpre, read_hidden[...], precision=HIGH)
     dh2_o[...] = dh2
-    dp = nt(dh2, wmix[1], precision=HIGH)
+    dp = product3(dh2, mix_t[1])
     da_o[0:32] = dp.astype(BF16)
     for order in (1, 2):
         weight = 2.0 * lam[1, order - 1 : order] * dp
@@ -400,50 +433,60 @@
     drel_o[...] = jnp.concatenate([dx, dy, dz, none, none, none, none, none], axis=0)
 
 
-def force_kernel(edges, folded, dh2, seed1, e1, e2, wup, wmix, v, drel2, below_o, level_o, above_o, rows):
-    dh1 = dh2[...] + seed1[...] + nt(folded[...], wup[...], precision=HIGH)
-    dp = nt(dh1, wmix[0], precision=HIGH)
-    hi, lo = split(dp)
-    dp2 = jnp.concatenate([hi, lo], axis=0)
-    sender = edges[0:1]
-    recv = ones_at(edges[1:2], 32)
-    slot = ones_at(jnp.bitwise_and(sender, 31), 32).astype(BF16)
-    block = ones_at(jnp.right_shift(sender, 5), 32)
-    spread, pulled = [], []
-    for k in range(3):
-        q = nn(dp2, v[128 * k : 128 * k + 128])
-        q = q[0:32] + q[32:64]
-        drel = jnp.sum(q * recv, axis=0, keepdims=True) + drel2[k : k + 1]
-        force = drel * (-1.0 / cutoff_radius)
-        hi, lo = split(force)
-        hi, lo = hi.astype(F32), lo.astype(F32)
-        spread += [block * hi, block * lo]
-        pulled += [hi, lo]
-    pushed = nt(jnp.concatenate(spread, axis=0).astype(BF16), slot)
-    pulled = jnp.concatenate(pulled + [jnp.zeros_like(hi)] * 2, axis=0).astype(BF16)
-    pulled = nt(pulled, recv.astype(BF16))
+def force_kernel(*refs):
+    edges_all, folded, (dh2, seed1, e1, e2, wup_t, mix_t), v_all = refs[:3], refs[3], refs[4:10], refs[10:13]
+    drel2, outs, rows = refs[13], refs[14:17], refs[17]
     rows[...] = jnp.zeros_like(rows)
-    for k in range(3):
-        rows[:, 32 * k : 32 * k + 32] = pushed[64 * k : 64 * k + 32] + pushed[64 * k + 32 : 64 * k + 64]
-        rows[13:14, 32 * k : 32 * k + 32] = (
-            rows[13:14, 32 * k : 32 * k + 32] - pulled[2 * k : 2 * k + 1] - pulled[2 * k + 1 : 2 * k + 2]
-        )
-    rows[13:14, 96:128] = e1[...] + e2[0:1]
-    for dz in range(3):
-        for dy, out in enumerate((below_o, level_o, above_o)):
-            out[3 * dz : 3 * dz + 3] = rows[9 * dz + 3 * dy : 9 * dz + 3 * dy + 3]
-
-
-def spread_kernel(places, a, b, c, out):
+    dh1 = product3(folded[...], wup_t[...])
+    dh1 = jnp.concatenate([dh1[0:32], dh1[32:64] + dh2[...] + seed1[...], dh1[64:96]], axis=0)
+    dp = product3(dh1, mix_t[0])
+    for brick in range(3):
+        start = 9 * brick
+        edges, v = edges_all[brick], v_all[brick]
+        hi, lo = split(dp[32 * brick : 32 * brick + 32])
+        dp2 = jnp.concatenate([hi, lo], axis=0)
+        sender = edges[0:1]
+        recv = ones_at(edges[1:2], 32)
+        slot = ones_at(jnp.bitwise_and(sender, 31), 32).astype(BF16)
+        block = ones_at(jnp.right_shift(sender, 5), 32)
+        spread, pulled = [], []
+        for k in range(3):
+            q = nn(dp2, v[128 * k : 128 * k + 128])
+            q = q[0:32] + q[32:64]
+            drel = jnp.sum(q * recv, axis=0, keepdims=True)
+            if brick == 1:
+                drel = drel + drel2[k : k + 1]
+            force = drel * (-1.0 / cutoff_radius)
+            hi, lo = split(force)
+            hi, lo = hi.astype(F32), lo.astype(F32)
+            spread += [block * hi, block * lo]
+            pulled += [hi, lo]
+        pushed = nt(jnp.concatenate(spread, axis=0).astype(BF16), slot)
+        pulled = jnp.concatenate(pulled + [jnp.zeros_like(hi)] * 2, axis=0).astype(BF16)
+        pulled = nt(pulled, recv.astype(BF16))
+        middle = start + 13
+        for k in range(3):
+            lanes = slice(32 * k, 32 * k + 32)
+            rows[start : start + 27, lanes] += (
+                pushed[64 * k : 64 * k + 27] + pushed[64 * k + 32 : 64 * k + 59]
+            )
+            rows[middle : middle + 1, lanes] -= pulled[2 * k : 2 * k + 1] + pulled[2 * k + 1 : 2 * k + 2]
+    rows[22:23, 96:128] = e1[...] + e2[0:1]
+    for dx in range(5):
+        for dy, out in enumerate(outs):
+            out[3 * dx : 3 * dx + 3] = rows[9 * dx + 3 * dy : 9 * dx + 3 * dy + 3]
+
+
+def spread_kernel(brick, a, b, c, out):
     out[...] = jnp.zeros_like(out)
     total = a[...] + b[...] + c[...]
-    for k in range(9):
-        out[places[k]] = total[k : k + 1]
+    for k in range(15):
+        out[pl.ds(around(brick, k), 1)] = total[k : k + 1]
 
 
 def last_kernel(rows, energy_o, forces_o):
     atoms = energy_o.shape[-1]
-    total = jnp.sum(rows[...], axis=0)
+    total = jnp.sum(rows[...], axis=0, keepdims=True)
     energy_o[0, 0] = total[:, 3 * atoms : 4 * atoms]
     for k in range(3):
         forces_o[k, 0, 0] = total[:, atoms * k : atoms * k + atoms]
@@ -457,82 +500,95 @@
     count = sender.shape[-1]
     box = (SIDE * 4 * lattice_step, SIDE * 4 * lattice_step, SIDE * (atoms // 16) * lattice_step)
 
-    places = around()
+    brick = here()
     rows, edges = call(
-        pack_kernel, [((SIDE * SIDE, 1, 4 * atoms), F32), ((2, count), jnp.int32)],
+        pack_kernel, [((SIDE * SIDE, 4 * atoms), F32), ((2, count), jnp.int32)],
         atom_count, edge_count, positions, species, sender, receiver, far=True,
         scratch=like(positions, species, sender, receiver),
     )
+    edges = move(edges, bring_home())
     level = exchange(rows)
-    below, level, above = widen(level, 1)
-    edges = move(edges, bring_home())
 
     weights = call(
         weights_kernel,
         [((128, 128), F32), ((128, 256), BF16), ((2, 64, 32), BF16), ((2, 384, 192), BF16),
-         ((2, 64, 384), BF16), ((128, 256), BF16), ((128, 128), F32), ((2, 2, 128), F32), ((2, 128, 128), F32),
-         ((1, 128), F32), ((16, 128), F32), ((1, 16), F32)],
-        embed, radial_in, radial_out, w_up, lam, w_mix, read_one[None], read_hidden.T, read_out[None],
-        far=True, scratch=like(embed, radial_in, radial_out, w_up),
-    )
-    emb, t0, win, wout, woutb, wup, wup_t, lam, w_mix, read_one, read_hidden, read_out = weights
-
-    h1, e1, seed1, seed2, geo, pool, at, lift, base = call(
-        functools.partial(first_kernel, box),
-        [((32, 128), BF16), ((1, 32), F32), ((32, 128), F32), ((32, 16), F32), ((8, count), F32),
-         ((288, count), BF16), ((256, 128), BF16), ((128, count), BF16), ((384, count), BF16)],
-        places, below, level, above, edges, emb, t0, win, wout, lam, w_mix, read_one, read_out,
-        scratch=[pltpu.VMEM((32, 128), F32)], index=True,
-    )
-
-    line = jnp.concatenate(widen(h1, 0), axis=0)
+         ((2, 64, 384), BF16), ((128, 256), BF16), ((2, 384, 128), BF16), ((2, 384, 128), BF16), ((384, 128), BF16),
+         ((384, 16), BF16), ((2, 2, 128), F32), ((1, 128), F32), ((16, 128), F32), ((1, 16), F32)],
+        embed, radial_in, radial_out, w_up, w_mix, lam, read_one[None], read_hidden.T, read_out[None],
+        far=True, scratch=like(embed, radial_in, radial_out, w_up, w_mix),
+    )
+    level, weights, edges = lax.optimization_barrier((level, weights, edges))
+    emb, t0, win, wout, woutb, wup, mix, mix_t, wup_t, hidden_w, lam, read_one, read_hidden, read_out = weights
+    below, level, above = widen(level, 1)
+    edges, above = lax.optimization_barrier((edges, above))
+    before, edges, after = widen(edges, 0)
+    edges = (before, edges, after)
+
+    results = [((8, count), F32), ((288, count), BF16), ((256, 128), BF16), ((128, count), BF16),
+               ((384, count), BF16)]
+    e1, seed1, seed2, h1, parts, table, *own = call(
+        functools.partial(own_kernel, box),
+        [((1, 32), F32), ((32, 128), F32), ((32, 16), F32), ((32, 128), BF16), ((4, 56, 96), F32),
+         ((56, 128), F32)] + results,
+        brick, below, level, above, edges[1], emb, t0, win, wout, lam, mix, read_one, read_out,
+        index=True,
+    )
+    h1, *sides = call(
+        functools.partial(sides_kernel, box), [((96, 128), BF16)] + results * 2,
+        edges[0], edges[2], parts, table, h1, emb, t0, win, wout, lam, mix,
+    )
+    per_brick = (sides[:5], own, sides[5:])
+    geo, pool = per_brick[1][:2]
+
+    def direction(brick, found=None):
+        found = per_brick[brick] if found is None else found
+        return call(
+            direction_kernel, [((384, count), BF16)], edges[brick], *found, win, wout,
+            flops=1_000_000_000,
+        )[0]
+
     hidden = call(
         radial_kernel,
         [((864, count), BF16), ((384, count), F32), ((64, count), F32)],
-        edges, geo, win, wout, flops=1_000_000_000,
-    )
-    line, (hotref, rad, slope) = lax.optimization_barrier((line, hidden))
-    plane = jnp.concatenate(widen(line, 1), axis=0)
-    hidden = call(
-        direction_kernel, [((384, count), BF16)], edges, geo, pool, at, lift, base, win, wout,
-        flops=1_000_000_000,
-    )
-    plane, (v,) = lax.optimization_barrier((plane, hidden))
+        edges[1], geo, win, wout, flops=1_000_000_000,
+    )
+    plane = jnp.concatenate(widen(h1, 1), axis=0)
+    plane, (hotref, rad, slope) = lax.optimization_barrier((plane, hidden))
     left, own, right = widen(plane, 2)
+    left, right, v_own = lax.optimization_barrier((left, right, direction(1)))
 
     dleft, down, dright, dh2, e2, drad, base2, da = call(
         second_kernel,
         [((288, 128), BF16), ((288, 128), F32), ((288, 128), BF16), ((32, 128), F32), ((8, 32), F32),
          ((384, count), BF16), ((384, count), BF16), ((288, 128), BF16)],
-        left, own, right, hotref, rad, pool, wup, lam, w_mix, read_hidden, seed2,
-    )
+        left, own, right, hotref, rad, pool, wup, lam, mix, mix_t, hidden_w, read_hidden, seed2,
+    )
+    dh2, before = lax.optimization_barrier((dh2, per_brick[0]))
+    v_before = direction(0, before)
 
     plane = down + move(dleft, shift(2, 1)).astype(F32) + move(dright, shift(2, -1)).astype(F32)
-    line = (
+    plane, v_before, after = lax.optimization_barrier((plane, v_before, per_brick[2]))
+    v_after = direction(2, after)
+    folded = (
         plane[96:192]
         + move(plane[0:96].astype(BF16), shift(1, 1)).astype(F32)
         + move(plane[192:288].astype(BF16), shift(1, -1)).astype(F32)
     )
-    folded = (
-        line[32:64]
-        + move(line[0:32].astype(BF16), shift(0, 1)).astype(F32)
-        + move(line[64:96].astype(BF16), shift(0, -1)).astype(F32)
-    )
 
     (drel2,) = call(
-        slope_kernel, [((8, count), F32)], edges, geo, slope, drad, base2, da, woutb,
+        slope_kernel, [((8, count), F32)], edges[1], geo, slope, drad, base2, da, woutb,
         flops=1_000_000_000,
     )
 
     below, level, above = call(
-        force_kernel, [((9, 128), F32)] * 3,
-        edges, folded, dh2, seed1, e1, e2, wup_t, w_mix, v, drel2,
-        scratch=[pltpu.VMEM((32, 128), F32)],
+        force_kernel, [((15, 128), F32)] * 3,
+        *edges, folded, dh2, seed1, e1, e2, wup_t, mix_t, v_before, v_own, v_after, drel2,
+        scratch=[pltpu.VMEM((48, 128), F32)],
     )
 
     (rows,) = call(
-        spread_kernel, [((SIDE * SIDE, 1, 4 * atoms), F32)],
-        places, level, move(below, shift(1, 1)), move(above, shift(1, -1)), index=True,
+        spread_kernel, [((SIDE * SIDE, 4 * atoms), F32)],
+        brick, level, move(below, shift(1, 1)), move(above, shift(1, -1)), index=True,
     )
     return call(
         last_kernel, [((1, 1, 1, atoms), F32), ((3, 1, 1, 1, atoms), F32)], exchange(rows)

time: 120 us -> 111 us (0.925)
  waiting for transfers between devices: 19.5 us -> 9.75 us
  Pallas kernels: 16.9 us -> 25 us
  blocking collectives: 21 us -> 16.4 us
  starting transfers between devices: 58.8 us -> 56.7 us
    pallas_call x10 -> x13, Pallas kernels: 16.9 us -> 25 us  [call(): pl.pallas_call(kernel, out_shape=tuple((jax.ShapeDtypeStruct(s, d) for s,...]
    all_to_all x1, waiting for transfers between devices: 5.63 us -> 0.01 us  [exchange(): return lax.all_to_all(rows, ('gx', 'gz'), 0, 0, tiled=True).reshape(x.shape)]
    all_to_all x1, blocking collectives: 21 us -> 16.4 us  [exchange(): return lax.all_to_all(rows, ('gx', 'gz'), 0, 0, tiled=True).reshape(x.shape)]
    ppermute x17 -> x15, waiting for transfers between devices: 13.8 us -> 9.74 us  [move(): return lax.ppermute(x, AXES, pairs)]
    ppermute x17 -> x15, starting transfers between devices: 43.9 us -> 41.9 us  [move(): return lax.ppermute(x, AXES, pairs)]
  transfers between devices with their start and end apart: 18 -> 16, of which waited for: 10 -> 4; matrix products, arithmetic and copies ran while one was open for 1% -> 0% of each run, Pallas kernels for 5% -> 12%
where the time goes in v3:
time: 111 us; the launch traced here: 110 us
  starting transfers between devices  56.7 us (51%)
  Pallas kernels  25 us (23%)
  blocking collectives  16.4 us (15%)
  waiting for transfers between devices  9.75 us (9%)
  between operations  2.22 us (2%)
    ppermute x15, starting transfers between devices, move(): return lax.ppermute(x, AXES, pairs)  41.9 us
    pallas_call x13, Pallas kernels, call(): pl.pallas_call(kernel, out_shape=tuple((jax.ShapeDtypeStruct(s, d) for s,...  25 us
    all_to_all x1, blocking collectives, exchange(): return lax.all_to_all(rows, ('gx', 'gz'), 0, 0, tiled=True).reshape(x.shape)  16.4 us
    all_to_all x1, starting transfers between devices, exchange(): return lax.all_to_all(rows, ('gx', 'gz'), 0, 0, tiled=True).reshape(x.shape)  14.8 us
    ppermute x15, waiting for transfers between devices, move(): return lax.ppermute(x, AXES, pairs)  9.74 us
  transfers between devices with their start and end apart: 16, of which 4 were waited for; matrix products, arithmetic and copies ran while one was open for 0% of the time, Pallas kernels for 12%

profile of v3, /device:TPU:1, one launch (start us, length us, event | category | flops | bytes accessed | tf_op | source)
XLA Modules:
  0.0 110.2 jit_solution(15538344975052029286)
XLA Ops:
  1.9 1.5 %shard_map.158 = (f32[64,128]{1,0:T(8,128)}, s32[2,1792]{1,0:T(2,128)S(1)}) custom-call(s32[1,1,1]{2,1,0:T(1,128)S(6)} %copy.19.refs_0_, s32[1,1,1]{2,1,0:T(1,128)S(6)} %copy.20.refs_1_, f32[3,1,1,1,32]{4,3,2,1,0:T(1,128)} %refs_2_.2, s32[1,1,1,32]{3,2,1,0:T(1,128)} %refs_3_.2, s32[1,1,1,1792]{3,2,1,0:T(1,128)} %refs_4_.2, s32[1,1,1,1792]{3,2,1,0:T(1,128)} %refs_5_.2), custom_call_target="tpu_custom_call" | custom-call | flops 1000000 | bytes 1000000 | tf_op jit(solution)/shard_map/pallas_call | solution.py:146
  3.4 14.8 %all-to-all-start = ((f32[64,1,128]{2,1,0:T(1,128)}), f32[64,1,128]{2,1,0:T(1,128)S(1)}, u32[]{:S(2)}, u32[]{:S(2)}) async-start(f32[64,1,128]{2,1,0:T(1,128)} %bitcast.3), calls=%async_computation | async-start | bytes 65536 | tf_op jit(solution)/shard_map/all_to_all | solution.py:55
  18.3 3.5 %collective-permute-start = (s32[2,1792]{1,0:T(2,128)S(1)}, s32[2,1792]{1,0:T(2,128)S(1)}, u32[]{:S(2)}, u32[]{:S(2)}) collective-permute-start(s32[2,1792]{1,0:T(2,128)S(1)} %get-tuple-element.107), channel_id=1, source_target_pairs={{0,0},{1,64},{2,2},{3,66},{4,4},{5,68},{6,6},{7,70},{8,8},{9,72},{... | collective-permute-start | bytes 43016 | tf_op jit(solution)/shard_map/ppermute | solution.py:36
  21.8 1.5 %shard_map.159 = (f32[128,128]{1,0:T(8,128)S(1)}, bf16[128,256]{1,0:T(8,128)(2,1)S(1)}, bf16[2,64,32]{2,1,0:T(8,128)(2,1)S(1)}, bf16[2,384,192]{2,1,0:T(8,128)(2...) custom-call(f32[89,128]{1,0:T(8,128)} %refs_0_.2, ...), custom_call_target="tpu_custom_call" | custom-call | flops 1000000 | bytes 1000000 | tf_op jit(solution)/shard_map/pallas_call | solution.py:146
  23.4 4.1 %collective-permute-done.refs_4_.edges.refs_1_ = s32[2,1792]{1,0:T(2,128)S(1)} collective-permute-done((s32[2,1792]{1,0:T(2,128)S(1)}, s32[2,1792]{1,0:T(2,128)S(1)}, u32[]{:S(2)}, u32[]{:S(2)}) %collective-permute-start) | collective-permute-done | bytes 14368 | tf_op jit(solution)/shard_map/ppermute | solution.py:36
  27.5 0.0 all-to-all-done
  27.5 5.1 %collective-permute-start.1 = (f32[64,128]{1,0:T(8,128)S(1)}, f32[64,128]{1,0:T(8,128)S(1)}, u32[]{:S(2)}, u32[]{:S(2)}) collective-permute-start(f32[64,128]{1,0:T(8,128)S(1)} %bitcast.13), channel_id=1, source_target_pairs={{8,0},{72,64},{10,2},{74,66},{12,4},{76,68},{14,6},{78,70},{16,8},... | collective-permute-start | bytes 98312 | tf_op jit(solution)/shard_map/ppermute | solution.py:36
  32.7 1.9 %collective-permute-start.4 = (f32[64,128]{1,0:T(8,128)S(1)}, f32[64,128]{1,0:T(8,128)S(1)}, u32[]{:S(2)}, u32[]{:S(2)}) collective-permute-start(f32[64,128]{1,0:T(8,128)S(1)} %bitcast.14), channel_id=1, source_target_pairs={{56,0},{120,64},{58,2},{122,66},{60,4},{124,68},{62,6},{126,70},{0... | collective-permute-start | bytes 98312 | tf_op jit(solution)/shard_map/ppermute | solution.py:36
  34.6 0.0 collective-permute-done.1.refs_3_
  34.6 2.5 %collective-permute-start.3 = (s32[2,1792]{1,0:T(2,128)S(1)}, s32[2,1792]{1,0:T(2,128)S(1)}, u32[]{:S(2)}, u32[]{:S(2)}) collective-permute-start(s32[2,1792]{1,0:T(2,128)S(1)} %collective-permute-done.refs_4_.edges.refs_1_), channel_id=1, source_target_pairs={{128,0},{192,64},{130,2},{194,66},{132,4},{196,68},{134,6},{198,70... | collective-permute-start | bytes 43016 | tf_op jit(solution)/shard_map/ppermute | solution.py:36
  37.1 2.8 %collective-permute-start.2 = (s32[2,1792]{1,0:T(2,128)S(1)}, s32[2,1792]{1,0:T(2,128)S(1)}, u32[]{:S(2)}, u32[]{:S(2)}) collective-permute-start(s32[2,1792]{1,0:T(2,128)S(1)} %collective-permute-done.refs_4_.edges.refs_1_), channel_id=1, source_target_pairs={{385,0},{449,64},{387,2},{451,66},{389,4},{453,68},{391,6},{455,70... | collective-permute-start | bytes 43016 | tf_op jit(solution)/shard_map/ppermute | solution.py:36
  39.9 0.1 pad_add_fusion.refs_0_.brick
  40.0 0.0 collective-permute-done.4.refs_1_
  40.0 2.8 %shard_map.160 = (f32[1,32]{1,0:T(1,128)S(1)}, f32[32,128]{1,0:T(8,128)S(1)}, f32[32,16]{1,0:T(8,128)S(1)}, bf16[32,128]{1,0:T(8,128)(2,1)S(1)}, f32[4,56,96]{2,...) custom-call(s32[2]{0:T(128)S(1)} %pad_add_fusion.refs_0_.brick, ...), custom_call_target="tpu_custom_call" | custom-call | flops 1000000 | bytes 1000000 | tf_op jit(solution)/shard_map/pallas_call | solution.py:146
  42.7 0.0 collective-permute-done.3.after.edges.refs_2_
  42.7 0.0 collective-permute-done.2.before.edges.refs_0_
  42.7 3.6 %shard_map.161 = (bf16[96,128]{1,0:T(8,128)(2,1)S(1)}, f32[8,1792]{1,0:T(8,128)S(1)}, bf16[288,1792]{1,0:T(8,128)(2,1)S(1)}, bf16[256,128]{1,0:T(8,128)(2,1)S(1)...) custom-call(s32[2,1792]{1,0:T(2,128)S(1)} %collective-permute-done.2, ...), custom_call_target="tpu_custom_call" | custom-call | flops 1000000 | bytes 1000000 | tf_op jit(solution)/shard_map/pallas_call | solution.py:146
  46.4 4.6 %collective-permute-start.6 = (bf16[96,128]{1,0:T(8,128)(2,1)S(1)}, bf16[96,128]{1,0:T(8,128)(2,1)S(1)}, u32[]{:S(2)}, u32[]{:S(2)}) collective-permute-start(bf16[96,128]{1,0:T(8,128)(2,1)S(1)} %get-tuple-element.123), channel_id=1, source_target_pairs={{8,0},{72,64},{10,2},{74,66},{12,4},{76,68},{14,6},{78,70},{16,8},... | collective-permute-start | bytes 73736 | tf_op jit(solution)/shard_map/ppermute | solution.py:36
  50.9 2.1 %collective-permute-start.5 = (bf16[96,128]{1,0:T(8,128)(2,1)S(1)}, bf16[96,128]{1,0:T(8,128)(2,1)S(1)}, u32[]{:S(2)}, u32[]{:S(2)}) collective-permute-start(bf16[96,128]{1,0:T(8,128)(2,1)S(1)} %get-tuple-element.123), channel_id=1, source_target_pairs={{56,0},{120,64},{58,2},{122,66},{60,4},{124,68},{62,6},{126,70},{0... | collective-permute-start | bytes 73736 | tf_op jit(solution)/shard_map/ppermute | solution.py:36
  53.1 1.5 %shard_map.162 = (bf16[864,1792]{1,0:T(8,128)(2,1)S(1)}, f32[384,1792]{1,0:T(8,128)S(1)}, f32[64,1792]{1,0:T(8,128)S(1)}) custom-call(s32[2,1792]{1,0:T(2,128)S(1)} %collective-permute-done.refs_4_.edges.refs_1_, f32[8,1792]{1,0:T(8,128)S(1)} %get-tuple-element.124.geo, bf16[2,64,32]{2,1,0:T(8,128)(2,1)S(1)} %get-tuple-element.114.refs_7_.refs_2_.win, ...), custom_call_target="tpu_custom_call" | custom-call | flops 1000000000 | bytes 1000000 | tf_op jit(solution)/shard_map/pallas_call | solution.py:146
  54.6 0.0 collective-permute-done.6
  54.6 2.1 %collective-permute-done.5 = bf16[96,128]{1,0:T(8,128)(2,1)S(1)} collective-permute-done((bf16[96,128]{1,0:T(8,128)(2,1)S(1)}, bf16[96,128]{1,0:T(8,128)(2,1)S(1)}, u32[]{:S(2)}, u32[]{:S(2)}) %collective-permute-start.5) | collective-permute-done | bytes 24608 | tf_op jit(solution)/shard_map/ppermute | solution.py:36
  56.7 5.7 %collective-permute-start.8 = (bf16[288,128]{1,0:T(8,128)(2,1)S(1)}, bf16[288,128]{1,0:T(8,128)(2,1)S(1)}, u32[]{:S(2)}, u32[]{:S(2)}) collective-permute-start(bf16[288,128]{1,0:T(8,128)(2,1)S(1)} %pad_maximum_fusion.own), channel_id=1, source_target_pairs={{64,0},{2,64},{66,2},{4,66},{68,4},{6,68},{70,6},{0,70},{72,8},{10... | collective-permute-start | bytes 221192 | tf_op jit(solution)/shard_map/ppermute | solution.py:36
  62.5 1.1 collective-permute-start.7
  63.6 2.1 %shard_map.163.refs_11_ = bf16[384,1792]{1,0:T(8,128)(2,1)S(1)} custom-call(s32[2,1792]{1,0:T(2,128)S(1)} %collective-permute-done.refs_4_.edges.refs_1_, f32[8,1792]{1,0:T(8,128)S(1)} %get-tuple-element.124.geo, bf16[288,1792]{1,0:T(8,128)(2,1)S(1)} %get-tuple-element.129.pool, bf16[256,128]{1,0:T(8,128)(2,1)S(1)} %get-tuple-element.130.at, ...), custom_call_target="tpu_custom_call" | custom-call | flops 1000000000 | bytes 1000000 | tf_op jit(solution)/shard_map/pallas_call | solution.py:146
  65.7 0.0 collective-permute-done.8.right
  65.7 0.0 collective-permute-done.7.left
  65.7 3.6 %shard_map.164 = (bf16[288,128]{1,0:T(8,128)(2,1)S(1)}, f32[288,128]{1,0:T(8,128)S(1)}, bf16[288,128]{1,0:T(8,128)(2,1)S(1)}, f32[32,128]{1,0:T(8,128)S(1)}, f32...) custom-call(bf16[288,128]{1,0:T(8,128)(2,1)S(1)} %collective-permute, ...), custom_call_target="tpu_custom_call" | custom-call | flops 1000000 | bytes 1000000 | tf_op jit(solution)/shard_map/pallas_call | solution.py:146
  69.3 1.8 %collective-permute-start.9 = (bf16[288,128]{1,0:T(8,128)(2,1)S(1)}, bf16[288,128]{1,0:T(8,128)(2,1)S(1)}, u32[]{:S(2)}, u32[]{:S(2)}) collective-permute-start(bf16[288,128]{1,0:T(8,128)(2,1)S(1)} %get-tuple-element.143), channel_id=1, source_target_pairs={{64,0},{2,64},{66,2},{4,66},{68,4},{6,68},{70,6},{0,70},{72,8},{10... | collective-permute-start | bytes 221192 | tf_op jit(solution)/shard_map/ppermute | solution.py:36
  71.1 0.0 collective-permute-start.10
  71.1 0.7 shard_map.167.refs_13_
  71.8 2.1 %shard_map.165.refs_10_ = bf16[384,1792]{1,0:T(8,128)(2,1)S(1)} custom-call(s32[2,1792]{1,0:T(2,128)S(1)} %collective-permute-done.2.before.edges.refs_0_, f32[8,1792]{1,0:T(8,128)S(1)} %get-tuple-element.151.geo, bf16[288,1792]{1,0:T(8,128)(2,1)S(1)} %get-tuple-element.152.pool, bf16[256,128]{1,0:T(8,128)(2,1)S(1)} %get-tuple-element.153.at, ...), custom_call_target="tpu_custom_call" | custom-call | flops 1000000000 | bytes 1000000 | tf_op jit(solution)/shard_map/pallas_call | solution.py:146
  73.9 0.0 collective-permute-done.9
  73.9 0.0 collective-permute-done.10
  74.0 1.9 %collective-permute-start.11 = (bf16[96,128]{1,0:T(8,128)(2,1)S(1)}, bf16[96,128]{1,0:T(8,128)(2,1)S(1)}, u32[]{:S(2)}, u32[]{:S(2)}) collective-permute-start(bf16[96,128]{1,0:T(8,128)(2,1)S(1)} %get-tuple-element.182), channel_id=1, source_target_pairs={{8,0},{72,64},{10,2},{74,66},{12,4},{76,68},{14,6},{78,70},{16,8},... | collective-permute-start | bytes 73736 | tf_op jit(solution)/shard_map/ppermute | solution.py:36
  75.9 3.6 %collective-permute-start.12 = (bf16[96,128]{1,0:T(8,128)(2,1)S(1)}, bf16[96,128]{1,0:T(8,128)(2,1)S(1)}, u32[]{:S(2)}, u32[]{:S(2)}) collective-permute-start(bf16[96,128]{1,0:T(8,128)(2,1)S(1)} %get-tuple-element.183), channel_id=1, source_target_pairs={{56,0},{120,64},{58,2},{122,66},{60,4},{124,68},{62,6},{126,70},{0... | collective-permute-start | bytes 73736 | tf_op jit(solution)/shard_map/ppermute | solution.py:36
  79.5 2.1 %shard_map.166.refs_12_ = bf16[384,1792]{1,0:T(8,128)(2,1)S(1)} custom-call(s32[2,1792]{1,0:T(2,128)S(1)} %collective-permute-done.3.after.edges.refs_2_, f32[8,1792]{1,0:T(8,128)S(1)} %get-tuple-element.169.geo, bf16[288,1792]{1,0:T(8,128)(2,1)S(1)} %get-tuple-element.170.pool, bf16[256,128]{1,0:T(8,128)(2,1)S(1)} %get-tuple-element.171.at, ...), custom_call_target="tpu_custom_call" | custom-call | flops 1000000000 | bytes 1000000 | tf_op jit(solution)/shard_map/pallas_call | solution.py:146
  81.6 0.0 collective-permute-done.11
  81.6 0.1 collective-permute-done.12
  81.7 2.2 %shard_map.168 = (f32[15,128]{1,0:T(8,128)S(1)}, f32[15,128]{1,0:T(8,128)S(1)}, f32[15,128]{1,0:T(8,128)S(1)}) custom-call(s32[2,1792]{1,0:T(2,128)S(1)} %collective-permute-done.2.before.edges.refs_0_, s32[2,1792]{1,0:T(2,128)S(1)} %collective-permute-done.refs_4_.edges.refs_1_, s32[2,1792]{1,0:T(2,128)S(1)} %collective-permute-done.3.after.edges.refs_2_, ...), custom_call_target="tpu_custom_call" | custom-call | flops 1000000 | bytes 1000000 | tf_op jit(solution)/shard_map/pallas_call | solution.py:146
  83.9 3.0 %collective-permute-start.13 = (f32[15,128]{1,0:T(8,128)S(1)}, f32[15,128]{1,0:T(8,128)S(1)}, u32[]{:S(2)}, u32[]{:S(2)}) collective-permute-start(f32[15,128]{1,0:T(8,128)S(1)} %get-tuple-element.180), channel_id=1, source_target_pairs={{8,0},{72,64},{10,2},{74,66},{12,4},{76,68},{14,6},{78,70},{16,8},... | collective-permute-start | bytes 23048 | tf_op jit(solution)/shard_map/ppermute | solution.py:36
  87.0 2.2 %collective-permute-start.14 = (f32[15,128]{1,0:T(8,128)S(1)}, f32[15,128]{1,0:T(8,128)S(1)}, u32[]{:S(2)}, u32[]{:S(2)}) collective-permute-start(f32[15,128]{1,0:T(8,128)S(1)} %get-tuple-element.181), channel_id=1, source_target_pairs={{56,0},{120,64},{58,2},{122,66},{60,4},{124,68},{62,6},{126,70},{0... | collective-permute-start | bytes 23048 | tf_op jit(solution)/shard_map/ppermute | solution.py:36
  89.2 0.0 collective-permute-done.13.b
  89.2 3.3 %collective-permute-done.14.c = f32[15,128]{1,0:T(8,128)S(1)} collective-permute-done((f32[15,128]{1,0:T(8,128)S(1)}, f32[15,128]{1,0:T(8,128)S(1)}, u32[]{:S(2)}, u32[]{:S(2)}) %collective-permute-start.14) | collective-permute-done | bytes 7712 | tf_op jit(solution)/shard_map/ppermute | solution.py:36
  92.6 0.6 shard_map.169
  93.2 16.4 %all_to_all.10 = f32[64,1,128]{2,1,0:T(1,128)S(1)} all-to-all(f32[64,1,128]{2,1,0:T(1,128)S(1)} %bitcast.16), channel_id=1, replica_groups=mesh['gx'=8,'gy'=8,'gz'=8] {'gx','gz'}, dimensions={0} | all-to-all | bytes 65536 | tf_op jit(solution)/shard_map/all_to_all | solution.py:55
  109.6 0.6 shard_map.170
  (5 shorter events, 0.1 us)
Async XLA Ops:
  3.4 24.1 %all-to-all-start = ((f32[64,1,128]{2,1,0:T(1,128)}), f32[64,1,128]{2,1,0:T(1,128)S(1)}, u32[]{:S(2)}, u32[]{:S(2)}) async-start(f32[64,1,128]{2,1,0:T(1,128)} %bitcast.3), calls=%async_computation | async-start | bytes 65536 | tf_op jit(solution)/shard_map/all_to_all | solution.py:55
  18.3 9.2 %collective-permute-start = (s32[2,1792]{1,0:T(2,128)S(1)}, s32[2,1792]{1,0:T(2,128)S(1)}, u32[]{:S(2)}, u32[]{:S(2)}) collective-permute-start(s32[2,1792]{1,0:T(2,128)S(1)} %get-tuple-element.107), channel_id=1, source_target_pairs={{0,0},{1,64},{2,2},{3,66},{4,4},{5,68},{6,6},{7,70},{8,8},{9,72},{... | collective-permute-start | bytes 43016 | tf_op jit(solution)/shard_map/ppermute | solution.py:36
  27.5 7.1 %collective-permute-start.1 = (f32[64,128]{1,0:T(8,128)S(1)}, f32[64,128]{1,0:T(8,128)S(1)}, u32[]{:S(2)}, u32[]{:S(2)}) collective-permute-start(f32[64,128]{1,0:T(8,128)S(1)} %bitcast.13), channel_id=1, source_target_pairs={{8,0},{72,64},{10,2},{74,66},{12,4},{76,68},{14,6},{78,70},{16,8},... | collective-permute-start | bytes 98312 | tf_op jit(solution)/shard_map/ppermute | solution.py:36
  32.7 7.3 %collective-permute-start.4 = (f32[64,128]{1,0:T(8,128)S(1)}, f32[64,128]{1,0:T(8,128)S(1)}, u32[]{:S(2)}, u32[]{:S(2)}) collective-permute-start(f32[64,128]{1,0:T(8,128)S(1)} %bitcast.14), channel_id=1, source_target_pairs={{56,0},{120,64},{58,2},{122,66},{60,4},{124,68},{62,6},{126,70},{0... | collective-permute-start | bytes 98312 | tf_op jit(solution)/shard_map/ppermute | solution.py:36
  34.6 8.1 %collective-permute-start.3 = (s32[2,1792]{1,0:T(2,128)S(1)}, s32[2,1792]{1,0:T(2,128)S(1)}, u32[]{:S(2)}, u32[]{:S(2)}) collective-permute-start(s32[2,1792]{1,0:T(2,128)S(1)} %collective-permute-done.refs_4_.edges.refs_1_), channel_id=1, source_target_pairs={{128,0},{192,64},{130,2},{194,66},{132,4},{196,68},{134,6},{198,70... | collective-permute-start | bytes 43016 | tf_op jit(solution)/shard_map/ppermute | solution.py:36
  37.1 5.7 %collective-permute-start.2 = (s32[2,1792]{1,0:T(2,128)S(1)}, s32[2,1792]{1,0:T(2,128)S(1)}, u32[]{:S(2)}, u32[]{:S(2)}) collective-permute-start(s32[2,1792]{1,0:T(2,128)S(1)} %collective-permute-done.refs_4_.edges.refs_1_), channel_id=1, source_target_pairs={{385,0},{449,64},{387,2},{451,66},{389,4},{453,68},{391,6},{455,70... | collective-permute-start | bytes 43016 | tf_op jit(solution)/shard_map/ppermute | solution.py:36
  46.4 8.2 %collective-permute-start.6 = (bf16[96,128]{1,0:T(8,128)(2,1)S(1)}, bf16[96,128]{1,0:T(8,128)(2,1)S(1)}, u32[]{:S(2)}, u32[]{:S(2)}) collective-permute-start(bf16[96,128]{1,0:T(8,128)(2,1)S(1)} %get-tuple-element.123), channel_id=1, source_target_pairs={{8,0},{72,64},{10,2},{74,66},{12,4},{76,68},{14,6},{78,70},{16,8},... | collective-permute-start | bytes 73736 | tf_op jit(solution)/shard_map/ppermute | solution.py:36
  50.9 5.8 %collective-permute-start.5 = (bf16[96,128]{1,0:T(8,128)(2,1)S(1)}, bf16[96,128]{1,0:T(8,128)(2,1)S(1)}, u32[]{:S(2)}, u32[]{:S(2)}) collective-permute-start(bf16[96,128]{1,0:T(8,128)(2,1)S(1)} %get-tuple-element.123), channel_id=1, source_target_pairs={{56,0},{120,64},{58,2},{122,66},{60,4},{124,68},{62,6},{126,70},{0... | collective-permute-start | bytes 73736 | tf_op jit(solution)/shard_map/ppermute | solution.py:36
  56.7 8.9 %collective-permute-start.8 = (bf16[288,128]{1,0:T(8,128)(2,1)S(1)}, bf16[288,128]{1,0:T(8,128)(2,1)S(1)}, u32[]{:S(2)}, u32[]{:S(2)}) collective-permute-start(bf16[288,128]{1,0:T(8,128)(2,1)S(1)} %pad_maximum_fusion.own), channel_id=1, source_target_pairs={{64,0},{2,64},{66,2},{4,66},{68,4},{6,68},{70,6},{0,70},{72,8},{10... | collective-permute-start | bytes 221192 | tf_op jit(solution)/shard_map/ppermute | solution.py:36
  62.5 3.2 %collective-permute-start.7 = (bf16[288,128]{1,0:T(8,128)(2,1)S(1)}, bf16[288,128]{1,0:T(8,128)(2,1)S(1)}, u32[]{:S(2)}, u32[]{:S(2)}) collective-permute-start(bf16[288,128]{1,0:T(8,128)(2,1)S(1)} %pad_maximum_fusion.own), channel_id=1, source_target_pairs={{70,0},{0,64},{64,2},{2,66},{66,4},{4,68},{68,6},{6,70},{78,8},{8,... | collective-permute-start | bytes 221192 | tf_op jit(solution)/shard_map/ppermute | solution.py:36
  69.3 4.6 %collective-permute-start.9 = (bf16[288,128]{1,0:T(8,128)(2,1)S(1)}, bf16[288,128]{1,0:T(8,128)(2,1)S(1)}, u32[]{:S(2)}, u32[]{:S(2)}) collective-permute-start(bf16[288,128]{1,0:T(8,128)(2,1)S(1)} %get-tuple-element.143), channel_id=1, source_target_pairs={{64,0},{2,64},{66,2},{4,66},{68,4},{6,68},{70,6},{0,70},{72,8},{10... | collective-permute-start | bytes 221192 | tf_op jit(solution)/shard_map/ppermute | solution.py:36
  71.1 2.8 %collective-permute-start.10 = (bf16[288,128]{1,0:T(8,128)(2,1)S(1)}, bf16[288,128]{1,0:T(8,128)(2,1)S(1)}, u32[]{:S(2)}, u32[]{:S(2)}) collective-permute-start(bf16[288,128]{1,0:T(8,128)(2,1)S(1)} %get-tuple-element.144), channel_id=1, source_target_pairs={{70,0},{0,64},{64,2},{2,66},{66,4},{4,68},{68,6},{6,70},{78,8},{8,... | collective-permute-start | bytes 221192 | tf_op jit(solution)/shard_map/ppermute | solution.py:36
  74.0 7.6 %collective-permute-start.11 = (bf16[96,128]{1,0:T(8,128)(2,1)S(1)}, bf16[96,128]{1,0:T(8,128)(2,1)S(1)}, u32[]{:S(2)}, u32[]{:S(2)}) collective-permute-start(bf16[96,128]{1,0:T(8,128)(2,1)S(1)} %get-tuple-element.182), channel_id=1, source_target_pairs={{8,0},{72,64},{10,2},{74,66},{12,4},{76,68},{14,6},{78,70},{16,8},... | collective-permute-start | bytes 73736 | tf_op jit(solution)/shard_map/ppermute | solution.py:36
  75.9 5.8 %collective-permute-start.12 = (bf16[96,128]{1,0:T(8,128)(2,1)S(1)}, bf16[96,128]{1,0:T(8,128)(2,1)S(1)}, u32[]{:S(2)}, u32[]{:S(2)}) collective-permute-start(bf16[96,128]{1,0:T(8,128)(2,1)S(1)} %get-tuple-element.183), channel_id=1, source_target_pairs={{56,0},{120,64},{58,2},{122,66},{60,4},{124,68},{62,6},{126,70},{0... | collective-permute-start | bytes 73736 | tf_op jit(solution)/shard_map/ppermute | solution.py:36
  83.9 5.3 %collective-permute-start.13 = (f32[15,128]{1,0:T(8,128)S(1)}, f32[15,128]{1,0:T(8,128)S(1)}, u32[]{:S(2)}, u32[]{:S(2)}) collective-permute-start(f32[15,128]{1,0:T(8,128)S(1)} %get-tuple-element.180), channel_id=1, source_target_pairs={{8,0},{72,64},{10,2},{74,66},{12,4},{76,68},{14,6},{78,70},{16,8},... | collective-permute-start | bytes 23048 | tf_op jit(solution)/shard_map/ppermute | solution.py:36
  87.0 5.6 %collective-permute-start.14 = (f32[15,128]{1,0:T(8,128)S(1)}, f32[15,128]{1,0:T(8,128)S(1)}, u32[]{:S(2)}, u32[]{:S(2)}) collective-permute-start(f32[15,128]{1,0:T(8,128)S(1)} %get-tuple-element.181), channel_id=1, source_target_pairs={{56,0},{120,64},{58,2},{122,66},{60,4},{124,68},{62,6},{126,70},{0... | collective-permute-start | bytes 23048 | tf_op jit(solution)/shard_map/ppermute | solution.py:36

commit v4 on v3

--- a/solution.py
+++ b/solution.py
@@ -40,14 +40,14 @@
     return [(place(a, b, d), home(a, b, d)) for a, b, d in bricks()]
 
 
-def here():
+def around():
     gx, gz = lax.axis_index("gx"), lax.axis_index("gz")
-    return jnp.stack([(gz % 2) * 4 + gx // 2, (gz // 2) * 2 + gx % 2])
-
-
-def around(brick, k):
-    a, d = brick[0] + (k // 3 - 2 + SIDE), brick[1] + (k % 3 - 1 + SIDE)
-    return jnp.bitwise_and(a, SIDE - 1) * SIDE + jnp.bitwise_and(d, SIDE - 1)
+    a, d = (gz % 2) * 4 + gx // 2, (gz // 2) * 2 + gx % 2
+    k = lax.broadcasted_iota(jnp.int32, (16, SIDE * SIDE), 0)
+    at = lax.broadcasted_iota(jnp.int32, (16, SIDE * SIDE), 1)
+    i = k // 3
+    place_k = ((a + i + SIDE - 2) % SIDE) * SIDE + (d + k - 3 * i + SIDE - 1) % SIDE
+    return jnp.where((place_k == at) & (k < 15), 1.0, 0.0).astype(F32)
 
 
 def exchange(x):
@@ -129,12 +129,8 @@
     return act * env, dact * env + act * denv
 
 
-def call(kernel, outs, *args, flops=1_000_000, limit=16, scratch=(), far=False, index=False):
+def call(kernel, outs, *args, flops=1_000_000, limit=16, scratch=(), far=False):
     params = {}
-    if index:
-        params["in_specs"] = [pl.BlockSpec(memory_space=pltpu.SMEM)] + [
-            pl.BlockSpec(memory_space=pltpu.VMEM)
-        ] * (len(args) - 1)
     if far:
         spaces = [pltpu.SMEM if a.size == 1 else pltpu.HBM for a in args]
         args = [
@@ -214,15 +210,13 @@
 
 
 def own_kernel(box, *refs):
-    (brick, below, level, above, edges), weights = refs[:5], refs[5:13]
-    (e1_o, seed1_o, seed2_o, h1_o, parts, table), results = refs[13:19], refs[19:24]
-    read_one, read_out = weights[6:]
+    (chosen, below, level, above, edges), weights = refs[:5], refs[5:11]
+    (mask_o, full_o, h1_o, parts, table), results = refs[11:16], refs[16:21]
     table[...] = jnp.zeros_like(table)
-    for k in range(15):
-        at = pl.ds(around(brick, k), 1)
-        for dy, plane in enumerate((below, level, above)):
-            row = k // 3 * 9 + dy * 3 + k % 3
-            table[row : row + 1] = plane[at]
+    for dy, plane in enumerate((below, level, above)):
+        near = nn(chosen[...], plane[...], precision=HIGH)
+        for i in range(5):
+            table[9 * i + 3 * dy : 9 * i + 3 * dy + 3] = near[3 * i : 3 * i + 3]
     rows = table[...]
     hi = rows.astype(BF16).astype(F32)
     rest = rows - hi
@@ -230,14 +224,10 @@
     low = rest - mid
     for c in range(4):
         parts[c] = jnp.concatenate([p[:, 32 * c : 32 * c + 32] for p in (hi, mid, low)], axis=1)
-    h1, mask = first_layer(box, 9, edges, *weights[:6], *results, table, parts)
+    h1, mask = first_layer(box, 9, edges, *weights, *results, table, parts)
     h1_o[...] = h1.astype(BF16)
-    e1_o[...] = nt(read_one[...], h1, precision=HIGH) * mask
-    mask8 = jnp.concatenate([mask, jnp.zeros((7, 32), F32)], axis=0)
-    zero = lax.broadcasted_iota(jnp.int32, (8, 128), 0) == 0
-    seed1_o[...] = tn(mask8, jnp.where(zero, read_one[...], 0.0), precision=HIGH)
-    zero = lax.broadcasted_iota(jnp.int32, (8, 16), 0) == 0
-    seed2_o[...] = tn(mask8, jnp.where(zero, read_out[...], 0.0), precision=HIGH)
+    full_o[...] = h1
+    mask_o[...] = mask
 
 
 def sides_kernel(box, before, after, parts, table, h1, *refs):
@@ -319,7 +309,9 @@
     return h0 + product3(product, mix[0]), mask
 
 
-def radial_kernel(edges, geo, win, wout, hot_o, rad_o, slope_o):
+def radial_kernel(
+    edges, geo, win, wout, mask, h1, read_one, read_out, hot_o, rad_o, slope_o, e1_o, seed1_o, seed2_o
+):
     s = edges[0:1]
     block, slot = jnp.right_shift(s, 5), jnp.bitwise_and(s, 31)
     one = lambda flag: jnp.where(flag, 1, 0)
@@ -335,6 +327,12 @@
     hidden, slope = hidden_units(geo[3:4], geo[4:5], geo[5:6], win[1])
     rad_o[...] = nn(wout[1], stack3(hidden))
     slope_o[...] = slope
+    e1_o[...] = nt(read_one[...], h1[...], precision=HIGH) * mask[...]
+    mask8 = jnp.concatenate([mask[...], jnp.zeros((7, 32), F32)], axis=0)
+    zero = lax.broadcasted_iota(jnp.int32, (8, 128), 0) == 0
+    seed1_o[...] = tn(mask8, jnp.where(zero, read_one[...], 0.0), precision=HIGH)
+    zero = lax.broadcasted_iota(jnp.int32, (8, 16), 0) == 0
+    seed2_o[...] = tn(mask8, jnp.where(zero, read_out[...], 0.0), precision=HIGH)
 
 
 def direction_kernel(edges, geo, pool, at, lift, base, win, wout, v_o):
@@ -475,13 +473,12 @@
     for dx in range(5):
         for dy, out in enumerate(outs):
             out[3 * dx : 3 * dx + 3] = rows[9 * dx + 3 * dy : 9 * dx + 3 * dy + 3]
-
-
-def spread_kernel(brick, a, b, c, out):
-    out[...] = jnp.zeros_like(out)
-    total = a[...] + b[...] + c[...]
-    for k in range(15):
-        out[pl.ds(around(brick, k), 1)] = total[k : k + 1]
+    for out in outs:
+        out[15:16] = jnp.zeros((1, 128), F32)
+
+
+def spread_kernel(chosen, a, b, c, out):
+    out[...] = tn(chosen[...], a[...] + b[...] + c[...], precision=HIGH)
 
 
 def last_kernel(rows, energy_o, forces_o):
@@ -500,7 +497,7 @@
     count = sender.shape[-1]
     box = (SIDE * 4 * lattice_step, SIDE * 4 * lattice_step, SIDE * (atoms // 16) * lattice_step)
 
-    brick = here()
+    chosen = around()
     rows, edges = call(
         pack_kernel, [((SIDE * SIDE, 4 * atoms), F32), ((2, count), jnp.int32)],
         atom_count, edge_count, positions, species, sender, receiver, far=True,
@@ -526,12 +523,11 @@
 
     results = [((8, count), F32), ((288, count), BF16), ((256, 128), BF16), ((128, count), BF16),
                ((384, count), BF16)]
-    e1, seed1, seed2, h1, parts, table, *own = call(
+    mask, h1_full, h1, parts, table, *own = call(
         functools.partial(own_kernel, box),
-        [((1, 32), F32), ((32, 128), F32), ((32, 16), F32), ((32, 128), BF16), ((4, 56, 96), F32),
-         ((56, 128), F32)] + results,
-        brick, below, level, above, edges[1], emb, t0, win, wout, lam, mix, read_one, read_out,
-        index=True,
+        [((1, 32), F32), ((32, 128), F32), ((32, 128), BF16), ((4, 56, 96), F32), ((56, 128), F32)]
+        + results,
+        chosen, below, level, above, edges[1], emb, t0, win, wout, lam, mix,
     )
     h1, *sides = call(
         functools.partial(sides_kernel, box), [((96, 128), BF16)] + results * 2,
@@ -549,11 +545,12 @@
 
     hidden = call(
         radial_kernel,
-        [((864, count), BF16), ((384, count), F32), ((64, count), F32)],
-        edges[1], geo, win, wout, flops=1_000_000_000,
+        [((864, count), BF16), ((384, count), F32), ((64, count), F32), ((1, 32), F32), ((32, 128), F32),
+         ((32, 16), F32)],
+        edges[1], geo, win, wout, mask, h1_full, read_one, read_out, flops=1_000_000_000,
     )
     plane = jnp.concatenate(widen(h1, 1), axis=0)
-    plane, (hotref, rad, slope) = lax.optimization_barrier((plane, hidden))
+    plane, (hotref, rad, slope, e1, seed1, seed2) = lax.optimization_barrier((plane, hidden))
     left, own, right = widen(plane, 2)
     left, right, v_own = lax.optimization_barrier((left, right, direction(1)))
 
@@ -581,14 +578,14 @@
     )
 
     below, level, above = call(
-        force_kernel, [((15, 128), F32)] * 3,
+        force_kernel, [((16, 128), F32)] * 3,
         *edges, folded, dh2, seed1, e1, e2, wup_t, mix_t, v_before, v_own, v_after, drel2,
         scratch=[pltpu.VMEM((48, 128), F32)],
     )
 
     (rows,) = call(
         spread_kernel, [((SIDE * SIDE, 4 * atoms), F32)],
-        brick, level, move(below, shift(1, 1)), move(above, shift(1, -1)), index=True,
+        chosen, level, move(below, shift(1, 1)), move(above, shift(1, -1)),
     )
     return call(
         last_kernel, [((1, 1, 1, atoms), F32), ((3, 1, 1, 1, atoms), F32)], exchange(rows)

time: 111 us -> 110 us (level)
  transfers between devices with their start and end apart: 16 -> 16, of which waited for: 4 -> 5; matrix products, arithmetic and copies ran while one was open for 0% -> 0% of each run, Pallas kernels for 12% -> 11%
where the time goes in v4:
time: 110 us
  starting transfers between devices  56.8 us (52%)
  Pallas kernels  24.2 us (22%)
  blocking collectives  16.5 us (15%)
  waiting for transfers between devices  10.1 us (9%)
  between operations  2.27 us (2%)
    ppermute x15, starting transfers between devices, move(): return lax.ppermute(x, AXES, pairs)  41.9 us
    pallas_call x13, Pallas kernels, call(): pl.pallas_call(kernel, out_shape=tuple((jax.ShapeDtypeStruct(s, d) for s,...  24.2 us
    all_to_all x1, blocking collectives, exchange(): return lax.all_to_all(rows, ('gx', 'gz'), 0, 0, tiled=True).reshape(x.shape)  16.5 us
    all_to_all x1, starting transfers between devices, exchange(): return lax.all_to_all(rows, ('gx', 'gz'), 0, 0, tiled=True).reshape(x.shape)  14.8 us
    ppermute x15, waiting for transfers between devices, move(): return lax.ppermute(x, AXES, pairs)  10.1 us
  transfers between devices with their start and end apart: 16, of which 5 were waited for; matrix products, arithmetic and copies ran while one was open for 0% of the time, Pallas kernels for 11%

profile of v4, /device:TPU:1, one launch (start us, length us, event | category | flops | bytes accessed | tf_op | source)
XLA Modules:
  0.0 109.9 jit_solution(4620103819783428861)
XLA Ops:
  1.9 1.5 %shard_map.158 = (f32[64,128]{1,0:T(8,128)}, s32[2,1792]{1,0:T(2,128)S(1)}) custom-call(s32[1,1,1]{2,1,0:T(1,128)S(6)} %copy.19.refs_0_, s32[1,1,1]{2,1,0:T(1,128)S(6)} %copy.20.refs_1_, f32[3,1,1,1,32]{4,3,2,1,0:T(1,128)} %refs_2_.2, s32[1,1,1,32]{3,2,1,0:T(1,128)} %refs_3_.2, s32[1,1,1,1792]{3,2,1,0:T(1,128)} %refs_4_.2, s32[1,1,1,1792]{3,2,1,0:T(1,128)} %refs_5_.2), custom_call_target="tpu_custom_call" | custom-call | flops 1000000 | bytes 1000000 | tf_op jit(solution)/shard_map/pallas_call | solution.py:142
  3.4 14.8 %all-to-all-start = ((f32[64,1,128]{2,1,0:T(1,128)}), f32[64,1,128]{2,1,0:T(1,128)S(1)}, u32[]{:S(2)}, u32[]{:S(2)}) async-start(f32[64,1,128]{2,1,0:T(1,128)} %bitcast.1), calls=%async_computation | async-start | bytes 65536 | tf_op jit(solution)/shard_map/all_to_all | solution.py:55
  18.3 3.5 %collective-permute-start = (s32[2,1792]{1,0:T(2,128)S(1)}, s32[2,1792]{1,0:T(2,128)S(1)}, u32[]{:S(2)}, u32[]{:S(2)}) collective-permute-start(s32[2,1792]{1,0:T(2,128)S(1)} %get-tuple-element.112), channel_id=1, source_target_pairs={{0,0},{1,64},{2,2},{3,66},{4,4},{5,68},{6,6},{7,70},{8,8},{9,72},{... | collective-permute-start | bytes 43016 | tf_op jit(solution)/shard_map/ppermute | solution.py:36
  21.9 1.5 %shard_map.159 = (f32[128,128]{1,0:T(8,128)S(1)}, bf16[128,256]{1,0:T(8,128)(2,1)S(1)}, bf16[2,64,32]{2,1,0:T(8,128)(2,1)S(1)}, bf16[2,384,192]{2,1,0:T(8,128)(2...) custom-call(f32[89,128]{1,0:T(8,128)} %refs_0_.2, ...), custom_call_target="tpu_custom_call" | custom-call | flops 1000000 | bytes 1000000 | tf_op jit(solution)/shard_map/pallas_call | solution.py:142
  23.5 4.1 %collective-permute-done.refs_4_.edges.refs_1_ = s32[2,1792]{1,0:T(2,128)S(1)} collective-permute-done((s32[2,1792]{1,0:T(2,128)S(1)}, s32[2,1792]{1,0:T(2,128)S(1)}, u32[]{:S(2)}, u32[]{:S(2)}) %collective-permute-start) | collective-permute-done | bytes 14368 | tf_op jit(solution)/shard_map/ppermute | solution.py:36
  27.5 0.0 all-to-all-done
  27.5 5.1 %collective-permute-start.1 = (f32[64,128]{1,0:T(8,128)S(1)}, f32[64,128]{1,0:T(8,128)S(1)}, u32[]{:S(2)}, u32[]{:S(2)}) collective-permute-start(f32[64,128]{1,0:T(8,128)S(1)} %bitcast.13), channel_id=1, source_target_pairs={{8,0},{72,64},{10,2},{74,66},{12,4},{76,68},{14,6},{78,70},{16,8},... | collective-permute-start | bytes 98312 | tf_op jit(solution)/shard_map/ppermute | solution.py:36
  32.6 1.9 %collective-permute-start.4 = (f32[64,128]{1,0:T(8,128)S(1)}, f32[64,128]{1,0:T(8,128)S(1)}, u32[]{:S(2)}, u32[]{:S(2)}) collective-permute-start(f32[64,128]{1,0:T(8,128)S(1)} %bitcast.14), channel_id=1, source_target_pairs={{56,0},{120,64},{58,2},{122,66},{60,4},{124,68},{62,6},{126,70},{0... | collective-permute-start | bytes 98312 | tf_op jit(solution)/shard_map/ppermute | solution.py:36
  34.6 0.0 collective-permute-done.1.refs_3_
  34.6 2.5 %collective-permute-start.3 = (s32[2,1792]{1,0:T(2,128)S(1)}, s32[2,1792]{1,0:T(2,128)S(1)}, u32[]{:S(2)}, u32[]{:S(2)}) collective-permute-start(s32[2,1792]{1,0:T(2,128)S(1)} %collective-permute-done.refs_4_.edges.refs_1_), channel_id=1, source_target_pairs={{128,0},{192,64},{130,2},{194,66},{132,4},{196,68},{134,6},{198,70... | collective-permute-start | bytes 43016 | tf_op jit(solution)/shard_map/ppermute | solution.py:36
  37.1 2.8 %collective-permute-start.2 = (s32[2,1792]{1,0:T(2,128)S(1)}, s32[2,1792]{1,0:T(2,128)S(1)}, u32[]{:S(2)}, u32[]{:S(2)}) collective-permute-start(s32[2,1792]{1,0:T(2,128)S(1)} %collective-permute-done.refs_4_.edges.refs_1_), channel_id=1, source_target_pairs={{385,0},{449,64},{387,2},{451,66},{389,4},{453,68},{391,6},{455,70... | collective-permute-start | bytes 43016 | tf_op jit(solution)/shard_map/ppermute | solution.py:36
  39.9 0.1 and_select_fusion.refs_0_.chosen
  40.0 0.0 collective-permute-done.4.refs_1_
  40.0 2.3 %shard_map.160 = (f32[1,32]{1,0:T(1,128)S(1)}, f32[32,128]{1,0:T(8,128)S(1)}, bf16[32,128]{1,0:T(8,128)(2,1)S(1)}, f32[4,56,96]{2,1,0:T(8,128)S(1)}, f32[56,128]...) custom-call(f32[16,64]{1,0:T(8,128)S(1)} %and_select_fusion.refs_0_., ...), custom_call_target="tpu_custom_call" | custom-call | flops 1000000 | bytes 1000000 | tf_op jit(solution)/shard_map/pallas_call | solution.py:142
  42.3 0.0 collective-permute-done.3.after.edges.refs_2_
  42.3 0.5 collective-permute-done.2.before.edges.refs_0_
  42.7 3.6 %shard_map.161 = (bf16[96,128]{1,0:T(8,128)(2,1)S(1)}, f32[8,1792]{1,0:T(8,128)S(1)}, bf16[288,1792]{1,0:T(8,128)(2,1)S(1)}, bf16[256,128]{1,0:T(8,128)(2,1)S(1)...) custom-call(s32[2,1792]{1,0:T(2,128)S(1)} %collective-permute-done.2, ...), custom_call_target="tpu_custom_call" | custom-call | flops 1000000 | bytes 1000000 | tf_op jit(solution)/shard_map/pallas_call | solution.py:142
  46.3 4.6 %collective-permute-start.6 = (bf16[96,128]{1,0:T(8,128)(2,1)S(1)}, bf16[96,128]{1,0:T(8,128)(2,1)S(1)}, u32[]{:S(2)}, u32[]{:S(2)}) collective-permute-start(bf16[96,128]{1,0:T(8,128)(2,1)S(1)} %get-tuple-element.126), channel_id=1, source_target_pairs={{8,0},{72,64},{10,2},{74,66},{12,4},{76,68},{14,6},{78,70},{16,8},... | collective-permute-start | bytes 73736 | tf_op jit(solution)/shard_map/ppermute | solution.py:36
  50.9 2.1 %collective-permute-start.5 = (bf16[96,128]{1,0:T(8,128)(2,1)S(1)}, bf16[96,128]{1,0:T(8,128)(2,1)S(1)}, u32[]{:S(2)}, u32[]{:S(2)}) collective-permute-start(bf16[96,128]{1,0:T(8,128)(2,1)S(1)} %get-tuple-element.126), channel_id=1, source_target_pairs={{56,0},{120,64},{58,2},{122,66},{60,4},{124,68},{62,6},{126,70},{0... | collective-permute-start | bytes 73736 | tf_op jit(solution)/shard_map/ppermute | solution.py:36
  53.0 1.6 %shard_map.162 = (bf16[864,1792]{1,0:T(8,128)(2,1)S(1)}, f32[384,1792]{1,0:T(8,128)S(1)}, f32[64,1792]{1,0:T(8,128)S(1)}, f32[1,32]{1,0:T(1,128)S(1)}, f32[32,128]{1,0:T(8,128)S(1)}, /*index=5*/f32[32,16]{1,0:T(8,128)S(1)}) custom-call(s32[2,1792]{1,0:T(2,128)S(1)} %collective-permute-done.refs_4_.edges.refs_1_, f32[8,1792]{1,0:T(8,128)S(1)} %get-tuple-element.127.geo, ...), custom_call_target="tpu_custom_call" | custom-call | flops 1000000000 | bytes 1000000 | tf_op jit(solution)/shard_map/pallas_call | solution.py:142
  54.7 0.0 collective-permute-done.6
  54.7 2.1 %collective-permute-done.5 = bf16[96,128]{1,0:T(8,128)(2,1)S(1)} collective-permute-done((bf16[96,128]{1,0:T(8,128)(2,1)S(1)}, bf16[96,128]{1,0:T(8,128)(2,1)S(1)}, u32[]{:S(2)}, u32[]{:S(2)}) %collective-permute-start.5) | collective-permute-done | bytes 24608 | tf_op jit(solution)/shard_map/ppermute | solution.py:36
  56.7 5.7 %collective-permute-start.8 = (bf16[288,128]{1,0:T(8,128)(2,1)S(1)}, bf16[288,128]{1,0:T(8,128)(2,1)S(1)}, u32[]{:S(2)}, u32[]{:S(2)}) collective-permute-start(bf16[288,128]{1,0:T(8,128)(2,1)S(1)} %pad_maximum_fusion.own), channel_id=1, source_target_pairs={{64,0},{2,64},{66,2},{4,66},{68,4},{6,68},{70,6},{0,70},{72,8},{10... | collective-permute-start | bytes 221192 | tf_op jit(solution)/shard_map/ppermute | solution.py:36
  62.4 1.1 %collective-permute-start.7 = (bf16[288,128]{1,0:T(8,128)(2,1)S(1)}, bf16[288,128]{1,0:T(8,128)(2,1)S(1)}, u32[]{:S(2)}, u32[]{:S(2)}) collective-permute-start(bf16[288,128]{1,0:T(8,128)(2,1)S(1)} %pad_maximum_fusion.own), channel_id=1, source_target_pairs={{70,0},{0,64},{64,2},{2,66},{66,4},{4,68},{68,6},{6,70},{78,8},{8,... | collective-permute-start | bytes 221192 | tf_op jit(solution)/shard_map/ppermute | solution.py:36
  63.5 2.1 %shard_map.163.refs_11_ = bf16[384,1792]{1,0:T(8,128)(2,1)S(1)} custom-call(s32[2,1792]{1,0:T(2,128)S(1)} %collective-permute-done.refs_4_.edges.refs_1_, f32[8,1792]{1,0:T(8,128)S(1)} %get-tuple-element.127.geo, bf16[288,1792]{1,0:T(8,128)(2,1)S(1)} %get-tuple-element.139.pool, bf16[256,128]{1,0:T(8,128)(2,1)S(1)} %get-tuple-element.140.at, ...), custom_call_target="tpu_custom_call" | custom-call | flops 1000000000 | bytes 1000000 | tf_op jit(solution)/shard_map/pallas_call | solution.py:142
  65.7 0.0 collective-permute-done.8.right
  65.7 0.0 collective-permute-done.7.left
  65.7 3.6 %shard_map.164 = (bf16[288,128]{1,0:T(8,128)(2,1)S(1)}, f32[288,128]{1,0:T(8,128)S(1)}, bf16[288,128]{1,0:T(8,128)(2,1)S(1)}, f32[32,128]{1,0:T(8,128)S(1)}, f32...) custom-call(bf16[288,128]{1,0:T(8,128)(2,1)S(1)} %collective-permute, ...), custom_call_target="tpu_custom_call" | custom-call | flops 1000000 | bytes 1000000 | tf_op jit(solution)/shard_map/pallas_call | solution.py:142
  69.3 1.8 %collective-permute-start.9 = (bf16[288,128]{1,0:T(8,128)(2,1)S(1)}, bf16[288,128]{1,0:T(8,128)(2,1)S(1)}, u32[]{:S(2)}, u32[]{:S(2)}) collective-permute-start(bf16[288,128]{1,0:T(8,128)(2,1)S(1)} %get-tuple-element.153), channel_id=1, source_target_pairs={{64,0},{2,64},{66,2},{4,66},{68,4},{6,68},{70,6},{0,70},{72,8},{10... | collective-permute-start | bytes 221192 | tf_op jit(solution)/shard_map/ppermute | solution.py:36
  71.1 0.0 collective-permute-start.10
  71.1 0.7 shard_map.167.refs_13_
  71.8 2.1 %shard_map.165.refs_10_ = bf16[384,1792]{1,0:T(8,128)(2,1)S(1)} custom-call(s32[2,1792]{1,0:T(2,128)S(1)} %collective-permute-done.2.before.edges.refs_0_, f32[8,1792]{1,0:T(8,128)S(1)} %get-tuple-element.161.geo, bf16[288,1792]{1,0:T(8,128)(2,1)S(1)} %get-tuple-element.162.pool, bf16[256,128]{1,0:T(8,128)(2,1)S(1)} %get-tuple-element.163.at, ...), custom_call_target="tpu_custom_call" | custom-call | flops 1000000000 | bytes 1000000 | tf_op jit(solution)/shard_map/pallas_call | solution.py:142
  73.9 0.0 collective-permute-done.9
  73.9 0.0 collective-permute-done.10
  74.0 1.9 %collective-permute-start.11 = (bf16[96,128]{1,0:T(8,128)(2,1)S(1)}, bf16[96,128]{1,0:T(8,128)(2,1)S(1)}, u32[]{:S(2)}, u32[]{:S(2)}) collective-permute-start(bf16[96,128]{1,0:T(8,128)(2,1)S(1)} %get-tuple-element.192), channel_id=1, source_target_pairs={{8,0},{72,64},{10,2},{74,66},{12,4},{76,68},{14,6},{78,70},{16,8},... | collective-permute-start | bytes 73736 | tf_op jit(solution)/shard_map/ppermute | solution.py:36
  75.9 3.6 %collective-permute-start.12 = (bf16[96,128]{1,0:T(8,128)(2,1)S(1)}, bf16[96,128]{1,0:T(8,128)(2,1)S(1)}, u32[]{:S(2)}, u32[]{:S(2)}) collective-permute-start(bf16[96,128]{1,0:T(8,128)(2,1)S(1)} %get-tuple-element.193), channel_id=1, source_target_pairs={{56,0},{120,64},{58,2},{122,66},{60,4},{124,68},{62,6},{126,70},{0... | collective-permute-start | bytes 73736 | tf_op jit(solution)/shard_map/ppermute | solution.py:36
  79.5 2.1 %shard_map.166.refs_12_ = bf16[384,1792]{1,0:T(8,128)(2,1)S(1)} custom-call(s32[2,1792]{1,0:T(2,128)S(1)} %collective-permute-done.3.after.edges.refs_2_, f32[8,1792]{1,0:T(8,128)S(1)} %get-tuple-element.179.geo, bf16[288,1792]{1,0:T(8,128)(2,1)S(1)} %get-tuple-element.180.pool, bf16[256,128]{1,0:T(8,128)(2,1)S(1)} %get-tuple-element.181.at, ...), custom_call_target="tpu_custom_call" | custom-call | flops 1000000000 | bytes 1000000 | tf_op jit(solution)/shard_map/pallas_call | solution.py:142
  81.6 0.0 collective-permute-done.11
  81.6 0.1 collective-permute-done.12
  81.7 2.2 %shard_map.168 = (f32[16,128]{1,0:T(8,128)S(1)}, f32[16,128]{1,0:T(8,128)S(1)}, f32[16,128]{1,0:T(8,128)S(1)}) custom-call(s32[2,1792]{1,0:T(2,128)S(1)} %collective-permute-done.2.before.edges.refs_0_, s32[2,1792]{1,0:T(2,128)S(1)} %collective-permute-done.refs_4_.edges.refs_1_, s32[2,1792]{1,0:T(2,128)S(1)} %collective-permute-done.3.after.edges.refs_2_, ...), custom_call_target="tpu_custom_call" | custom-call | flops 1000000 | bytes 1000000 | tf_op jit(solution)/shard_map/pallas_call | solution.py:142
  83.9 3.0 %collective-permute-start.13 = (f32[16,128]{1,0:T(8,128)S(1)}, f32[16,128]{1,0:T(8,128)S(1)}, u32[]{:S(2)}, u32[]{:S(2)}) collective-permute-start(f32[16,128]{1,0:T(8,128)S(1)} %get-tuple-element.190), channel_id=1, source_target_pairs={{8,0},{72,64},{10,2},{74,66},{12,4},{76,68},{14,6},{78,70},{16,8},... | collective-permute-start | bytes 24584 | tf_op jit(solution)/shard_map/ppermute | solution.py:36
  87.0 2.3 %collective-permute-start.14 = (f32[16,128]{1,0:T(8,128)S(1)}, f32[16,128]{1,0:T(8,128)S(1)}, u32[]{:S(2)}, u32[]{:S(2)}) collective-permute-start(f32[16,128]{1,0:T(8,128)S(1)} %get-tuple-element.191), channel_id=1, source_target_pairs={{56,0},{120,64},{58,2},{122,66},{60,4},{124,68},{62,6},{126,70},{0... | collective-permute-start | bytes 24584 | tf_op jit(solution)/shard_map/ppermute | solution.py:36
  89.2 0.0 collective-permute-done.13.b
  89.2 3.3 %collective-permute-done.14.c = f32[16,128]{1,0:T(8,128)S(1)} collective-permute-done((f32[16,128]{1,0:T(8,128)S(1)}, f32[16,128]{1,0:T(8,128)S(1)}, u32[]{:S(2)}, u32[]{:S(2)}) %collective-permute-start.14) | collective-permute-done | bytes 8224 | tf_op jit(solution)/shard_map/ppermute | solution.py:36
  92.6 0.2 shard_map.169
  92.8 16.5 %all_to_all.10 = f32[64,1,128]{2,1,0:T(1,128)S(1)} all-to-all(f32[64,1,128]{2,1,0:T(1,128)S(1)} %bitcast.11), channel_id=1, replica_groups=mesh['gx'=8,'gy'=8,'gz'=8] {'gx','gz'}, dimensions={0} | all-to-all | bytes 65536 | tf_op jit(solution)/shard_map/all_to_all | solution.py:55
  109.3 0.6 shard_map.170
  (8 shorter events, 0.1 us)
Async XLA Ops:
  3.4 24.1 %all-to-all-start = ((f32[64,1,128]{2,1,0:T(1,128)}), f32[64,1,128]{2,1,0:T(1,128)S(1)}, u32[]{:S(2)}, u32[]{:S(2)}) async-start(f32[64,1,128]{2,1,0:T(1,128)} %bitcast.1), calls=%async_computation | async-start | bytes 65536 | tf_op jit(solution)/shard_map/all_to_all | solution.py:55
  18.3 9.2 %collective-permute-start = (s32[2,1792]{1,0:T(2,128)S(1)}, s32[2,1792]{1,0:T(2,128)S(1)}, u32[]{:S(2)}, u32[]{:S(2)}) collective-permute-start(s32[2,1792]{1,0:T(2,128)S(1)} %get-tuple-element.112), channel_id=1, source_target_pairs={{0,0},{1,64},{2,2},{3,66},{4,4},{5,68},{6,6},{7,70},{8,8},{9,72},{... | collective-permute-start | bytes 43016 | tf_op jit(solution)/shard_map/ppermute | solution.py:36
  27.5 7.1 %collective-permute-start.1 = (f32[64,128]{1,0:T(8,128)S(1)}, f32[64,128]{1,0:T(8,128)S(1)}, u32[]{:S(2)}, u32[]{:S(2)}) collective-permute-start(f32[64,128]{1,0:T(8,128)S(1)} %bitcast.13), channel_id=1, source_target_pairs={{8,0},{72,64},{10,2},{74,66},{12,4},{76,68},{14,6},{78,70},{16,8},... | collective-permute-start | bytes 98312 | tf_op jit(solution)/shard_map/ppermute | solution.py:36
  32.6 7.3 %collective-permute-start.4 = (f32[64,128]{1,0:T(8,128)S(1)}, f32[64,128]{1,0:T(8,128)S(1)}, u32[]{:S(2)}, u32[]{:S(2)}) collective-permute-start(f32[64,128]{1,0:T(8,128)S(1)} %bitcast.14), channel_id=1, source_target_pairs={{56,0},{120,64},{58,2},{122,66},{60,4},{124,68},{62,6},{126,70},{0... | collective-permute-start | bytes 98312 | tf_op jit(solution)/shard_map/ppermute | solution.py:36
  34.6 7.7 %collective-permute-start.3 = (s32[2,1792]{1,0:T(2,128)S(1)}, s32[2,1792]{1,0:T(2,128)S(1)}, u32[]{:S(2)}, u32[]{:S(2)}) collective-permute-start(s32[2,1792]{1,0:T(2,128)S(1)} %collective-permute-done.refs_4_.edges.refs_1_), channel_id=1, source_target_pairs={{128,0},{192,64},{130,2},{194,66},{132,4},{196,68},{134,6},{198,70... | collective-permute-start | bytes 43016 | tf_op jit(solution)/shard_map/ppermute | solution.py:36
  37.1 5.7 %collective-permute-start.2 = (s32[2,1792]{1,0:T(2,128)S(1)}, s32[2,1792]{1,0:T(2,128)S(1)}, u32[]{:S(2)}, u32[]{:S(2)}) collective-permute-start(s32[2,1792]{1,0:T(2,128)S(1)} %collective-permute-done.refs_4_.edges.refs_1_), channel_id=1, source_target_pairs={{385,0},{449,64},{387,2},{451,66},{389,4},{453,68},{391,6},{455,70... | collective-permute-start | bytes 43016 | tf_op jit(solution)/shard_map/ppermute | solution.py:36
  46.3 8.3 %collective-permute-start.6 = (bf16[96,128]{1,0:T(8,128)(2,1)S(1)}, bf16[96,128]{1,0:T(8,128)(2,1)S(1)}, u32[]{:S(2)}, u32[]{:S(2)}) collective-permute-start(bf16[96,128]{1,0:T(8,128)(2,1)S(1)} %get-tuple-element.126), channel_id=1, source_target_pairs={{8,0},{72,64},{10,2},{74,66},{12,4},{76,68},{14,6},{78,70},{16,8},... | collective-permute-start | bytes 73736 | tf_op jit(solution)/shard_map/ppermute | solution.py:36
  50.9 5.8 %collective-permute-start.5 = (bf16[96,128]{1,0:T(8,128)(2,1)S(1)}, bf16[96,128]{1,0:T(8,128)(2,1)S(1)}, u32[]{:S(2)}, u32[]{:S(2)}) collective-permute-start(bf16[96,128]{1,0:T(8,128)(2,1)S(1)} %get-tuple-element.126), channel_id=1, source_target_pairs={{56,0},{120,64},{58,2},{122,66},{60,4},{124,68},{62,6},{126,70},{0... | collective-permute-start | bytes 73736 | tf_op jit(solution)/shard_map/ppermute | solution.py:36
  56.7 8.9 %collective-permute-start.8 = (bf16[288,128]{1,0:T(8,128)(2,1)S(1)}, bf16[288,128]{1,0:T(8,128)(2,1)S(1)}, u32[]{:S(2)}, u32[]{:S(2)}) collective-permute-start(bf16[288,128]{1,0:T(8,128)(2,1)S(1)} %pad_maximum_fusion.own), channel_id=1, source_target_pairs={{64,0},{2,64},{66,2},{4,66},{68,4},{6,68},{70,6},{0,70},{72,8},{10... | collective-permute-start | bytes 221192 | tf_op jit(solution)/shard_map/ppermute | solution.py:36
  62.4 3.2 %collective-permute-start.7 = (bf16[288,128]{1,0:T(8,128)(2,1)S(1)}, bf16[288,128]{1,0:T(8,128)(2,1)S(1)}, u32[]{:S(2)}, u32[]{:S(2)}) collective-permute-start(bf16[288,128]{1,0:T(8,128)(2,1)S(1)} %pad_maximum_fusion.own), channel_id=1, source_target_pairs={{70,0},{0,64},{64,2},{2,66},{66,4},{4,68},{68,6},{6,70},{78,8},{8,... | collective-permute-start | bytes 221192 | tf_op jit(solution)/shard_map/ppermute | solution.py:36
  69.3 4.6 %collective-permute-start.9 = (bf16[288,128]{1,0:T(8,128)(2,1)S(1)}, bf16[288,128]{1,0:T(8,128)(2,1)S(1)}, u32[]{:S(2)}, u32[]{:S(2)}) collective-permute-start(bf16[288,128]{1,0:T(8,128)(2,1)S(1)} %get-tuple-element.153), channel_id=1, source_target_pairs={{64,0},{2,64},{66,2},{4,66},{68,4},{6,68},{70,6},{0,70},{72,8},{10... | collective-permute-start | bytes 221192 | tf_op jit(solution)/shard_map/ppermute | solution.py:36
  71.1 2.8 %collective-permute-start.10 = (bf16[288,128]{1,0:T(8,128)(2,1)S(1)}, bf16[288,128]{1,0:T(8,128)(2,1)S(1)}, u32[]{:S(2)}, u32[]{:S(2)}) collective-permute-start(bf16[288,128]{1,0:T(8,128)(2,1)S(1)} %get-tuple-element.154), channel_id=1, source_target_pairs={{70,0},{0,64},{64,2},{2,66},{66,4},{4,68},{68,6},{6,70},{78,8},{8,... | collective-permute-start | bytes 221192 | tf_op jit(solution)/shard_map/ppermute | solution.py:36
  74.0 7.6 %collective-permute-start.11 = (bf16[96,128]{1,0:T(8,128)(2,1)S(1)}, bf16[96,128]{1,0:T(8,128)(2,1)S(1)}, u32[]{:S(2)}, u32[]{:S(2)}) collective-permute-start(bf16[96,128]{1,0:T(8,128)(2,1)S(1)} %get-tuple-element.192), channel_id=1, source_target_pairs={{8,0},{72,64},{10,2},{74,66},{12,4},{76,68},{14,6},{78,70},{16,8},... | collective-permute-start | bytes 73736 | tf_op jit(solution)/shard_map/ppermute | solution.py:36
  75.9 5.8 %collective-permute-start.12 = (bf16[96,128]{1,0:T(8,128)(2,1)S(1)}, bf16[96,128]{1,0:T(8,128)(2,1)S(1)}, u32[]{:S(2)}, u32[]{:S(2)}) collective-permute-start(bf16[96,128]{1,0:T(8,128)(2,1)S(1)} %get-tuple-element.193), channel_id=1, source_target_pairs={{56,0},{120,64},{58,2},{122,66},{60,4},{124,68},{62,6},{126,70},{0... | collective-permute-start | bytes 73736 | tf_op jit(solution)/shard_map/ppermute | solution.py:36
  83.9 5.3 %collective-permute-start.13 = (f32[16,128]{1,0:T(8,128)S(1)}, f32[16,128]{1,0:T(8,128)S(1)}, u32[]{:S(2)}, u32[]{:S(2)}) collective-permute-start(f32[16,128]{1,0:T(8,128)S(1)} %get-tuple-element.190), channel_id=1, source_target_pairs={{8,0},{72,64},{10,2},{74,66},{12,4},{76,68},{14,6},{78,70},{16,8},... | collective-permute-start | bytes 24584 | tf_op jit(solution)/shard_map/ppermute | solution.py:36
  87.0 5.6 %collective-permute-start.14 = (f32[16,128]{1,0:T(8,128)S(1)}, f32[16,128]{1,0:T(8,128)S(1)}, u32[]{:S(2)}, u32[]{:S(2)}) collective-permute-start(f32[16,128]{1,0:T(8,128)S(1)} %get-tuple-element.191), channel_id=1, source_target_pairs={{56,0},{120,64},{58,2},{122,66},{60,4},{124,68},{62,6},{126,70},{0... | collective-permute-start | bytes 24584 | tf_op jit(solution)/shard_map/ppermute | solution.py:36

commit v5 on v4

--- a/solution.py
+++ b/solution.py
@@ -209,12 +209,15 @@
     wup_o[...] = jnp.concatenate([hi, lo], axis=1)
 
 
+def pick_kernel(chosen, plane, out):
+    out[...] = nn(chosen[...], plane[...], precision=HIGH)
+
+
 def own_kernel(box, *refs):
-    (chosen, below, level, above, edges), weights = refs[:5], refs[5:11]
-    (mask_o, full_o, h1_o, parts, table), results = refs[11:16], refs[16:21]
+    (below, level, above, edges), weights = refs[:4], refs[4:10]
+    (mask_o, full_o, h1_o, parts, table), results = refs[10:15], refs[15:20]
     table[...] = jnp.zeros_like(table)
-    for dy, plane in enumerate((below, level, above)):
-        near = nn(chosen[...], plane[...], precision=HIGH)
+    for dy, near in enumerate((below, level, above)):
         for i in range(5):
             table[9 * i + 3 * dy : 9 * i + 3 * dy + 3] = near[3 * i : 3 * i + 3]
     rows = table[...]
@@ -514,12 +517,16 @@
         embed, radial_in, radial_out, w_up, w_mix, lam, read_one[None], read_hidden.T, read_out[None],
         far=True, scratch=like(embed, radial_in, radial_out, w_up, w_mix),
     )
-    level, weights, edges = lax.optimization_barrier((level, weights, edges))
+    level, weights = lax.optimization_barrier((level, weights))
+    (level,) = call(pick_kernel, [((16, 128), F32)], chosen, level)
     emb, t0, win, wout, woutb, wup, mix, mix_t, wup_t, hidden_w, lam, read_one, read_hidden, read_out = weights
     below, level, above = widen(level, 1)
     edges, above = lax.optimization_barrier((edges, above))
-    before, edges, after = widen(edges, 0)
-    edges = (before, edges, after)
+    both = edges[0:1] + edges[1:2] * 65536
+    edges = [
+        e if k == 1 else jnp.concatenate([jnp.bitwise_and(e, 65535), jnp.right_shift(e, 16)], axis=0)
+        for k, e in enumerate((move(both, shift(0, -1)), edges, move(both, shift(0, 1))))
+    ]
 
     results = [((8, count), F32), ((288, count), BF16), ((256, 128), BF16), ((128, count), BF16),
                ((384, count), BF16)]
@@ -527,7 +534,7 @@
         functools.partial(own_kernel, box),
         [((1, 32), F32), ((32, 128), F32), ((32, 128), BF16), ((4, 56, 96), F32), ((56, 128), F32)]
         + results,
-        chosen, below, level, above, edges[1], emb, t0, win, wout, lam, mix,
+        below, level, above, edges[1], emb, t0, win, wout, lam, mix,
     )
     h1, *sides = call(
         functools.partial(sides_kernel, box), [((96, 128), BF16)] + results * 2,

time: 110 us -> 110 us (level)
  starting transfers between devices: 56.8 us -> 55 us
    all_to_all x1, waiting for transfers between devices: 0.01 us -> 3.9 us  [exchange(): return lax.all_to_all(rows, ('gx', 'gz'), 0, 0, tiled=True).reshape(x.shape)]
    ppermute x15, waiting for transfers between devices: 10.1 us -> 6.19 us  [move(): return lax.ppermute(x, AXES, pairs)]
    ppermute x15, starting transfers between devices: 41.9 us -> 40.1 us  [move(): return lax.ppermute(x, AXES, pairs)]
    pallas_call x13 -> x14, Pallas kernels: 24.2 us -> 24.1 us  [call(): pl.pallas_call(kernel, out_shape=tuple((jax.ShapeDtypeStruct(s, d) for s,...]
where the time goes in v5:
time: 110 us; the launch traced here: 109 us
  starting transfers between devices  55 us (50%)
  Pallas kernels  24.1 us (22%)
  blocking collectives  17.5 us (16%)
  waiting for transfers between devices  10.1 us (9%)
  between operations  2.32 us (2%)
    ppermute x15, starting transfers between devices, move(): return lax.ppermute(x, AXES, pairs)  40.1 us
    pallas_call x14, Pallas kernels, call(): pl.pallas_call(kernel, out_shape=tuple((jax.ShapeDtypeStruct(s, d) for s,...  24.1 us
    all_to_all x1, blocking collectives, exchange(): return lax.all_to_all(rows, ('gx', 'gz'), 0, 0, tiled=True).reshape(x.shape)  17.5 us
    all_to_all x1, starting transfers between devices, exchange(): return lax.all_to_all(rows, ('gx', 'gz'), 0, 0, tiled=True).reshape(x.shape)  14.8 us
    ppermute x15, waiting for transfers between devices, move(): return lax.ppermute(x, AXES, pairs)  6.19 us
    all_to_all x1, waiting for transfers between devices, exchange(): return lax.all_to_all(rows, ('gx', 'gz'), 0, 0, tiled=True).reshape(x.shape)  3.9 us
  transfers between devices with their start and end apart: 16, of which 5 were waited for; matrix products, arithmetic and copies ran while one was open for 0% of the time, Pallas kernels for 11%

profile of v5, /device:TPU:1, one launch (start us, length us, event | category | flops | bytes accessed | tf_op | source)
XLA Modules:
  0.0 109.3 jit_solution(850012210616590996)
XLA Ops:
  1.9 1.5 %shard_map.158 = (f32[64,128]{1,0:T(8,128)}, s32[2,1792]{1,0:T(2,128)S(1)}) custom-call(s32[1,1,1]{2,1,0:T(1,128)S(6)} %copy.19.refs_0_, s32[1,1,1]{2,1,0:T(1,128)S(6)} %copy.20.refs_1_, f32[3,1,1,1,32]{4,3,2,1,0:T(1,128)} %refs_2_.2, s32[1,1,1,32]{3,2,1,0:T(1,128)} %refs_3_.2, s32[1,1,1,1792]{3,2,1,0:T(1,128)} %refs_4_.2, s32[1,1,1,1792]{3,2,1,0:T(1,128)} %refs_5_.2), custom_call_target="tpu_custom_call" | custom-call | flops 1000000 | bytes 1000000 | tf_op jit(solution)/shard_map/pallas_call | solution.py:142
  3.4 14.8 %all-to-all-start = ((f32[64,1,128]{2,1,0:T(1,128)}), f32[64,1,128]{2,1,0:T(1,128)S(1)}, u32[]{:S(2)}, u32[]{:S(2)}) async-start(f32[64,1,128]{2,1,0:T(1,128)} %bitcast.1), calls=%async_computation | async-start | bytes 65536 | tf_op jit(solution)/shard_map/all_to_all | solution.py:55
  18.3 3.5 %collective-permute-start = (s32[2,1792]{1,0:T(2,128)S(1)}, s32[2,1792]{1,0:T(2,128)S(1)}, u32[]{:S(2)}, u32[]{:S(2)}) collective-permute-start(s32[2,1792]{1,0:T(2,128)S(1)} %get-tuple-element.96), channel_id=1, source_target_pairs={{0,0},{1,64},{2,2},{3,66},{4,4},{5,68},{6,6},{7,70},{8,8},{9,72},{... | collective-permute-start | bytes 43016 | tf_op jit(solution)/shard_map/ppermute | solution.py:36
  21.9 0.1 and_select_fusion.chosen
  22.0 1.5 %shard_map.159 = (f32[128,128]{1,0:T(8,128)S(1)}, bf16[128,256]{1,0:T(8,128)(2,1)S(1)}, bf16[2,64,32]{2,1,0:T(8,128)(2,1)S(1)}, bf16[2,384,192]{2,1,0:T(8,128)(2...) custom-call(f32[89,128]{1,0:T(8,128)} %refs_0_.2, ...), custom_call_target="tpu_custom_call" | custom-call | flops 1000000 | bytes 1000000 | tf_op jit(solution)/shard_map/pallas_call | solution.py:142
  23.6 3.9 %all-to-all-done = f32[64,1,128]{2,1,0:T(1,128)S(1)} async-done(((f32[64,1,128]{2,1,0:T(1,128)}), f32[64,1,128]{2,1,0:T(1,128)S(1)}, u32[]{:S(2)}, u32[]{:S(2)}) %all-to-all-start) | async-done | bytes 32800 | tf_op jit(solution)/shard_map/all_to_all | solution.py:55
  27.5 0.1 shard_map.160.refs_1_
  27.6 5.1 %collective-permute-start.1 = (f32[16,128]{1,0:T(8,128)S(1)}, f32[16,128]{1,0:T(8,128)S(1)}, u32[]{:S(2)}, u32[]{:S(2)}) collective-permute-start(f32[16,128]{1,0:T(8,128)S(1)} %shard_map.160.refs_1_), channel_id=1, source_target_pairs={{8,0},{72,64},{10,2},{74,66},{12,4},{76,68},{14,6},{78,70},{16,8},... | collective-permute-start | bytes 24584 | tf_op jit(solution)/shard_map/ppermute | solution.py:36
  32.7 1.9 %collective-permute-start.4 = (f32[16,128]{1,0:T(8,128)S(1)}, f32[16,128]{1,0:T(8,128)S(1)}, u32[]{:S(2)}, u32[]{:S(2)}) collective-permute-start(f32[16,128]{1,0:T(8,128)S(1)} %shard_map.160.refs_1_), channel_id=1, source_target_pairs={{56,0},{120,64},{58,2},{122,66},{60,4},{124,68},{62,6},{126,70},{0... | collective-permute-start | bytes 24584 | tf_op jit(solution)/shard_map/ppermute | solution.py:36
  34.6 0.0 collective-permute-done.refs_3_.edges.refs_1_
  34.7 0.0 collective-permute-done.1.refs_2_
  34.7 2.5 %collective-permute-start.3 = (s32[1,1792]{1,0:T(1,128)S(1)}, s32[1,1792]{1,0:T(1,128)S(1)}, u32[]{:S(2)}, u32[]{:S(2)}) collective-permute-start(s32[1,1792]{1,0:T(1,128)S(1)} %multiply_add_fusion), channel_id=1, source_target_pairs={{128,0},{192,64},{130,2},{194,66},{132,4},{196,68},{134,6},{198,70... | collective-permute-start | bytes 21512 | tf_op jit(solution)/shard_map/ppermute | solution.py:36
  37.2 2.8 %collective-permute-start.2 = (s32[1,1792]{1,0:T(1,128)S(1)}, s32[1,1792]{1,0:T(1,128)S(1)}, u32[]{:S(2)}, u32[]{:S(2)}) collective-permute-start(s32[1,1792]{1,0:T(1,128)S(1)} %multiply_add_fusion), channel_id=1, source_target_pairs={{385,0},{449,64},{387,2},{451,66},{389,4},{453,68},{391,6},{455,70... | collective-permute-start | bytes 21512 | tf_op jit(solution)/shard_map/ppermute | solution.py:36
  40.0 0.0 collective-permute-done.4.refs_0_
  40.0 2.0 %shard_map.161 = (f32[1,32]{1,0:T(1,128)S(1)}, f32[32,128]{1,0:T(8,128)S(1)}, bf16[32,128]{1,0:T(8,128)(2,1)S(1)}, f32[4,56,96]{2,1,0:T(8,128)S(1)}, f32[56,128]...) custom-call(f32[16,128]{1,0:T(8,128)S(1)} %collective-permute-done.4, ...), custom_call_target="tpu_custom_call" | custom-call | flops 1000000 | bytes 1000000 | tf_op jit(solution)/shard_map/pallas_call | solution.py:142
  42.0 0.0 collective-permute-done.3
  42.1 0.7 collective-permute-done.2
  42.8 3.6 %shard_map.162 = (bf16[96,128]{1,0:T(8,128)(2,1)S(1)}, f32[8,1792]{1,0:T(8,128)S(1)}, bf16[288,1792]{1,0:T(8,128)(2,1)S(1)}, bf16[256,128]{1,0:T(8,128)(2,1)S(1)...) custom-call(s32[2,1792]{1,0:T(2,128)S(1)} %pad_add_fusion.before.edg, ...), custom_call_target="tpu_custom_call" | custom-call | flops 1000000 | bytes 1000000 | tf_op jit(solution)/shard_map/pallas_call | solution.py:142
  46.4 4.6 %collective-permute-start.6 = (bf16[96,128]{1,0:T(8,128)(2,1)S(1)}, bf16[96,128]{1,0:T(8,128)(2,1)S(1)}, u32[]{:S(2)}, u32[]{:S(2)}) collective-permute-start(bf16[96,128]{1,0:T(8,128)(2,1)S(1)} %get-tuple-element.124), channel_id=1, source_target_pairs={{8,0},{72,64},{10,2},{74,66},{12,4},{76,68},{14,6},{78,70},{16,8},... | collective-permute-start | bytes 73736 | tf_op jit(solution)/shard_map/ppermute | solution.py:36
  51.0 2.1 %collective-permute-start.5 = (bf16[96,128]{1,0:T(8,128)(2,1)S(1)}, bf16[96,128]{1,0:T(8,128)(2,1)S(1)}, u32[]{:S(2)}, u32[]{:S(2)}) collective-permute-start(bf16[96,128]{1,0:T(8,128)(2,1)S(1)} %get-tuple-element.124), channel_id=1, source_target_pairs={{56,0},{120,64},{58,2},{122,66},{60,4},{124,68},{62,6},{126,70},{0... | collective-permute-start | bytes 73736 | tf_op jit(solution)/shard_map/ppermute | solution.py:36
  53.1 1.6 %shard_map.163 = (bf16[864,1792]{1,0:T(8,128)(2,1)S(1)}, f32[384,1792]{1,0:T(8,128)S(1)}, f32[64,1792]{1,0:T(8,128)S(1)}, f32[1,32]{1,0:T(1,128)S(1)}, f32[32,128]{1,0:T(8,128)S(1)}, /*index=5*/f32[32,16]{1,0:T(8,128)S(1)}) custom-call(s32[2,1792]{1,0:T(2,128)S(1)} %collective-permute-done.refs_3_.edges.refs_1_, f32[8,1792]{1,0:T(8,128)S(1)} %get-tuple-element.125.geo, ...), custom_call_target="tpu_custom_call" | custom-call | flops 1000000000 | bytes 1000000 | tf_op jit(solution)/shard_map/pallas_call | solution.py:142
  54.7 0.0 collective-permute-done.6
  54.7 2.1 %collective-permute-done.5 = bf16[96,128]{1,0:T(8,128)(2,1)S(1)} collective-permute-done((bf16[96,128]{1,0:T(8,128)(2,1)S(1)}, bf16[96,128]{1,0:T(8,128)(2,1)S(1)}, u32[]{:S(2)}, u32[]{:S(2)}) %collective-permute-start.5) | collective-permute-done | bytes 24608 | tf_op jit(solution)/shard_map/ppermute | solution.py:36
  56.8 4.0 %collective-permute-start.8 = (bf16[288,128]{1,0:T(8,128)(2,1)S(1)}, bf16[288,128]{1,0:T(8,128)(2,1)S(1)}, u32[]{:S(2)}, u32[]{:S(2)}) collective-permute-start(bf16[288,128]{1,0:T(8,128)(2,1)S(1)} %pad_maximum_fusion.own), channel_id=1, source_target_pairs={{64,0},{2,64},{66,2},{4,66},{68,4},{6,68},{70,6},{0,70},{72,8},{10... | collective-permute-start | bytes 221192 | tf_op jit(solution)/shard_map/ppermute | solution.py:36
  60.7 0.2 collective-permute-start.7
  60.9 2.1 %shard_map.164.refs_11_ = bf16[384,1792]{1,0:T(8,128)(2,1)S(1)} custom-call(s32[2,1792]{1,0:T(2,128)S(1)} %collective-permute-done.refs_3_.edges.refs_1_, f32[8,1792]{1,0:T(8,128)S(1)} %get-tuple-element.125.geo, bf16[288,1792]{1,0:T(8,128)(2,1)S(1)} %get-tuple-element.137.pool, bf16[256,128]{1,0:T(8,128)(2,1)S(1)} %get-tuple-element.138.at, ...), custom_call_target="tpu_custom_call" | custom-call | flops 1000000000 | bytes 1000000 | tf_op jit(solution)/shard_map/pallas_call | solution.py:142
  63.0 0.0 collective-permute-done.8.right
  63.0 0.0 collective-permute-done.7.left
  63.0 3.6 %shard_map.165 = (bf16[288,128]{1,0:T(8,128)(2,1)S(1)}, f32[288,128]{1,0:T(8,128)S(1)}, bf16[288,128]{1,0:T(8,128)(2,1)S(1)}, f32[32,128]{1,0:T(8,128)S(1)}, f32...) custom-call(bf16[288,128]{1,0:T(8,128)(2,1)S(1)} %collective-permute, ...), custom_call_target="tpu_custom_call" | custom-call | flops 1000000 | bytes 1000000 | tf_op jit(solution)/shard_map/pallas_call | solution.py:142
  66.7 2.7 %collective-permute-start.9 = (bf16[288,128]{1,0:T(8,128)(2,1)S(1)}, bf16[288,128]{1,0:T(8,128)(2,1)S(1)}, u32[]{:S(2)}, u32[]{:S(2)}) collective-permute-start(bf16[288,128]{1,0:T(8,128)(2,1)S(1)} %get-tuple-element.151), channel_id=1, source_target_pairs={{64,0},{2,64},{66,2},{4,66},{68,4},{6,68},{70,6},{0,70},{72,8},{10... | collective-permute-start | bytes 221192 | tf_op jit(solution)/shard_map/ppermute | solution.py:36
  69.4 0.0 collective-permute-start.10
  69.4 0.7 shard_map.168.refs_13_
  70.1 2.1 %shard_map.166.refs_10_ = bf16[384,1792]{1,0:T(8,128)(2,1)S(1)} custom-call(s32[2,1792]{1,0:T(2,128)S(1)} %pad_add_fusion.before.edges.refs_0_, f32[8,1792]{1,0:T(8,128)S(1)} %get-tuple-element.159.geo, bf16[288,1792]{1,0:T(8,128)(2,1)S(1)} %get-tuple-element.160.pool, bf16[256,128]{1,0:T(8,128)(2,1)S(1)} %get-tuple-element.161.at, ...), custom_call_target="tpu_custom_call" | custom-call | flops 1000000000 | bytes 1000000 | tf_op jit(solution)/shard_map/pallas_call | solution.py:142
  72.2 0.0 collective-permute-done.9
  72.2 0.0 collective-permute-done.10
  72.3 1.9 %collective-permute-start.11 = (bf16[96,128]{1,0:T(8,128)(2,1)S(1)}, bf16[96,128]{1,0:T(8,128)(2,1)S(1)}, u32[]{:S(2)}, u32[]{:S(2)}) collective-permute-start(bf16[96,128]{1,0:T(8,128)(2,1)S(1)} %get-tuple-element.190), channel_id=1, source_target_pairs={{8,0},{72,64},{10,2},{74,66},{12,4},{76,68},{14,6},{78,70},{16,8},... | collective-permute-start | bytes 73736 | tf_op jit(solution)/shard_map/ppermute | solution.py:36
  74.2 3.6 %collective-permute-start.12 = (bf16[96,128]{1,0:T(8,128)(2,1)S(1)}, bf16[96,128]{1,0:T(8,128)(2,1)S(1)}, u32[]{:S(2)}, u32[]{:S(2)}) collective-permute-start(bf16[96,128]{1,0:T(8,128)(2,1)S(1)} %get-tuple-element.191), channel_id=1, source_target_pairs={{56,0},{120,64},{58,2},{122,66},{60,4},{124,68},{62,6},{126,70},{0... | collective-permute-start | bytes 73736 | tf_op jit(solution)/shard_map/ppermute | solution.py:36
  77.8 2.1 %shard_map.167.refs_12_ = bf16[384,1792]{1,0:T(8,128)(2,1)S(1)} custom-call(s32[2,1792]{1,0:T(2,128)S(1)} %pad_add_fusion.1.after.edges.refs_2_, f32[8,1792]{1,0:T(8,128)S(1)} %get-tuple-element.177.geo, bf16[288,1792]{1,0:T(8,128)(2,1)S(1)} %get-tuple-element.178.pool, bf16[256,128]{1,0:T(8,128)(2,1)S(1)} %get-tuple-element.179.at, ...), custom_call_target="tpu_custom_call" | custom-call | flops 1000000000 | bytes 1000000 | tf_op jit(solution)/shard_map/pallas_call | solution.py:142
  79.9 0.0 collective-permute-done.11
  79.9 0.1 collective-permute-done.12
  80.0 2.2 %shard_map.169 = (f32[16,128]{1,0:T(8,128)S(1)}, f32[16,128]{1,0:T(8,128)S(1)}, f32[16,128]{1,0:T(8,128)S(1)}) custom-call(s32[2,1792]{1,0:T(2,128)S(1)} %pad_add_fusion.before.edges.refs_0_, s32[2,1792]{1,0:T(2,128)S(1)} %collective-permute-done.refs_3_.edges.refs_1_, s32[2,1792]{1,0:T(2,128)S(1)} %pad_add_fusion.1.after.edges.refs_2_, ...), custom_call_target="tpu_custom_call" | custom-call | flops 1000000 | bytes 1000000 | tf_op jit(solution)/shard_map/pallas_call | solution.py:142
  82.2 3.0 %collective-permute-start.13 = (f32[16,128]{1,0:T(8,128)S(1)}, f32[16,128]{1,0:T(8,128)S(1)}, u32[]{:S(2)}, u32[]{:S(2)}) collective-permute-start(f32[16,128]{1,0:T(8,128)S(1)} %get-tuple-element.188), channel_id=1, source_target_pairs={{8,0},{72,64},{10,2},{74,66},{12,4},{76,68},{14,6},{78,70},{16,8},... | collective-permute-start | bytes 24584 | tf_op jit(solution)/shard_map/ppermute | solution.py:36
  85.3 2.3 %collective-permute-start.14 = (f32[16,128]{1,0:T(8,128)S(1)}, f32[16,128]{1,0:T(8,128)S(1)}, u32[]{:S(2)}, u32[]{:S(2)}) collective-permute-start(f32[16,128]{1,0:T(8,128)S(1)} %get-tuple-element.189), channel_id=1, source_target_pairs={{56,0},{120,64},{58,2},{122,66},{60,4},{124,68},{62,6},{126,70},{0... | collective-permute-start | bytes 24584 | tf_op jit(solution)/shard_map/ppermute | solution.py:36
  87.5 0.0 collective-permute-done.13.b
  87.5 3.3 %collective-permute-done.14.c = f32[16,128]{1,0:T(8,128)S(1)} collective-permute-done((f32[16,128]{1,0:T(8,128)S(1)}, f32[16,128]{1,0:T(8,128)S(1)}, u32[]{:S(2)}, u32[]{:S(2)}) %collective-permute-start.14) | collective-permute-done | bytes 8224 | tf_op jit(solution)/shard_map/ppermute | solution.py:36
  90.9 0.2 shard_map.170
  91.1 17.5 %all_to_all.10 = f32[64,1,128]{2,1,0:T(1,128)S(1)} all-to-all(f32[64,1,128]{2,1,0:T(1,128)S(1)} %bitcast.12), channel_id=1, replica_groups=mesh['gx'=8,'gy'=8,'gz'=8] {'gx','gz'}, dimensions={0} | all-to-all | bytes 65536 | tf_op jit(solution)/shard_map/all_to_all | solution.py:55
  108.6 0.6 shard_map.171
  (13 shorter events, 0.2 us)
Async XLA Ops:
  3.4 24.1 %all-to-all-start = ((f32[64,1,128]{2,1,0:T(1,128)}), f32[64,1,128]{2,1,0:T(1,128)S(1)}, u32[]{:S(2)}, u32[]{:S(2)}) async-start(f32[64,1,128]{2,1,0:T(1,128)} %bitcast.1), calls=%async_computation | async-start | bytes 65536 | tf_op jit(solution)/shard_map/all_to_all | solution.py:55
  18.3 16.4 %collective-permute-start = (s32[2,1792]{1,0:T(2,128)S(1)}, s32[2,1792]{1,0:T(2,128)S(1)}, u32[]{:S(2)}, u32[]{:S(2)}) collective-permute-start(s32[2,1792]{1,0:T(2,128)S(1)} %get-tuple-element.96), channel_id=1, source_target_pairs={{0,0},{1,64},{2,2},{3,66},{4,4},{5,68},{6,6},{7,70},{8,8},{9,72},{... | collective-permute-start | bytes 43016 | tf_op jit(solution)/shard_map/ppermute | solution.py:36
  27.6 7.0 %collective-permute-start.1 = (f32[16,128]{1,0:T(8,128)S(1)}, f32[16,128]{1,0:T(8,128)S(1)}, u32[]{:S(2)}, u32[]{:S(2)}) collective-permute-start(f32[16,128]{1,0:T(8,128)S(1)} %shard_map.160.refs_1_), channel_id=1, source_target_pairs={{8,0},{72,64},{10,2},{74,66},{12,4},{76,68},{14,6},{78,70},{16,8},... | collective-permute-start | bytes 24584 | tf_op jit(solution)/shard_map/ppermute | solution.py:36
  32.7 7.3 %collective-permute-start.4 = (f32[16,128]{1,0:T(8,128)S(1)}, f32[16,128]{1,0:T(8,128)S(1)}, u32[]{:S(2)}, u32[]{:S(2)}) collective-permute-start(f32[16,128]{1,0:T(8,128)S(1)} %shard_map.160.refs_1_), channel_id=1, source_target_pairs={{56,0},{120,64},{58,2},{122,66},{60,4},{124,68},{62,6},{126,70},{0... | collective-permute-start | bytes 24584 | tf_op jit(solution)/shard_map/ppermute | solution.py:36
  34.7 7.4 %collective-permute-start.3 = (s32[1,1792]{1,0:T(1,128)S(1)}, s32[1,1792]{1,0:T(1,128)S(1)}, u32[]{:S(2)}, u32[]{:S(2)}) collective-permute-start(s32[1,1792]{1,0:T(1,128)S(1)} %multiply_add_fusion), channel_id=1, source_target_pairs={{128,0},{192,64},{130,2},{194,66},{132,4},{196,68},{134,6},{198,70... | collective-permute-start | bytes 21512 | tf_op jit(solution)/shard_map/ppermute | solution.py:36
  37.2 5.6 %collective-permute-start.2 = (s32[1,1792]{1,0:T(1,128)S(1)}, s32[1,1792]{1,0:T(1,128)S(1)}, u32[]{:S(2)}, u32[]{:S(2)}) collective-permute-start(s32[1,1792]{1,0:T(1,128)S(1)} %multiply_add_fusion), channel_id=1, source_target_pairs={{385,0},{449,64},{387,2},{451,66},{389,4},{453,68},{391,6},{455,70... | collective-permute-start | bytes 21512 | tf_op jit(solution)/shard_map/ppermute | solution.py:36
  46.4 8.3 %collective-permute-start.6 = (bf16[96,128]{1,0:T(8,128)(2,1)S(1)}, bf16[96,128]{1,0:T(8,128)(2,1)S(1)}, u32[]{:S(2)}, u32[]{:S(2)}) collective-permute-start(bf16[96,128]{1,0:T(8,128)(2,1)S(1)} %get-tuple-element.124), channel_id=1, source_target_pairs={{8,0},{72,64},{10,2},{74,66},{12,4},{76,68},{14,6},{78,70},{16,8},... | collective-permute-start | bytes 73736 | tf_op jit(solution)/shard_map/ppermute | solution.py:36
  51.0 5.8 %collective-permute-start.5 = (bf16[96,128]{1,0:T(8,128)(2,1)S(1)}, bf16[96,128]{1,0:T(8,128)(2,1)S(1)}, u32[]{:S(2)}, u32[]{:S(2)}) collective-permute-start(bf16[96,128]{1,0:T(8,128)(2,1)S(1)} %get-tuple-element.124), channel_id=1, source_target_pairs={{56,0},{120,64},{58,2},{122,66},{60,4},{124,68},{62,6},{126,70},{0... | collective-permute-start | bytes 73736 | tf_op jit(solution)/shard_map/ppermute | solution.py:36
  56.8 6.2 %collective-permute-start.8 = (bf16[288,128]{1,0:T(8,128)(2,1)S(1)}, bf16[288,128]{1,0:T(8,128)(2,1)S(1)}, u32[]{:S(2)}, u32[]{:S(2)}) collective-permute-start(bf16[288,128]{1,0:T(8,128)(2,1)S(1)} %pad_maximum_fusion.own), channel_id=1, source_target_pairs={{64,0},{2,64},{66,2},{4,66},{68,4},{6,68},{70,6},{0,70},{72,8},{10... | collective-permute-start | bytes 221192 | tf_op jit(solution)/shard_map/ppermute | solution.py:36
  60.7 2.3 %collective-permute-start.7 = (bf16[288,128]{1,0:T(8,128)(2,1)S(1)}, bf16[288,128]{1,0:T(8,128)(2,1)S(1)}, u32[]{:S(2)}, u32[]{:S(2)}) collective-permute-start(bf16[288,128]{1,0:T(8,128)(2,1)S(1)} %pad_maximum_fusion.own), channel_id=1, source_target_pairs={{70,0},{0,64},{64,2},{2,66},{66,4},{4,68},{68,6},{6,70},{78,8},{8,... | collective-permute-start | bytes 221192 | tf_op jit(solution)/shard_map/ppermute | solution.py:36
  66.7 5.5 %collective-permute-start.9 = (bf16[288,128]{1,0:T(8,128)(2,1)S(1)}, bf16[288,128]{1,0:T(8,128)(2,1)S(1)}, u32[]{:S(2)}, u32[]{:S(2)}) collective-permute-start(bf16[288,128]{1,0:T(8,128)(2,1)S(1)} %get-tuple-element.151), channel_id=1, source_target_pairs={{64,0},{2,64},{66,2},{4,66},{68,4},{6,68},{70,6},{0,70},{72,8},{10... | collective-permute-start | bytes 221192 | tf_op jit(solution)/shard_map/ppermute | solution.py:36
  69.4 2.8 %collective-permute-start.10 = (bf16[288,128]{1,0:T(8,128)(2,1)S(1)}, bf16[288,128]{1,0:T(8,128)(2,1)S(1)}, u32[]{:S(2)}, u32[]{:S(2)}) collective-permute-start(bf16[288,128]{1,0:T(8,128)(2,1)S(1)} %get-tuple-element.152), channel_id=1, source_target_pairs={{70,0},{0,64},{64,2},{2,66},{66,4},{4,68},{68,6},{6,70},{78,8},{8,... | collective-permute-start | bytes 221192 | tf_op jit(solution)/shard_map/ppermute | solution.py:36
  72.3 7.6 %collective-permute-start.11 = (bf16[96,128]{1,0:T(8,128)(2,1)S(1)}, bf16[96,128]{1,0:T(8,128)(2,1)S(1)}, u32[]{:S(2)}, u32[]{:S(2)}) collective-permute-start(bf16[96,128]{1,0:T(8,128)(2,1)S(1)} %get-tuple-element.190), channel_id=1, source_target_pairs={{8,0},{72,64},{10,2},{74,66},{12,4},{76,68},{14,6},{78,70},{16,8},... | collective-permute-start | bytes 73736 | tf_op jit(solution)/shard_map/ppermute | solution.py:36
  74.2 5.8 %collective-permute-start.12 = (bf16[96,128]{1,0:T(8,128)(2,1)S(1)}, bf16[96,128]{1,0:T(8,128)(2,1)S(1)}, u32[]{:S(2)}, u32[]{:S(2)}) collective-permute-start(bf16[96,128]{1,0:T(8,128)(2,1)S(1)} %get-tuple-element.191), channel_id=1, source_target_pairs={{56,0},{120,64},{58,2},{122,66},{60,4},{124,68},{62,6},{126,70},{0... | collective-permute-start | bytes 73736 | tf_op jit(solution)/shard_map/ppermute | solution.py:36
  82.2 5.3 %collective-permute-start.13 = (f32[16,128]{1,0:T(8,128)S(1)}, f32[16,128]{1,0:T(8,128)S(1)}, u32[]{:S(2)}, u32[]{:S(2)}) collective-permute-start(f32[16,128]{1,0:T(8,128)S(1)} %get-tuple-element.188), channel_id=1, source_target_pairs={{8,0},{72,64},{10,2},{74,66},{12,4},{76,68},{14,6},{78,70},{16,8},... | collective-permute-start | bytes 24584 | tf_op jit(solution)/shard_map/ppermute | solution.py:36
  85.3 5.6 %collective-permute-start.14 = (f32[16,128]{1,0:T(8,128)S(1)}, f32[16,128]{1,0:T(8,128)S(1)}, u32[]{:S(2)}, u32[]{:S(2)}) collective-permute-start(f32[16,128]{1,0:T(8,128)S(1)} %get-tuple-element.189), channel_id=1, source_target_pairs={{56,0},{120,64},{58,2},{122,66},{60,4},{124,68},{62,6},{126,70},{0... | collective-permute-start | bytes 24584 | tf_op jit(solution)/shard_map/ppermute | solution.py:36

commit v6 on v5

--- a/solution.py
+++ b/solution.py
@@ -120,8 +120,10 @@
     centre = lax.broadcasted_iota(jnp.int32, (8, edges), 0).astype(F32) * (1.0 / 7.0)
     gap = d2 - centre
     basis = jnp.exp(-64.0 * gap * gap)
+    pre = nn(win, small_stack(basis))
+    if denv is None:
+        return pre / (1.0 + jnp.exp(-pre)) * env, None
     slope = basis * (-128.0 * gap)
-    pre = nn(win, small_stack(basis))
     dpre = nn(win, small_stack(slope))
     sig = 1.0 / (1.0 + jnp.exp(-pre))
     act = pre * sig
@@ -245,7 +247,7 @@
 def first_layer(
     box, start, edges, emb, t0, win, wout, lam, mix, geo_o, pool_o, at_o, lift_o, base_o, table, parts
 ):
-    lhs = jnp.concatenate([parts[c, start : start + 32] for c in range(4)], axis=0).astype(BF16)
+    lhs = jnp.concatenate([parts[c, start : start + 32] for c in range(4)], axis=0)
     middle = start + 13
     mine = [parts[c, middle : middle + 1] for c in range(4)] + [jnp.zeros((4, 96), F32)]
     mine = jnp.concatenate(mine, axis=0)
@@ -255,8 +257,13 @@
     block = ones_at(jnp.right_shift(sender, 5), 32)
     recv = ones_at(receiver, 32)
     recv_b = recv.astype(BF16)
-    got = nn(lhs, jnp.concatenate([slot] * 3, axis=0))
-    at_recv = nn(mine.astype(BF16), jnp.concatenate([recv_b] * 3, axis=0))
+    lhs = jnp.concatenate([lhs, jnp.zeros((128, 96), F32)], axis=1)
+    mine = jnp.concatenate([jnp.zeros((8, 96), F32), mine], axis=1)
+    got = nn(
+        jnp.concatenate([lhs, mine], axis=0).astype(BF16),
+        jnp.concatenate([slot] * 3 + [recv_b] * 3, axis=0),
+    )
+    at_recv = got[128:136]
     sent = [jnp.sum(got[32 * c : 32 * c + 32] * block, axis=0, keepdims=True) for c in range(4)]
     rel = []
     for c in range(3):
@@ -282,7 +289,7 @@
     ]
     for m, value in enumerate(harmonics):
         pool_o[32 * m : 32 * m + 32] = (recv * (value * 0.125)).astype(BF16)
-    hidden, _ = hidden_units(d2, env, denv, win[0])
+    hidden, _ = hidden_units(d2, env, None, win[0])
     radial = nn(wout[0], stack3(hidden))
     kind = ones_at(sent[3].astype(jnp.int32), 128).astype(BF16)
     lift = nn(t0[...], jnp.concatenate([kind, kind], axis=0))

time: 110 us -> 110 us (level)
  no operation moved by 1% of the time
where the time goes in v6:
time: 110 us; the launch traced here: 109 us
  starting transfers between devices  55 us (50%)
  Pallas kernels  23.9 us (22%)
  blocking collectives  17.5 us (16%)
  waiting for transfers between devices  10.2 us (9%)
  between operations  2.32 us (2%)
    ppermute x15, starting transfers between devices, move(): return lax.ppermute(x, AXES, pairs)  40.1 us
    pallas_call x14, Pallas kernels, call(): pl.pallas_call(kernel, out_shape=tuple((jax.ShapeDtypeStruct(s, d) for s,...  23.9 us
    all_to_all x1, blocking collectives, exchange(): return lax.all_to_all(rows, ('gx', 'gz'), 0, 0, tiled=True).reshape(x.shape)  17.5 us
    all_to_all x1, starting transfers between devices, exchange(): return lax.all_to_all(rows, ('gx', 'gz'), 0, 0, tiled=True).reshape(x.shape)  14.8 us
    ppermute x15, waiting for transfers between devices, move(): return lax.ppermute(x, AXES, pairs)  6.26 us
    all_to_all x1, waiting for transfers between devices, exchange(): return lax.all_to_all(rows, ('gx', 'gz'), 0, 0, tiled=True).reshape(x.shape)  3.9 us
  transfers between devices with their start and end apart: 16, of which 5 were waited for; matrix products, arithmetic and copies ran while one was open for 0% of the time, Pallas kernels for 11%

profile of v6, /device:TPU:1, one launch (start us, length us, event | category | flops | bytes accessed | tf_op | source)
XLA Modules:
  0.0 109.2 jit_solution(13157926399451459715)
XLA Ops:
  1.9 1.5 %shard_map.158 = (f32[64,128]{1,0:T(8,128)}, s32[2,1792]{1,0:T(2,128)S(1)}) custom-call(s32[1,1,1]{2,1,0:T(1,128)S(6)} %copy.19.refs_0_, s32[1,1,1]{2,1,0:T(1,128)S(6)} %copy.20.refs_1_, f32[3,1,1,1,32]{4,3,2,1,0:T(1,128)} %refs_2_.2, s32[1,1,1,32]{3,2,1,0:T(1,128)} %refs_3_.2, s32[1,1,1,1792]{3,2,1,0:T(1,128)} %refs_4_.2, s32[1,1,1,1792]{3,2,1,0:T(1,128)} %refs_5_.2), custom_call_target="tpu_custom_call" | custom-call | flops 1000000 | bytes 1000000 | tf_op jit(solution)/shard_map/pallas_call | solution.py:144
  3.4 14.8 %all-to-all-start = ((f32[64,1,128]{2,1,0:T(1,128)}), f32[64,1,128]{2,1,0:T(1,128)S(1)}, u32[]{:S(2)}, u32[]{:S(2)}) async-start(f32[64,1,128]{2,1,0:T(1,128)} %bitcast.1), calls=%async_computation | async-start | bytes 65536 | tf_op jit(solution)/shard_map/all_to_all | solution.py:55
  18.3 3.5 %collective-permute-start = (s32[2,1792]{1,0:T(2,128)S(1)}, s32[2,1792]{1,0:T(2,128)S(1)}, u32[]{:S(2)}, u32[]{:S(2)}) collective-permute-start(s32[2,1792]{1,0:T(2,128)S(1)} %get-tuple-element.96), channel_id=1, source_target_pairs={{0,0},{1,64},{2,2},{3,66},{4,4},{5,68},{6,6},{7,70},{8,8},{9,72},{... | collective-permute-start | bytes 43016 | tf_op jit(solution)/shard_map/ppermute | solution.py:36
  21.9 0.1 and_select_fusion.chosen
  22.0 1.5 %shard_map.159 = (f32[128,128]{1,0:T(8,128)S(1)}, bf16[128,256]{1,0:T(8,128)(2,1)S(1)}, bf16[2,64,32]{2,1,0:T(8,128)(2,1)S(1)}, bf16[2,384,192]{2,1,0:T(8,128)(2...) custom-call(f32[89,128]{1,0:T(8,128)} %refs_0_.2, ...), custom_call_target="tpu_custom_call" | custom-call | flops 1000000 | bytes 1000000 | tf_op jit(solution)/shard_map/pallas_call | solution.py:144
  23.6 3.9 %all-to-all-done = f32[64,1,128]{2,1,0:T(1,128)S(1)} async-done(((f32[64,1,128]{2,1,0:T(1,128)}), f32[64,1,128]{2,1,0:T(1,128)S(1)}, u32[]{:S(2)}, u32[]{:S(2)}) %all-to-all-start) | async-done | bytes 32800 | tf_op jit(solution)/shard_map/all_to_all | solution.py:55
  27.5 0.1 shard_map.160.refs_1_
  27.6 5.1 %collective-permute-start.1 = (f32[16,128]{1,0:T(8,128)S(1)}, f32[16,128]{1,0:T(8,128)S(1)}, u32[]{:S(2)}, u32[]{:S(2)}) collective-permute-start(f32[16,128]{1,0:T(8,128)S(1)} %shard_map.160.refs_1_), channel_id=1, source_target_pairs={{8,0},{72,64},{10,2},{74,66},{12,4},{76,68},{14,6},{78,70},{16,8},... | collective-permute-start | bytes 24584 | tf_op jit(solution)/shard_map/ppermute | solution.py:36
  32.7 1.9 %collective-permute-start.4 = (f32[16,128]{1,0:T(8,128)S(1)}, f32[16,128]{1,0:T(8,128)S(1)}, u32[]{:S(2)}, u32[]{:S(2)}) collective-permute-start(f32[16,128]{1,0:T(8,128)S(1)} %shard_map.160.refs_1_), channel_id=1, source_target_pairs={{56,0},{120,64},{58,2},{122,66},{60,4},{124,68},{62,6},{126,70},{0... | collective-permute-start | bytes 24584 | tf_op jit(solution)/shard_map/ppermute | solution.py:36
  34.6 0.0 collective-permute-done.refs_3_.edges.refs_1_
  34.7 0.0 collective-permute-done.1.refs_2_
  34.7 2.5 %collective-permute-start.3 = (s32[1,1792]{1,0:T(1,128)S(1)}, s32[1,1792]{1,0:T(1,128)S(1)}, u32[]{:S(2)}, u32[]{:S(2)}) collective-permute-start(s32[1,1792]{1,0:T(1,128)S(1)} %multiply_add_fusion), channel_id=1, source_target_pairs={{128,0},{192,64},{130,2},{194,66},{132,4},{196,68},{134,6},{198,70... | collective-permute-start | bytes 21512 | tf_op jit(solution)/shard_map/ppermute | solution.py:36
  37.2 2.8 %collective-permute-start.2 = (s32[1,1792]{1,0:T(1,128)S(1)}, s32[1,1792]{1,0:T(1,128)S(1)}, u32[]{:S(2)}, u32[]{:S(2)}) collective-permute-start(s32[1,1792]{1,0:T(1,128)S(1)} %multiply_add_fusion), channel_id=1, source_target_pairs={{385,0},{449,64},{387,2},{451,66},{389,4},{453,68},{391,6},{455,70... | collective-permute-start | bytes 21512 | tf_op jit(solution)/shard_map/ppermute | solution.py:36
  40.0 0.0 collective-permute-done.4.refs_0_
  40.0 2.0 %shard_map.161 = (f32[1,32]{1,0:T(1,128)S(1)}, f32[32,128]{1,0:T(8,128)S(1)}, bf16[32,128]{1,0:T(8,128)(2,1)S(1)}, f32[4,56,96]{2,1,0:T(8,128)S(1)}, f32[56,128]...) custom-call(f32[16,128]{1,0:T(8,128)S(1)} %collective-permute-done.4, ...), custom_call_target="tpu_custom_call" | custom-call | flops 1000000 | bytes 1000000 | tf_op jit(solution)/shard_map/pallas_call | solution.py:144
  42.0 0.0 collective-permute-done.3
  42.0 0.7 collective-permute-done.2
  42.8 3.5 %shard_map.162 = (bf16[96,128]{1,0:T(8,128)(2,1)S(1)}, f32[8,1792]{1,0:T(8,128)S(1)}, bf16[288,1792]{1,0:T(8,128)(2,1)S(1)}, bf16[256,128]{1,0:T(8,128)(2,1)S(1)...) custom-call(s32[2,1792]{1,0:T(2,128)S(1)} %pad_add_fusion.before.edg, ...), custom_call_target="tpu_custom_call" | custom-call | flops 1000000 | bytes 1000000 | tf_op jit(solution)/shard_map/pallas_call | solution.py:144
  46.3 4.6 %collective-permute-start.6 = (bf16[96,128]{1,0:T(8,128)(2,1)S(1)}, bf16[96,128]{1,0:T(8,128)(2,1)S(1)}, u32[]{:S(2)}, u32[]{:S(2)}) collective-permute-start(bf16[96,128]{1,0:T(8,128)(2,1)S(1)} %get-tuple-element.124), channel_id=1, source_target_pairs={{8,0},{72,64},{10,2},{74,66},{12,4},{76,68},{14,6},{78,70},{16,8},... | collective-permute-start | bytes 73736 | tf_op jit(solution)/shard_map/ppermute | solution.py:36
  50.9 2.1 %collective-permute-start.5 = (bf16[96,128]{1,0:T(8,128)(2,1)S(1)}, bf16[96,128]{1,0:T(8,128)(2,1)S(1)}, u32[]{:S(2)}, u32[]{:S(2)}) collective-permute-start(bf16[96,128]{1,0:T(8,128)(2,1)S(1)} %get-tuple-element.124), channel_id=1, source_target_pairs={{56,0},{120,64},{58,2},{122,66},{60,4},{124,68},{62,6},{126,70},{0... | collective-permute-start | bytes 73736 | tf_op jit(solution)/shard_map/ppermute | solution.py:36
  53.0 1.6 %shard_map.163 = (bf16[864,1792]{1,0:T(8,128)(2,1)S(1)}, f32[384,1792]{1,0:T(8,128)S(1)}, f32[64,1792]{1,0:T(8,128)S(1)}, f32[1,32]{1,0:T(1,128)S(1)}, f32[32,128]{1,0:T(8,128)S(1)}, /*index=5*/f32[32,16]{1,0:T(8,128)S(1)}) custom-call(s32[2,1792]{1,0:T(2,128)S(1)} %collective-permute-done.refs_3_.edges.refs_1_, f32[8,1792]{1,0:T(8,128)S(1)} %get-tuple-element.125.geo, ...), custom_call_target="tpu_custom_call" | custom-call | flops 1000000000 | bytes 1000000 | tf_op jit(solution)/shard_map/pallas_call | solution.py:144
  54.6 0.0 collective-permute-done.6
  54.6 2.1 %collective-permute-done.5 = bf16[96,128]{1,0:T(8,128)(2,1)S(1)} collective-permute-done((bf16[96,128]{1,0:T(8,128)(2,1)S(1)}, bf16[96,128]{1,0:T(8,128)(2,1)S(1)}, u32[]{:S(2)}, u32[]{:S(2)}) %collective-permute-start.5) | collective-permute-done | bytes 24608 | tf_op jit(solution)/shard_map/ppermute | solution.py:36
  56.7 4.0 %collective-permute-start.8 = (bf16[288,128]{1,0:T(8,128)(2,1)S(1)}, bf16[288,128]{1,0:T(8,128)(2,1)S(1)}, u32[]{:S(2)}, u32[]{:S(2)}) collective-permute-start(bf16[288,128]{1,0:T(8,128)(2,1)S(1)} %pad_maximum_fusion.own), channel_id=1, source_target_pairs={{64,0},{2,64},{66,2},{4,66},{68,4},{6,68},{70,6},{0,70},{72,8},{10... | collective-permute-start | bytes 221192 | tf_op jit(solution)/shard_map/ppermute | solution.py:36
  60.6 0.2 collective-permute-start.7
  60.8 2.1 %shard_map.164.refs_11_ = bf16[384,1792]{1,0:T(8,128)(2,1)S(1)} custom-call(s32[2,1792]{1,0:T(2,128)S(1)} %collective-permute-done.refs_3_.edges.refs_1_, f32[8,1792]{1,0:T(8,128)S(1)} %get-tuple-element.125.geo, bf16[288,1792]{1,0:T(8,128)(2,1)S(1)} %get-tuple-element.137.pool, bf16[256,128]{1,0:T(8,128)(2,1)S(1)} %get-tuple-element.138.at, ...), custom_call_target="tpu_custom_call" | custom-call | flops 1000000000 | bytes 1000000 | tf_op jit(solution)/shard_map/pallas_call | solution.py:144
  62.9 0.0 collective-permute-done.8.right
  62.9 0.0 collective-permute-done.7.left
  62.9 3.6 %shard_map.165 = (bf16[288,128]{1,0:T(8,128)(2,1)S(1)}, f32[288,128]{1,0:T(8,128)S(1)}, bf16[288,128]{1,0:T(8,128)(2,1)S(1)}, f32[32,128]{1,0:T(8,128)S(1)}, f32...) custom-call(bf16[288,128]{1,0:T(8,128)(2,1)S(1)} %collective-permute, ...), custom_call_target="tpu_custom_call" | custom-call | flops 1000000 | bytes 1000000 | tf_op jit(solution)/shard_map/pallas_call | solution.py:144
  66.6 2.7 %collective-permute-start.9 = (bf16[288,128]{1,0:T(8,128)(2,1)S(1)}, bf16[288,128]{1,0:T(8,128)(2,1)S(1)}, u32[]{:S(2)}, u32[]{:S(2)}) collective-permute-start(bf16[288,128]{1,0:T(8,128)(2,1)S(1)} %get-tuple-element.151), channel_id=1, source_target_pairs={{64,0},{2,64},{66,2},{4,66},{68,4},{6,68},{70,6},{0,70},{72,8},{10... | collective-permute-start | bytes 221192 | tf_op jit(solution)/shard_map/ppermute | solution.py:36
  69.3 0.0 collective-permute-start.10
  69.3 0.7 shard_map.168.refs_13_
  70.0 2.1 %shard_map.166.refs_10_ = bf16[384,1792]{1,0:T(8,128)(2,1)S(1)} custom-call(s32[2,1792]{1,0:T(2,128)S(1)} %pad_add_fusion.before.edges.refs_0_, f32[8,1792]{1,0:T(8,128)S(1)} %get-tuple-element.159.geo, bf16[288,1792]{1,0:T(8,128)(2,1)S(1)} %get-tuple-element.160.pool, bf16[256,128]{1,0:T(8,128)(2,1)S(1)} %get-tuple-element.161.at, ...), custom_call_target="tpu_custom_call" | custom-call | flops 1000000000 | bytes 1000000 | tf_op jit(solution)/shard_map/pallas_call | solution.py:144
  72.1 0.0 collective-permute-done.9
  72.1 0.0 collective-permute-done.10
  72.2 1.9 %collective-permute-start.11 = (bf16[96,128]{1,0:T(8,128)(2,1)S(1)}, bf16[96,128]{1,0:T(8,128)(2,1)S(1)}, u32[]{:S(2)}, u32[]{:S(2)}) collective-permute-start(bf16[96,128]{1,0:T(8,128)(2,1)S(1)} %get-tuple-element.190), channel_id=1, source_target_pairs={{8,0},{72,64},{10,2},{74,66},{12,4},{76,68},{14,6},{78,70},{16,8},... | collective-permute-start | bytes 73736 | tf_op jit(solution)/shard_map/ppermute | solution.py:36
  74.1 3.6 %collective-permute-start.12 = (bf16[96,128]{1,0:T(8,128)(2,1)S(1)}, bf16[96,128]{1,0:T(8,128)(2,1)S(1)}, u32[]{:S(2)}, u32[]{:S(2)}) collective-permute-start(bf16[96,128]{1,0:T(8,128)(2,1)S(1)} %get-tuple-element.191), channel_id=1, source_target_pairs={{56,0},{120,64},{58,2},{122,66},{60,4},{124,68},{62,6},{126,70},{0... | collective-permute-start | bytes 73736 | tf_op jit(solution)/shard_map/ppermute | solution.py:36
  77.7 2.1 %shard_map.167.refs_12_ = bf16[384,1792]{1,0:T(8,128)(2,1)S(1)} custom-call(s32[2,1792]{1,0:T(2,128)S(1)} %pad_add_fusion.1.after.edges.refs_2_, f32[8,1792]{1,0:T(8,128)S(1)} %get-tuple-element.177.geo, bf16[288,1792]{1,0:T(8,128)(2,1)S(1)} %get-tuple-element.178.pool, bf16[256,128]{1,0:T(8,128)(2,1)S(1)} %get-tuple-element.179.at, ...), custom_call_target="tpu_custom_call" | custom-call | flops 1000000000 | bytes 1000000 | tf_op jit(solution)/shard_map/pallas_call | solution.py:144
  79.8 0.0 collective-permute-done.11
  79.8 0.1 collective-permute-done.12
  79.9 2.2 %shard_map.169 = (f32[16,128]{1,0:T(8,128)S(1)}, f32[16,128]{1,0:T(8,128)S(1)}, f32[16,128]{1,0:T(8,128)S(1)}) custom-call(s32[2,1792]{1,0:T(2,128)S(1)} %pad_add_fusion.before.edges.refs_0_, s32[2,1792]{1,0:T(2,128)S(1)} %collective-permute-done.refs_3_.edges.refs_1_, s32[2,1792]{1,0:T(2,128)S(1)} %pad_add_fusion.1.after.edges.refs_2_, ...), custom_call_target="tpu_custom_call" | custom-call | flops 1000000 | bytes 1000000 | tf_op jit(solution)/shard_map/pallas_call | solution.py:144
  82.1 3.0 %collective-permute-start.13 = (f32[16,128]{1,0:T(8,128)S(1)}, f32[16,128]{1,0:T(8,128)S(1)}, u32[]{:S(2)}, u32[]{:S(2)}) collective-permute-start(f32[16,128]{1,0:T(8,128)S(1)} %get-tuple-element.188), channel_id=1, source_target_pairs={{8,0},{72,64},{10,2},{74,66},{12,4},{76,68},{14,6},{78,70},{16,8},... | collective-permute-start | bytes 24584 | tf_op jit(solution)/shard_map/ppermute | solution.py:36
  85.2 2.2 %collective-permute-start.14 = (f32[16,128]{1,0:T(8,128)S(1)}, f32[16,128]{1,0:T(8,128)S(1)}, u32[]{:S(2)}, u32[]{:S(2)}) collective-permute-start(f32[16,128]{1,0:T(8,128)S(1)} %get-tuple-element.189), channel_id=1, source_target_pairs={{56,0},{120,64},{58,2},{122,66},{60,4},{124,68},{62,6},{126,70},{0... | collective-permute-start | bytes 24584 | tf_op jit(solution)/shard_map/ppermute | solution.py:36
  87.4 0.0 collective-permute-done.13.b
  87.4 3.3 %collective-permute-done.14.c = f32[16,128]{1,0:T(8,128)S(1)} collective-permute-done((f32[16,128]{1,0:T(8,128)S(1)}, f32[16,128]{1,0:T(8,128)S(1)}, u32[]{:S(2)}, u32[]{:S(2)}) %collective-permute-start.14) | collective-permute-done | bytes 8224 | tf_op jit(solution)/shard_map/ppermute | solution.py:36
  90.8 0.2 shard_map.170
  91.0 17.5 %all_to_all.10 = f32[64,1,128]{2,1,0:T(1,128)S(1)} all-to-all(f32[64,1,128]{2,1,0:T(1,128)S(1)} %bitcast.12), channel_id=1, replica_groups=mesh['gx'=8,'gy'=8,'gz'=8] {'gx','gz'}, dimensions={0} | all-to-all | bytes 65536 | tf_op jit(solution)/shard_map/all_to_all | solution.py:55
  108.5 0.6 shard_map.171
  (13 shorter events, 0.2 us)
Async XLA Ops:
  3.4 24.1 %all-to-all-start = ((f32[64,1,128]{2,1,0:T(1,128)}), f32[64,1,128]{2,1,0:T(1,128)S(1)}, u32[]{:S(2)}, u32[]{:S(2)}) async-start(f32[64,1,128]{2,1,0:T(1,128)} %bitcast.1), calls=%async_computation | async-start | bytes 65536 | tf_op jit(solution)/shard_map/all_to_all | solution.py:55
  18.3 16.4 %collective-permute-start = (s32[2,1792]{1,0:T(2,128)S(1)}, s32[2,1792]{1,0:T(2,128)S(1)}, u32[]{:S(2)}, u32[]{:S(2)}) collective-permute-start(s32[2,1792]{1,0:T(2,128)S(1)} %get-tuple-element.96), channel_id=1, source_target_pairs={{0,0},{1,64},{2,2},{3,66},{4,4},{5,68},{6,6},{7,70},{8,8},{9,72},{... | collective-permute-start | bytes 43016 | tf_op jit(solution)/shard_map/ppermute | solution.py:36
  27.6 7.0 %collective-permute-start.1 = (f32[16,128]{1,0:T(8,128)S(1)}, f32[16,128]{1,0:T(8,128)S(1)}, u32[]{:S(2)}, u32[]{:S(2)}) collective-permute-start(f32[16,128]{1,0:T(8,128)S(1)} %shard_map.160.refs_1_), channel_id=1, source_target_pairs={{8,0},{72,64},{10,2},{74,66},{12,4},{76,68},{14,6},{78,70},{16,8},... | collective-permute-start | bytes 24584 | tf_op jit(solution)/shard_map/ppermute | solution.py:36
  32.7 7.3 %collective-permute-start.4 = (f32[16,128]{1,0:T(8,128)S(1)}, f32[16,128]{1,0:T(8,128)S(1)}, u32[]{:S(2)}, u32[]{:S(2)}) collective-permute-start(f32[16,128]{1,0:T(8,128)S(1)} %shard_map.160.refs_1_), channel_id=1, source_target_pairs={{56,0},{120,64},{58,2},{122,66},{60,4},{124,68},{62,6},{126,70},{0... | collective-permute-start | bytes 24584 | tf_op jit(solution)/shard_map/ppermute | solution.py:36
  34.7 7.3 %collective-permute-start.3 = (s32[1,1792]{1,0:T(1,128)S(1)}, s32[1,1792]{1,0:T(1,128)S(1)}, u32[]{:S(2)}, u32[]{:S(2)}) collective-permute-start(s32[1,1792]{1,0:T(1,128)S(1)} %multiply_add_fusion), channel_id=1, source_target_pairs={{128,0},{192,64},{130,2},{194,66},{132,4},{196,68},{134,6},{198,70... | collective-permute-start | bytes 21512 | tf_op jit(solution)/shard_map/ppermute | solution.py:36
  37.2 5.6 %collective-permute-start.2 = (s32[1,1792]{1,0:T(1,128)S(1)}, s32[1,1792]{1,0:T(1,128)S(1)}, u32[]{:S(2)}, u32[]{:S(2)}) collective-permute-start(s32[1,1792]{1,0:T(1,128)S(1)} %multiply_add_fusion), channel_id=1, source_target_pairs={{385,0},{449,64},{387,2},{451,66},{389,4},{453,68},{391,6},{455,70... | collective-permute-start | bytes 21512 | tf_op jit(solution)/shard_map/ppermute | solution.py:36
  46.3 8.3 %collective-permute-start.6 = (bf16[96,128]{1,0:T(8,128)(2,1)S(1)}, bf16[96,128]{1,0:T(8,128)(2,1)S(1)}, u32[]{:S(2)}, u32[]{:S(2)}) collective-permute-start(bf16[96,128]{1,0:T(8,128)(2,1)S(1)} %get-tuple-element.124), channel_id=1, source_target_pairs={{8,0},{72,64},{10,2},{74,66},{12,4},{76,68},{14,6},{78,70},{16,8},... | collective-permute-start | bytes 73736 | tf_op jit(solution)/shard_map/ppermute | solution.py:36
  50.9 5.8 %collective-permute-start.5 = (bf16[96,128]{1,0:T(8,128)(2,1)S(1)}, bf16[96,128]{1,0:T(8,128)(2,1)S(1)}, u32[]{:S(2)}, u32[]{:S(2)}) collective-permute-start(bf16[96,128]{1,0:T(8,128)(2,1)S(1)} %get-tuple-element.124), channel_id=1, source_target_pairs={{56,0},{120,64},{58,2},{122,66},{60,4},{124,68},{62,6},{126,70},{0... | collective-permute-start | bytes 73736 | tf_op jit(solution)/shard_map/ppermute | solution.py:36
  56.7 6.2 %collective-permute-start.8 = (bf16[288,128]{1,0:T(8,128)(2,1)S(1)}, bf16[288,128]{1,0:T(8,128)(2,1)S(1)}, u32[]{:S(2)}, u32[]{:S(2)}) collective-permute-start(bf16[288,128]{1,0:T(8,128)(2,1)S(1)} %pad_maximum_fusion.own), channel_id=1, source_target_pairs={{64,0},{2,64},{66,2},{4,66},{68,4},{6,68},{70,6},{0,70},{72,8},{10... | collective-permute-start | bytes 221192 | tf_op jit(solution)/shard_map/ppermute | solution.py:36
  60.6 2.3 %collective-permute-start.7 = (bf16[288,128]{1,0:T(8,128)(2,1)S(1)}, bf16[288,128]{1,0:T(8,128)(2,1)S(1)}, u32[]{:S(2)}, u32[]{:S(2)}) collective-permute-start(bf16[288,128]{1,0:T(8,128)(2,1)S(1)} %pad_maximum_fusion.own), channel_id=1, source_target_pairs={{70,0},{0,64},{64,2},{2,66},{66,4},{4,68},{68,6},{6,70},{78,8},{8,... | collective-permute-start | bytes 221192 | tf_op jit(solution)/shard_map/ppermute | solution.py:36
  66.6 5.5 %collective-permute-start.9 = (bf16[288,128]{1,0:T(8,128)(2,1)S(1)}, bf16[288,128]{1,0:T(8,128)(2,1)S(1)}, u32[]{:S(2)}, u32[]{:S(2)}) collective-permute-start(bf16[288,128]{1,0:T(8,128)(2,1)S(1)} %get-tuple-element.151), channel_id=1, source_target_pairs={{64,0},{2,64},{66,2},{4,66},{68,4},{6,68},{70,6},{0,70},{72,8},{10... | collective-permute-start | bytes 221192 | tf_op jit(solution)/shard_map/ppermute | solution.py:36
  69.3 2.8 %collective-permute-start.10 = (bf16[288,128]{1,0:T(8,128)(2,1)S(1)}, bf16[288,128]{1,0:T(8,128)(2,1)S(1)}, u32[]{:S(2)}, u32[]{:S(2)}) collective-permute-start(bf16[288,128]{1,0:T(8,128)(2,1)S(1)} %get-tuple-element.152), channel_id=1, source_target_pairs={{70,0},{0,64},{64,2},{2,66},{66,4},{4,68},{68,6},{6,70},{78,8},{8,... | collective-permute-start | bytes 221192 | tf_op jit(solution)/shard_map/ppermute | solution.py:36
  72.2 7.6 %collective-permute-start.11 = (bf16[96,128]{1,0:T(8,128)(2,1)S(1)}, bf16[96,128]{1,0:T(8,128)(2,1)S(1)}, u32[]{:S(2)}, u32[]{:S(2)}) collective-permute-start(bf16[96,128]{1,0:T(8,128)(2,1)S(1)} %get-tuple-element.190), channel_id=1, source_target_pairs={{8,0},{72,64},{10,2},{74,66},{12,4},{76,68},{14,6},{78,70},{16,8},... | collective-permute-start | bytes 73736 | tf_op jit(solution)/shard_map/ppermute | solution.py:36
  74.1 5.8 %collective-permute-start.12 = (bf16[96,128]{1,0:T(8,128)(2,1)S(1)}, bf16[96,128]{1,0:T(8,128)(2,1)S(1)}, u32[]{:S(2)}, u32[]{:S(2)}) collective-permute-start(bf16[96,128]{1,0:T(8,128)(2,1)S(1)} %get-tuple-element.191), channel_id=1, source_target_pairs={{56,0},{120,64},{58,2},{122,66},{60,4},{124,68},{62,6},{126,70},{0... | collective-permute-start | bytes 73736 | tf_op jit(solution)/shard_map/ppermute | solution.py:36
  82.1 5.3 %collective-permute-start.13 = (f32[16,128]{1,0:T(8,128)S(1)}, f32[16,128]{1,0:T(8,128)S(1)}, u32[]{:S(2)}, u32[]{:S(2)}) collective-permute-start(f32[16,128]{1,0:T(8,128)S(1)} %get-tuple-element.188), channel_id=1, source_target_pairs={{8,0},{72,64},{10,2},{74,66},{12,4},{76,68},{14,6},{78,70},{16,8},... | collective-permute-start | bytes 24584 | tf_op jit(solution)/shard_map/ppermute | solution.py:36
  85.2 5.6 %collective-permute-start.14 = (f32[16,128]{1,0:T(8,128)S(1)}, f32[16,128]{1,0:T(8,128)S(1)}, u32[]{:S(2)}, u32[]{:S(2)}) collective-permute-start(f32[16,128]{1,0:T(8,128)S(1)} %get-tuple-element.189), channel_id=1, source_target_pairs={{56,0},{120,64},{58,2},{122,66},{60,4},{124,68},{62,6},{126,70},{0... | collective-permute-start | bytes 24584 | tf_op jit(solution)/shard_map/ppermute | solution.py:36
